TPU v7x, 32 devices: a whole 2x2x4 slice. The times are simulated.
32 devices in a mesh: dp: 16 (over z, x, core), narrow: 2 (over y).
Axes of the slice: x: 2, y: 2, z: 4, core: 2. Of those that a mesh axis runs over, the one named last changes fastest.
Arguments:
- tokens: bfloat16 [36864, 1024], P(('dp', 'narrow')), may hold values from -6 to 6
- cotangent: bfloat16 [36864, 1024], P(('dp', 'narrow')), may hold values from -6 to 6
- bucket: int32 [32], P(('dp', 'narrow')), may hold values from 0 to 1
- text_lengths: int32 [32, 3], P(('dp', 'narrow')), may hold values from 1 to 128, as said below
- attn_qkv: float32 [3, 1024, 1024], P(None, 'dp', 'narrow'), may hold values from -0.1875 to 0.1875
- attn_out: float32 [1024, 1024], P('dp', 'narrow'), may hold values from -2 to 2
- ffn_in: float32 [2, 1024, 2816], P(None, 'dp', 'narrow'), may hold values from -0.1875 to 0.1875
- ffn_out: float32 [2816, 1024], P('dp', 'narrow'), may hold values from -0.109375 to 0.109375
- norm_gains: float32 [2, 1024], P(None, ('dp', 'narrow')), may hold values from 0.5 to 1.5
- first_qkv: float32 [3, 1024, 1024], P(None, 'dp', 'narrow'), may hold values from -96 to 96
- first_out: float32 [1024, 1024], P('dp', 'narrow'), may hold values from -8 to 8
- first_ffin: float32 [2, 1024, 2816], P(None, 'dp', 'narrow'), may hold values from -48 to 48
- first_ffout: float32 [2816, 1024], P('dp', 'narrow'), may hold values from -80 to 80
- first_gains: float32 [2, 1024], P(None, ('dp', 'narrow')), may hold values from -128 to 128
- second_qkv: float32 [3, 1024, 1024], P(None, 'dp', 'narrow'), may hold values from 18.432 to 73.728
- second_out: float32 [1024, 1024], P('dp', 'narrow'), may hold values from 0.1856 to 0.736
- second_ffin: float32 [2, 1024, 2816], P(None, 'dp', 'narrow'), may hold values from 4.42368 to 18.432
- second_ffout: float32 [2816, 1024], P('dp', 'narrow'), may hold values from 13.27104 to 51.6096
- second_gains: float32 [2, 1024], P(None, ('dp', 'narrow')), may hold values from 36.864 to 147.456
Outputs:
- mixed: bfloat16 [36864, 1024], P(('dp', 'narrow'))
- input_grad: float32 [36864, 1024], P(('dp', 'narrow'))
- grad_qkv: float32 [3, 1024, 1024], P(None, 'dp', 'narrow')
- new_first_qkv: float32 [3, 1024, 1024], P(None, 'dp', 'narrow')
- new_second_qkv: float32 [3, 1024, 1024], P(None, 'dp', 'narrow')
- new_qkv: float32 [3, 1024, 1024], P(None, 'dp', 'narrow')
- grad_out: float32 [1024, 1024], P('dp', 'narrow')
- new_first_out: float32 [1024, 1024], P('dp', 'narrow')
- new_second_out: float32 [1024, 1024], P('dp', 'narrow')
- new_out: float32 [1024, 1024], P('dp', 'narrow')
- grad_ffin: float32 [2, 1024, 2816], P(None, 'dp', 'narrow')
- new_first_ffin: float32 [2, 1024, 2816], P(None, 'dp', 'narrow')
- new_second_ffin: float32 [2, 1024, 2816], P(None, 'dp', 'narrow')
- new_ffin: float32 [2, 1024, 2816], P(None, 'dp', 'narrow')
- grad_ffout: float32 [2816, 1024], P('dp', 'narrow')
- new_first_ffout: float32 [2816, 1024], P('dp', 'narrow')
- new_second_ffout: float32 [2816, 1024], P('dp', 'narrow')
- new_ffout: float32 [2816, 1024], P('dp', 'narrow')
- grad_gains: float32 [2, 1024], P(None, ('dp', 'narrow'))
- new_first_gains: float32 [2, 1024], P(None, ('dp', 'narrow'))
- new_second_gains: float32 [2, 1024], P(None, ('dp', 'narrow'))
- new_gains: float32 [2, 1024], P(None, ('dp', 'narrow'))
Inputs may be any that keep to these rules, and one draw needn't show every extreme that they name: `text_lengths`: text tokens of each example of a pack; the value 128 occurs in every draw.
All inputs are finite; a program needn't handle non-finite values.
Results may differ from a plain program's by a relative error of at most 0.025.
Values may be sent and summed in bfloat16 or wider, within the bound.
No kernel may reach another device: no remote copies, remote signals or barrier semaphores. Data moves between devices by JAX's collectives and lax.ppermute only.
A program may use at most 256 MiB of HBM per device.

v0:
```python
import jax
import jax.numpy as jnp
from jax import lax
from jax.sharding import PartitionSpec as P

HEADS = 16
DK = 64
SHORT_PATCH = 256
STEP = 10
HD = 1024
SLOT = 384
LONG = 1152
LONG_PATCH = 1024


norm_eps = 1e-06
score_scale = 0.125
masked_score = -1e30
beta_one = 0.9
beta_two = 0.999
adam_eps = 1e-08
decay_rate = 0.01
rates = (0.08, 0.8, 0.08, 0.05, 0.6)


def gelu_tanh(values):
    return (
        0.5
        * values
        * (1.0 + jnp.tanh(0.7978845608028654 * (values + 0.044715 * values * values * values)))
    )


def gelu_times(gate_in, upward_in):
    return gelu_tanh(gate_in) * upward_in


def norm_scaled(values, gain_row):
    return (
        values * lax.rsqrt(jnp.mean(values * values, axis=-1, keepdims=True) + norm_eps) * gain_row
    )


def segment_ids(bucket_one, text_one):
    position = jnp.arange(LONG, dtype=jnp.int32)
    slot_index = position // SLOT
    inside = position - slot_index * SLOT
    slot_length = SHORT_PATCH + jnp.where(
        slot_index == 0, text_one[0], jnp.where(slot_index == 1, text_one[1], text_one[2])
    )
    long_valid = position < LONG_PATCH + text_one[0]
    short_valid = inside < slot_length
    minus_one = jnp.full((LONG,), -1, dtype=jnp.int32)
    return jnp.where(
        bucket_one == 1,
        jnp.where(long_valid, jnp.zeros((LONG,), jnp.int32), minus_one),
        jnp.where(short_valid, slot_index, minus_one),
    )


def split_heads(columns):
    return columns.reshape(columns.shape[0], -1, DK)


def masked_scores(query_cols, key_cols, same_doc):
    scores = (
        jnp.einsum(
            "qhd,khd->hqk",
            split_heads(query_cols),
            split_heads(key_cols),
            preferred_element_type=jnp.float32,
        )
        * score_scale
    )
    return jnp.where(same_doc[None], scores, masked_score)


def attend_forward(query_cols, key_cols, value_cols, same_doc):
    scores = masked_scores(query_cols, key_cols, same_doc)
    row_top = jnp.max(scores, axis=-1, keepdims=True)
    expo = jnp.exp(scores - row_top)
    row_sum = jnp.sum(expo, axis=-1, keepdims=True)
    probs_low = (expo / row_sum).astype(jnp.bfloat16)
    result = jnp.einsum(
        "hqk,khd->qhd", probs_low, split_heads(value_cols), preferred_element_type=jnp.float32
    )
    return (
        result.astype(jnp.bfloat16).reshape(query_cols.shape[0], -1),
        (row_top + jnp.log(row_sum))[..., 0],
    )


def attend_backward(query_cols, key_cols, value_cols, grad_cols, log_total, same_doc):
    scores = masked_scores(query_cols, key_cols, same_doc)
    probs = jnp.exp(scores - log_total[..., None])
    grad_heads = split_heads(grad_cols)
    grad_value = jnp.einsum(
        "hqk,qhd->khd", probs.astype(jnp.bfloat16), grad_heads, preferred_element_type=jnp.float32
    )
    grad_probs = jnp.einsum(
        "qhd,khd->hqk", grad_heads, split_heads(value_cols), preferred_element_type=jnp.float32
    )
    inner_sum = jnp.sum(probs * grad_probs, axis=-1, keepdims=True)
    grad_scores = (probs * (grad_probs - inner_sum)).astype(jnp.bfloat16)
    grad_query = (
        jnp.einsum(
            "hqk,khd->qhd", grad_scores, split_heads(key_cols), preferred_element_type=jnp.float32
        )
        * score_scale
    )
    grad_key = (
        jnp.einsum(
            "hqk,qhd->khd", grad_scores, split_heads(query_cols), preferred_element_type=jnp.float32
        )
        * score_scale
    )
    rows = query_cols.shape[0]
    return jnp.stack(
        (grad_query.reshape(rows, -1), grad_key.reshape(rows, -1), grad_value.reshape(rows, -1))
    ).astype(jnp.bfloat16)


def head_width():
    return min(4, HEADS) * DK


def attention_forward(projected, seg_rows, packs):
    width = head_width()

    def one_pack(index_pack):
        seg_pack = lax.dynamic_index_in_dim(seg_rows, index_pack, 0, keepdims=False)
        same_doc = seg_pack[:, None] == seg_pack[None, :]

        def one_group(index_group):
            columns = lax.dynamic_slice_in_dim(projected, index_group * width, width, 2)
            return attend_forward(columns[0], columns[1], columns[2], same_doc)

        group_out, group_lse = lax.map(one_group, jnp.arange(HD // width))
        return (jnp.moveaxis(group_out, 0, 1).reshape(LONG, HD), group_lse)

    pack_out, pack_lse = lax.map(one_pack, jnp.arange(packs))
    return (pack_out.reshape(packs * LONG, HD), pack_lse)


def attention_backward(projected, grad_attended, pack_lse, seg_rows, packs):
    width = head_width()

    def one_pack(index_pack):
        lse_pack = lax.dynamic_index_in_dim(pack_lse, index_pack, 0, keepdims=False)
        seg_pack = lax.dynamic_index_in_dim(seg_rows, index_pack, 0, keepdims=False)
        same_doc = seg_pack[:, None] == seg_pack[None, :]

        def one_group(index_group):
            columns = lax.dynamic_slice_in_dim(projected, index_group * width, width, 2)
            grad_cols = lax.dynamic_slice_in_dim(grad_attended, index_group * width, width, 1)
            lse_group = lax.dynamic_index_in_dim(lse_pack, index_group, 0, keepdims=False)
            return attend_backward(
                columns[0], columns[1], columns[2], grad_cols, lse_group, same_doc
            )

        group_grad = lax.map(one_group, jnp.arange(HD // width))
        return jnp.moveaxis(group_grad, 0, 2).reshape(3, LONG, HD)

    pack_grad = lax.map(one_pack, jnp.arange(packs))
    return jnp.moveaxis(pack_grad, 0, 1).reshape(3, packs * LONG, HD)


def adamw(weight, grad_total, first, second, rate):
    first_new = beta_one * first + (1.0 - beta_one) * grad_total
    second_new = beta_two * second + (1.0 - beta_two) * grad_total * grad_total
    first_hat = first_new / (1.0 - beta_one**STEP)
    second_hat = second_new / (1.0 - beta_two**STEP)
    weight_new = weight - rate * (
        first_hat / (jnp.sqrt(second_hat) + adam_eps) + decay_rate * weight
    )
    return (grad_total, first_new, second_new, weight_new)


def local(
    tokens,
    cotangent,
    bucket,
    text_lengths,
    attn_qkv,
    attn_out,
    ffn_in,
    ffn_out,
    norm_gains,
    first_qkv,
    first_out,
    first_ffin,
    first_ffout,
    first_gains,
    second_qkv,
    second_out,
    second_ffin,
    second_ffout,
    second_gains,
):
    low_qkv = attn_qkv.astype(jnp.bfloat16)
    low_out = attn_out.astype(jnp.bfloat16)
    low_ffin = ffn_in.astype(jnp.bfloat16)
    low_ffout = ffn_out.astype(jnp.bfloat16)
    low_gains = norm_gains.astype(jnp.bfloat16)
    wide_rows = (
        lax.all_gather(low_qkv, "narrow", axis=2, tiled=True),
        lax.all_gather(low_out, "narrow", axis=1, tiled=True),
        lax.all_gather(low_ffin, "narrow", axis=2, tiled=True),
        lax.all_gather(low_ffout, "narrow", axis=1, tiled=True),
        lax.all_gather(low_gains, "narrow", axis=1, tiled=True),
    )
    full_qkv, full_out, full_ffin, full_ffout, full_gains = (
        lax.all_gather(wide_rows[0], "dp", axis=1, tiled=True),
        lax.all_gather(wide_rows[1], "dp", axis=0, tiled=True),
        lax.all_gather(wide_rows[2], "dp", axis=1, tiled=True),
        lax.all_gather(wide_rows[3], "dp", axis=0, tiled=True),
        lax.all_gather(wide_rows[4], "dp", axis=1, tiled=True),
    )
    packs = tokens.shape[0] // LONG
    seg_rows = jax.vmap(segment_ids)(bucket, text_lengths)
    valid = (seg_rows.reshape(-1) >= 0).astype(jnp.float32)[:, None]
    inputs = tokens.astype(jnp.float32)
    gain_one = full_gains[0].astype(jnp.float32)
    gain_two = full_gains[1].astype(jnp.float32)
    normed = norm_scaled(inputs, gain_one).astype(jnp.bfloat16)
    projected = jnp.einsum(
        "rd,cde->cre", normed, full_qkv, preferred_element_type=jnp.float32
    ).astype(jnp.bfloat16)
    attended, pack_lse = attention_forward(projected, seg_rows, packs)
    hidden_state = inputs + jnp.dot(attended, full_out, preferred_element_type=jnp.float32)
    normed_two = norm_scaled(hidden_state, gain_two).astype(jnp.bfloat16)
    gate_up = jnp.einsum("rd,cdf->crf", normed_two, full_ffin, preferred_element_type=jnp.float32)
    inner = gelu_times(gate_up[0], gate_up[1]).astype(jnp.bfloat16)
    mixed = (hidden_state + jnp.dot(inner, full_ffout, preferred_element_type=jnp.float32)).astype(
        jnp.bfloat16
    )
    again_rows = (
        lax.all_gather(low_qkv, "narrow", axis=2, tiled=True),
        lax.all_gather(low_out, "narrow", axis=1, tiled=True),
        lax.all_gather(low_ffin, "narrow", axis=2, tiled=True),
        lax.all_gather(low_ffout, "narrow", axis=1, tiled=True),
    )
    back_qkv, back_out, back_ffin, back_ffout = (
        lax.all_gather(again_rows[0], "dp", axis=1, tiled=True),
        lax.all_gather(again_rows[1], "dp", axis=0, tiled=True),
        lax.all_gather(again_rows[2], "dp", axis=1, tiled=True),
        lax.all_gather(again_rows[3], "dp", axis=0, tiled=True),
    )
    grad_mixed = cotangent.astype(jnp.float32) * valid
    grad_low = grad_mixed.astype(jnp.bfloat16)
    grad_ffout = jnp.einsum("rf,rd->fd", inner, grad_low, preferred_element_type=jnp.float32)
    grad_inner = jnp.einsum("rd,fd->rf", grad_low, back_ffout, preferred_element_type=jnp.float32)
    _, pull_gelu = jax.vjp(gelu_times, gate_up[0], gate_up[1])
    grad_gate, grad_upward = pull_gelu(grad_inner)
    grad_gate_up = jnp.stack((grad_gate, grad_upward)).astype(jnp.bfloat16)
    grad_ffin = jnp.einsum(
        "rd,crf->cdf", normed_two, grad_gate_up, preferred_element_type=jnp.float32
    )
    grad_normed_two = jnp.einsum(
        "crf,cdf->rd", grad_gate_up, back_ffin, preferred_element_type=jnp.float32
    )
    _, pull_norm_two = jax.vjp(norm_scaled, hidden_state, gain_two)
    grad_hidden_norm, grad_gain_two = pull_norm_two(grad_normed_two)
    grad_hidden = grad_mixed + grad_hidden_norm
    grad_branch = grad_hidden.astype(jnp.bfloat16)
    grad_out = jnp.einsum("rh,rd->hd", attended, grad_branch, preferred_element_type=jnp.float32)
    grad_attended = jnp.einsum(
        "rd,hd->rh", grad_branch, back_out, preferred_element_type=jnp.float32
    ).astype(jnp.bfloat16)
    grad_projected = attention_backward(projected, grad_attended, pack_lse, seg_rows, packs)
    grad_qkv = jnp.einsum("rd,cre->dce", normed, grad_projected, preferred_element_type=jnp.float32)
    grad_normed = jnp.einsum(
        "cre,cde->rd", grad_projected, back_qkv, preferred_element_type=jnp.float32
    )
    _, pull_norm_one = jax.vjp(norm_scaled, inputs, gain_one)
    grad_input_norm, grad_gain_one = pull_norm_one(grad_normed)
    input_grad = grad_hidden + grad_input_norm
    grad_gains_rows = jnp.stack((grad_gain_one, grad_gain_two), axis=1)
    grad_ffin_rows = jnp.moveaxis(grad_ffin, 1, 0)
    summed = (
        lax.psum_scatter(
            grad_qkv.astype(jnp.bfloat16), "dp", scatter_dimension=0, tiled=True
        ).astype(jnp.float32),
        lax.psum_scatter(
            grad_out.astype(jnp.bfloat16), "dp", scatter_dimension=0, tiled=True
        ).astype(jnp.float32),
        lax.psum_scatter(
            grad_ffin_rows.astype(jnp.bfloat16), "dp", scatter_dimension=0, tiled=True
        ).astype(jnp.float32),
        lax.psum_scatter(
            grad_ffout.astype(jnp.bfloat16), "dp", scatter_dimension=0, tiled=True
        ).astype(jnp.float32),
        lax.psum_scatter(
            grad_gains_rows.astype(jnp.bfloat16), "dp", scatter_dimension=0, tiled=True
        ).astype(jnp.float32),
    )
    owned = (
        lax.psum_scatter(
            summed[0].astype(jnp.bfloat16), "narrow", scatter_dimension=2, tiled=True
        ).astype(jnp.float32),
        lax.psum_scatter(
            summed[1].astype(jnp.bfloat16), "narrow", scatter_dimension=1, tiled=True
        ).astype(jnp.float32),
        lax.psum_scatter(
            summed[2].astype(jnp.bfloat16), "narrow", scatter_dimension=2, tiled=True
        ).astype(jnp.float32),
        lax.psum_scatter(
            summed[3].astype(jnp.bfloat16), "narrow", scatter_dimension=1, tiled=True
        ).astype(jnp.float32),
        lax.psum_scatter(
            summed[4].astype(jnp.bfloat16), "narrow", scatter_dimension=0, tiled=True
        ).astype(jnp.float32),
    )
    shares = (
        jnp.moveaxis(owned[0], 1, 0),
        owned[1],
        jnp.moveaxis(owned[2], 1, 0),
        owned[3],
        jnp.moveaxis(owned[4], 1, 0),
    )
    masters = (attn_qkv, attn_out, ffn_in, ffn_out, norm_gains)
    firsts = (first_qkv, first_out, first_ffin, first_ffout, first_gains)
    seconds = (second_qkv, second_out, second_ffin, second_ffout, second_gains)
    results = [mixed, input_grad]
    for index_weight in range(5):
        results.extend(
            adamw(
                masters[index_weight],
                shares[index_weight],
                firsts[index_weight],
                seconds[index_weight],
                rates[index_weight],
            )
        )
    return tuple(results)


def solution(mesh):
    in_specs = (
        P(("dp", "narrow"), None),
        P(("dp", "narrow"), None),
        P(("dp", "narrow")),
        P(("dp", "narrow"), None),
        P(None, "dp", "narrow"),
        P("dp", "narrow"),
        P(None, "dp", "narrow"),
        P("dp", "narrow"),
        P(None, ("dp", "narrow")),
        P(None, "dp", "narrow"),
        P("dp", "narrow"),
        P(None, "dp", "narrow"),
        P("dp", "narrow"),
        P(None, ("dp", "narrow")),
        P(None, "dp", "narrow"),
        P("dp", "narrow"),
        P(None, "dp", "narrow"),
        P("dp", "narrow"),
        P(None, ("dp", "narrow")),
    )
    out_specs = (
        P(("dp", "narrow"), None),
        P(("dp", "narrow"), None),
        P(None, "dp", "narrow"),
        P(None, "dp", "narrow"),
        P(None, "dp", "narrow"),
        P(None, "dp", "narrow"),
        P("dp", "narrow"),
        P("dp", "narrow"),
        P("dp", "narrow"),
        P("dp", "narrow"),
        P(None, "dp", "narrow"),
        P(None, "dp", "narrow"),
        P(None, "dp", "narrow"),
        P(None, "dp", "narrow"),
        P("dp", "narrow"),
        P("dp", "narrow"),
        P("dp", "narrow"),
        P("dp", "narrow"),
        P(None, ("dp", "narrow")),
        P(None, ("dp", "narrow")),
        P(None, ("dp", "narrow")),
        P(None, ("dp", "narrow")),
    )
    return jax.shard_map(local, mesh=mesh, in_specs=in_specs, out_specs=out_specs, check_vma=False)
```

profile of v0, /device:TPU:0, one launch (start us, length us, event | category | flops | bytes accessed | tf_op | source)
XLA Modules:
  0.0 1096.1 jit_solution(2155222977319154243)
XLA Ops:
  8.4 8.6 all_gather.40
  18.0 5.0 all_gather.42
  24.3 9.2 all_gather.44
  33.6 6.3 all_gather.46
  46.4 4.2 all-gather
  50.8 21.6 %all-gather.1 = bf16[16,64,2]{1,2,0:T(2,128)(2,1)S(1)} all-gather(bf16[1,64,2]{1,2,0:T(2,128)(2,1)S(1)} %reshape.276), channel_id=1, replica_groups=mesh['dp'=16,'narrow'=2] {'dp'}, dimensions={0}, use_global_device_ids=true | all-gather | bytes 4352 | tf_op jit(solution)/shard_map/all_gather | solution.py:217
  76.7 4.7 copy.94
  81.4 12.6 %convert_bitcast_fusion = bf16[3,1152,1024]{2,1,0:T(8,128)(2,1)} fusion(bf16[3,1024,1024]{2,1,0:T(8,128)(2,1)} %all-gather.7.cloned.1.call-done, bf16[1152,1024]{0,1:T(8,128)(2,1)S(1)} %copy.87, f32[1024]{0:T(1024)S(1)} %bitcast.231, f32[1152]{0:T(1024)S(1)} %fusion.59), kind=kOutput, calls=%fused_computation.61 | convolution fusion | flops 7256014848 | bytes 15737344 | tf_op jit(solution)/shard_map/rd,cde->cre/dot_general | solution.py:226
  94.0 9.8 copy.91
  103.8 118.9 %while.40 = (s32[]{:T(128)}, bf16[4,1152,256]{1,2,0:T(8,128)(2,1)}, f32[4,4,1152]{2,1,0:T(4,128)S(1)}, s32[4]{0:T(128)S(1)}, bf16[3,1152,1024]{1,2,0:T(8,128)(2,...) while((s32[]{:T(128)}, bf16[4,1152,256]{1,2,0:T(8,128)(2,1)}, ...), condition=%wide.region_4.5_spmd.clone, body=%wide.region_1.4_spmd.clone.sunk | while | flops 1403039232 | bytes 158520064 | solution.py:138
  108.3 4.9 fusion.124
  113.2 7.2 copy-done.1
  123.4 9.2 fusion.126
  137.9 4.9 fusion.124
  142.8 7.1 copy-done.1
  152.9 9.2 fusion.126
  167.5 4.9 fusion.124
  172.4 7.1 copy-done.1
  182.6 9.2 fusion.126
  197.1 4.9 fusion.124
  202.0 7.2 copy-done.1
  212.3 9.3 fusion.126
  222.8 8.2 multiply_reduce_fusion.2
  231.1 23.2 %convolution_bitcast_fusion = f32[2,1152,2816]{2,1,0:T(8,128)} fusion(bf16[2,1024,2816]{2,1,0:T(8,128)(2,1)} %all-gather.11.cloned.1.call-done, f32[1152,1024]{0,1:T(8,128)} %get-tuple-element.333, f32[1024]{0:T(1024)S(1)} %bitcast.227, f32[1152]{0:T(1024)S(1)} %fusion.60), kind=kOutput, calls=%fused_computation.38 | convolution fusion | flops 13291094016 | bytes 42213888 | tf_op jit(solution)/shard_map/rd,cdf->crf/dot_general | solution.py:232
  254.3 23.5 %all-gather.13.cloned.1.call-done = bf16[2816,1024]{1,0:T(8,128)(2,1)} async-done(((bf16[176,1024]{1,0:T(8,128)(2,1)}), bf16[2816,1024]{1,0:T(8,128)(2,1)}) %all-gather.13.cloned.1.call-update) | async-done | bytes 5767184 | tf_op jit(solution)/shard_map/all_gather | solution.py:216
  277.7 37.6 %fusion.29 = (bf16[1,1152,2816]{2,1,0:T(8,128)(2,1)}, bf16[1,1152,2816]{2,1,0:T(8,128)(2,1)}, bf16[1152,2816]{1,0:T(8,128)(2,1)}) fusion(f32[2,1152,2816]{2,1,0:T(8,128)} %convolution_bitcast_fusion, bf16[2816,1024]{1,0:T(8,128)(2,1)} %all-gather.13.cloned.1.call-done, bf16[1152,1024]{0,1:T(8,128)(2,1)S(1)} %copy-done.9, f32[1152]{0:T(1024)S(1)} %copy-done.24), kind=kOutput, calls=%fused_computation.65 | convolution fusion | flops 6744637440 | bytes 53547520 | tf_op jit(solution)/shard_map/rd,fd->rf/dot_general | solution.py:252
  315.3 24.1 %fusion.38 = (bf16[1024]{0:T(1024)(128)(2,1)S(1)}, f32[1152]{0:T(1024)S(1)}, f32[1152,1024,1]{0,1,2:T(8,128)}) fusion(f32[1152,1024]{0,1:T(8,128)} %get-tuple-element.333, f32[1152]{0:T(1024)S(1)} %fusion.60, f32[1024]{0:T(1024)S(1)} %bitcast.228, bf16[2,1024,2816]{2,1,0:T(8,128)(2,1)} %all-gather.11.cloned.1.call-done, ...), kind=kOutput, calls=%fused_computation.78 | convolution fusion | flops 13301118976 | bytes 33963008 | tf_op jit(solution)/shard_map/crf,cdf->rd/dot_general | solution.py:259
  340.0 5.2 fusion.34
  345.3 4.0 convolution_convert_fusion.1
  349.3 223.6 %while.41 = (s32[]{:T(128)}, bf16[4,3,1152,256]{2,3,0,1:T(8,128)(2,1)}, s32[4]{0:T(128)S(1)}, bf16[3,1152,1024]{1,2,0:T(8,128)(2,1)}, f32[4,4,1152]{2,1,0:T(4,12...) while((s32[]{:T(128)}, ...), condition=%wide.region_9.10_spmd.clone, body=%wide.region_7.9_spmd.clone.sunk | while | flops 3453267456 | bytes 229833920 | solution.py:161
  361.4 12.7 %multiply_reduce_fusion.4 = (f32[4,1152]{1,0:T(4,128)}, f32[4,1152,1152]{1,2,0:T(8,128)}) fusion(f32[4,1152,1152]{1,2,0:T(8,128)S(1)} %fusion.137, f32[4,1152]{1,0:T(4,128)S(1)} %dynamic-slice_bitcast_fusion.2, bf16[1152,4,64]{0,2,1:T(8,128)(2,1)} %bitcast.212, bf16[1152,4,64]{0,2,1:T(8,128)(2,1)} %bitcast.214, ...), kind=kOutput, calls=%fused_computation.20.clone.1 | convolution fusion | flops 706014720 | bytes 45010944 | tf_op jit(solution)/shard_map/while/body/eval_jaxpr/while/body/eval_jaxpr/qhd,khd->hqk/dot_general | solution.py:67
  374.2 13.3 %multiply_convert_fusion.5 = bf16[4,1152,1152]{1,2,0:T(8,128)(2,1)} fusion(f32[4,1152,1152]{1,2,0:T(8,128)} %get-tuple-element.434, f32[4,1152,1152]{1,2,0:T(8,128)S(1)} %fusion.137, f32[4,1152]{1,0:T(4,128)} %get-tuple-element.435), kind=kLoop, calls=%fused_computation.19.clone.1 | loop fusion | flops 15925248 | bytes 53102592 | tf_op jit(solution)/shard_map/while/body/eval_jaxpr/while/body/eval_jaxpr/convert_element_type | solution.py:104
  387.5 11.5 %fusion.138 = bf16[4,64,1152]{2,1,0:T(8,128)(2,1)} fusion(bf16[1152,4,64]{0,2,1:T(8,128)(2,1)} %bitcast.210, f32[4,1152,1152]{1,2,0:T(8,128)} %get-tuple-element.434), kind=kOutput, calls=%fused_computation.28.clone.1 | convolution fusion | flops 685080576 | bytes 22413312 | tf_op jit(solution)/shard_map/while/body/eval_jaxpr/while/body/eval_jaxpr/hqk,qhd->khd/dot_general | solution.py:97
  400.8 3.3 fusion.139
  417.2 12.7 %multiply_reduce_fusion.4 = (f32[4,1152]{1,0:T(4,128)}, f32[4,1152,1152]{1,2,0:T(8,128)}) fusion(f32[4,1152,1152]{1,2,0:T(8,128)S(1)} %fusion.137, f32[4,1152]{1,0:T(4,128)S(1)} %dynamic-slice_bitcast_fusion.2, bf16[1152,4,64]{0,2,1:T(8,128)(2,1)} %bitcast.212, bf16[1152,4,64]{0,2,1:T(8,128)(2,1)} %bitcast.214, ...), kind=kOutput, calls=%fused_computation.20.clone.1 | convolution fusion | flops 706014720 | bytes 45010944 | tf_op jit(solution)/shard_map/while/body/eval_jaxpr/while/body/eval_jaxpr/qhd,khd->hqk/dot_general | solution.py:67
  430.0 13.3 %multiply_convert_fusion.5 = bf16[4,1152,1152]{1,2,0:T(8,128)(2,1)} fusion(f32[4,1152,1152]{1,2,0:T(8,128)} %get-tuple-element.434, f32[4,1152,1152]{1,2,0:T(8,128)S(1)} %fusion.137, f32[4,1152]{1,0:T(4,128)} %get-tuple-element.435), kind=kLoop, calls=%fused_computation.19.clone.1 | loop fusion | flops 15925248 | bytes 53102592 | tf_op jit(solution)/shard_map/while/body/eval_jaxpr/while/body/eval_jaxpr/convert_element_type | solution.py:104
  443.3 11.5 %fusion.138 = bf16[4,64,1152]{2,1,0:T(8,128)(2,1)} fusion(bf16[1152,4,64]{0,2,1:T(8,128)(2,1)} %bitcast.210, f32[4,1152,1152]{1,2,0:T(8,128)} %get-tuple-element.434), kind=kOutput, calls=%fused_computation.28.clone.1 | convolution fusion | flops 685080576 | bytes 22413312 | tf_op jit(solution)/shard_map/while/body/eval_jaxpr/while/body/eval_jaxpr/hqk,qhd->khd/dot_general | solution.py:97
  456.6 3.3 fusion.139
  473.0 12.7 %multiply_reduce_fusion.4 = (f32[4,1152]{1,0:T(4,128)}, f32[4,1152,1152]{1,2,0:T(8,128)}) fusion(f32[4,1152,1152]{1,2,0:T(8,128)S(1)} %fusion.137, f32[4,1152]{1,0:T(4,128)S(1)} %dynamic-slice_bitcast_fusion.2, bf16[1152,4,64]{0,2,1:T(8,128)(2,1)} %bitcast.212, bf16[1152,4,64]{0,2,1:T(8,128)(2,1)} %bitcast.214, ...), kind=kOutput, calls=%fused_computation.20.clone.1 | convolution fusion | flops 706014720 | bytes 45010944 | tf_op jit(solution)/shard_map/while/body/eval_jaxpr/while/body/eval_jaxpr/qhd,khd->hqk/dot_general | solution.py:67
  485.7 13.3 %multiply_convert_fusion.5 = bf16[4,1152,1152]{1,2,0:T(8,128)(2,1)} fusion(f32[4,1152,1152]{1,2,0:T(8,128)} %get-tuple-element.434, f32[4,1152,1152]{1,2,0:T(8,128)S(1)} %fusion.137, f32[4,1152]{1,0:T(4,128)} %get-tuple-element.435), kind=kLoop, calls=%fused_computation.19.clone.1 | loop fusion | flops 15925248 | bytes 53102592 | tf_op jit(solution)/shard_map/while/body/eval_jaxpr/while/body/eval_jaxpr/convert_element_type | solution.py:104
  499.0 11.5 %fusion.138 = bf16[4,64,1152]{2,1,0:T(8,128)(2,1)} fusion(bf16[1152,4,64]{0,2,1:T(8,128)(2,1)} %bitcast.210, f32[4,1152,1152]{1,2,0:T(8,128)} %get-tuple-element.434), kind=kOutput, calls=%fused_computation.28.clone.1 | convolution fusion | flops 685080576 | bytes 22413312 | tf_op jit(solution)/shard_map/while/body/eval_jaxpr/while/body/eval_jaxpr/hqk,qhd->khd/dot_general | solution.py:97
  512.4 3.3 fusion.139
  528.8 12.7 %multiply_reduce_fusion.4 = (f32[4,1152]{1,0:T(4,128)}, f32[4,1152,1152]{1,2,0:T(8,128)}) fusion(f32[4,1152,1152]{1,2,0:T(8,128)S(1)} %fusion.137, f32[4,1152]{1,0:T(4,128)S(1)} %dynamic-slice_bitcast_fusion.2, bf16[1152,4,64]{0,2,1:T(8,128)(2,1)} %bitcast.212, bf16[1152,4,64]{0,2,1:T(8,128)(2,1)} %bitcast.214, ...), kind=kOutput, calls=%fused_computation.20.clone.1 | convolution fusion | flops 706014720 | bytes 45010944 | tf_op jit(solution)/shard_map/while/body/eval_jaxpr/while/body/eval_jaxpr/qhd,khd->hqk/dot_general | solution.py:67
  541.5 13.3 %multiply_convert_fusion.5 = bf16[4,1152,1152]{1,2,0:T(8,128)(2,1)} fusion(f32[4,1152,1152]{1,2,0:T(8,128)} %get-tuple-element.434, f32[4,1152,1152]{1,2,0:T(8,128)S(1)} %fusion.137, f32[4,1152]{1,0:T(4,128)} %get-tuple-element.435), kind=kLoop, calls=%fused_computation.19.clone.1 | loop fusion | flops 15925248 | bytes 53102592 | tf_op jit(solution)/shard_map/while/body/eval_jaxpr/while/body/eval_jaxpr/convert_element_type | solution.py:104
  554.8 11.5 %fusion.138 = bf16[4,64,1152]{2,1,0:T(8,128)(2,1)} fusion(bf16[1152,4,64]{0,2,1:T(8,128)(2,1)} %bitcast.210, f32[4,1152,1152]{1,2,0:T(8,128)} %get-tuple-element.434), kind=kOutput, calls=%fused_computation.28.clone.1 | convolution fusion | flops 685080576 | bytes 22413312 | tf_op jit(solution)/shard_map/while/body/eval_jaxpr/while/body/eval_jaxpr/hqk,qhd->khd/dot_general | solution.py:97
  568.1 3.3 fusion.139
  572.9 14.7 %fusion.33 = (bf16[1024]{0:T(1024)(128)(2,1)S(1)}, f32[1152]{0:T(1024)S(1)}, f32[1152,1024,1]{0,1,2:T(8,128)}) fusion(bf16[1152,1024]{0,1:T(8,128)(2,1)} %copy-done.6, f32[1152]{0:T(1024)S(1)} %copy-done.29, f32[1024]{0:T(1024)} %bitcast.232, bf16[3,1024,1024]{2,1,0:T(8,128)(2,1)} %all-gather.7.cloned.1.call-done, bf16[3,1152,1024]{1,2,0:T(8,128)(2,1)} %bitcast.236), kind=kOutput, calls=%fused_computation.70 | convolution fusion | flops 7256012800 | bytes 20462592 | tf_op jit(solution)/shard_map/cre,cde->rd/dot_general | solution.py:272
  588.6 7.5 convolution_convert_fusion.3
  596.2 12.5 %convolution_convert_fusion = bf16[2816,1024]{1,0:T(8,128)(2,1)} fusion(bf16[1152,2816]{1,0:T(8,128)(2,1)} %get-tuple-element.326, bf16[1152,1024]{0,1:T(8,128)(2,1)S(1)} %copy-done.10, f32[1152]{0:T(1024)S(1)} %copy-done.25), kind=kOutput, calls=%fused_computation.66 | convolution fusion | flops 6650200064 | bytes 14619136 | tf_op jit(solution)/shard_map/rf,rd->fd/dot_general | solution.py:251
  610.4 13.6 %convolution_convert_fusion.2 = bf16[1024,3,1024]{2,0,1:T(8,128)(2,1)} fusion(bf16[3,1152,1024]{1,2,0:T(8,128)(2,1)} %bitcast.237, bf16[1152,1024]{0,1:T(8,128)(2,1)S(1)} %copy-done.7, f32[1024]{0:T(1024)S(1)} %bitcast.233, f32[1152]{0:T(1024)S(1)} %copy-done.29), kind=kOutput, calls=%fused_computation.86 | convolution fusion | flops 7255621632 | bytes 15737344 | tf_op jit(solution)/shard_map/rd,cre->dce/dot_general | solution.py:271
  624.7 22.2 %fusion.27 = bf16[1024,2,2816]{2,0,1:T(8,128)(2,1)} fusion(bf16[1,1152,2816]{2,1,0:T(8,128)(2,1)} %get-tuple-element.325, bf16[1,1152,2816]{2,1,0:T(8,128)(2,1)} %get-tuple-element.324, f32[1152,1024]{0,1:T(8,128)} %get-tuple-element.333, f32[1024]{0:T(1024)S(1)} %bitcast.230, f32[1152]{0:T(1024)S(1)} %copy-done.27), kind=kOutput, calls=%fused_computation.60 | convolution fusion | flops 13322813440 | bytes 29237760 | tf_op jit(solution)/shard_map/rd,crf->cdf/dot_general | solution.py:256
  647.6 59.3 %reduce-scatter.21.cloned.1.call-done = bf16[64,1024]{1,0:T(8,128)(2,1)} async-done(((bf16[1024,1024]{1,0:T(8,128)(2,1)}), bf16[64,1024]{1,0:T(8,128)(2,1)}) %reduce-scatter.21.cloned.1.call-update) | async-done | bytes 131088 | tf_op jit(solution)/shard_map/reduce_scatter | solution.py:284
  706.9 84.9 %reduce-scatter.27.cloned.1.call-done = bf16[176,1024]{1,0:T(8,128)(2,1)} async-done(((bf16[2816,1024]{1,0:T(8,128)(2,1)}), bf16[176,1024]{1,0:T(8,128)(2,1)}) %reduce-scatter.27.cloned.1.call-update) | async-done | bytes 360464 | tf_op jit(solution)/shard_map/reduce_scatter | solution.py:290
  791.9 88.8 %reduce-scatter.17.cloned.1.call-done = bf16[64,3,1024]{2,0,1:T(8,128)(2,1)} async-done(((bf16[1024,3,1024]{2,0,1:T(8,128)(2,1)}), bf16[64,3,1024]{2,0,1:T(8,128)(2,1)}) %reduce-scatter.17.cloned.1.call-update) | async-done | bytes 393232 | tf_op jit(solution)/shard_map/reduce_scatter | solution.py:281
  880.8 13.6 %add_convert_fusion = bf16[1152,1024]{0,1:T(8,128)(2,1)} fusion(f32[1152,1024]{0,1:T(8,128)} %get-tuple-element.333, bf16[1152,2816]{1,0:T(8,128)(2,1)} %get-tuple-element.326, bf16[2816,1024]{1,0:T(8,128)(2,1)} %all-gather.13.cloned.1.call-done), kind=kOutput, calls=%fused_computation.82 | convolution fusion | flops 6646136832 | bytes 19333120 | tf_op jit(solution)/shard_map/dot_general | solution.py:234
  894.4 115.8 %reduce-scatter.25.cloned.1.call-done = bf16[64,2,2816]{2,0,1:T(8,128)(2,1)} async-done(((bf16[1024,2,2816]{2,0,1:T(8,128)(2,1)}), bf16[64,2,2816]{2,0,1:T(8,128)(2,1)}) %reduce-scatter.25.cloned.1.call-update) | async-done | bytes 720912 | tf_op jit(solution)/shard_map/reduce_scatter | solution.py:287
  1010.2 4.2 copy.123
  1014.4 3.5 reshape.286
  1018.0 7.1 fusion.35
  1025.1 4.3 copy.104
  1029.4 6.2 copy.105
  1038.9 10.6 reduce-scatter.29.cloned.1.call-done
  1051.8 13.1 %reduce-scatter.19.cloned.1.call-done = bf16[64,3,512]{2,0,1:T(8,128)(2,1)} async-done(((bf16[64,3,1024]{2,0,1:T(8,128)(2,1)}), bf16[64,3,512]{2,0,1:T(8,128)(2,1)}) %reduce-scatter.19.cloned.1.call-update) | async-done | bytes 196624 | tf_op jit(solution)/shard_map/reduce_scatter | solution.py:298
  1067.4 17.0 %reduce-scatter.31.cloned.1.call-done = bf16[1408,128]{1,0:T(8,128)(2,1)} async-done(((bf16[2816,128]{1,0:T(8,128)(2,1)}), bf16[1408,128]{1,0:T(8,128)(2,1)}) %reduce-scatter.31.cloned.1.call-update) | async-done | bytes 360464
  (274 shorter events, 110.4 us)
Async XLA Ops:
  7.2 26.4 %copy-start.13 = (f32[176,512]{1,0:T(8,128)S(1)}, f32[176,512]{1,0:T(8,128)}, u32[]{:S(2)}) copy-start(f32[176,512]{1,0:T(8,128)} %param.30) | copy-start | bytes 1081348
  7.2 33.4 %copy-start.35 = (s32[1,3]{1,0:T(1,128)S(1)}, s32[1,3]{1,0:T(1,128)}, u32[]{:S(2)}) copy-start(s32[1,3]{1,0:T(1,128)} %param.26) | copy-start | bytes 40
  7.2 39.2 %copy-start.37 = (f32[2,32]{1,0:T(2,128)S(1)}, f32[2,32]{1,0:T(2,128)}, u32[]{:S(2)}) copy-start(f32[2,32]{1,0:T(2,128)} %param.31) | copy-start | bytes 772
  7.2 74.2 %all-gather.7.cloned.1.call-start = ((), (), s32[]{:S(2)}) async-start(), calls=%async_computation.10 | async-start | bytes 6684672 | tf_op jit(solution)/shard_map/all_gather | solution.py:213
  17.0 205.7 %all-gather.9.cloned.1.call-start = ((), (), s32[]{:S(2)}) async-start(), calls=%async_computation.11 | async-start | bytes 2228224 | tf_op jit(solution)/shard_map/all_gather | solution.py:214
  23.1 208.0 %all-gather.11.cloned.1.call-start = ((), (), s32[]{:S(2)}) async-start(), calls=%async_computation.12 | async-start | bytes 12255232 | tf_op jit(solution)/shard_map/all_gather | solution.py:215
  33.5 244.2 %all-gather.13.cloned.1.call-start = ((), (), s32[]{:S(2)}) async-start(), calls=%async_computation.13 | async-start | bytes 6127616 | tf_op jit(solution)/shard_map/all_gather | solution.py:216
  39.9 607.1 %reduce-scatter.33.cloned.1.call-start = ((), (), s32[]{:S(2)}) async-start(), calls=%async_computation.22 | async-start | bytes 278528
  73.1 8.3 copy-start.33
  76.1 17.9 %copy-start.6 = (bf16[1152,1024]{0,1:T(8,128)(2,1)}, bf16[1152,1024]{0,1:T(8,128)(2,1)S(1)}, u32[]{:S(2)}) copy-start(bf16[1152,1024]{0,1:T(8,128)(2,1)S(1)} %copy.87) | copy-start | bytes 7077892
  76.7 17.3 %copy-start.22 = (f32[1152]{0:T(1024)}, f32[1152]{0:T(1024)S(1)}, u32[]{:S(2)}) copy-start(f32[1152]{0:T(1024)S(1)} %fusion.36) | copy-start | bytes 13828
  76.7 17.3 %copy-start.28 = (f32[1152]{0:T(1024)}, f32[1152]{0:T(1024)S(1)}, u32[]{:S(2)}) copy-start(f32[1152]{0:T(1024)S(1)} %fusion.59) | copy-start | bytes 13828
  113.2 7.2 copy-start.1
  142.8 7.1 copy-start.1
  172.4 7.1 copy-start.1
  202.0 7.2 copy-start.1
  222.8 8.3 copy-start.30
  231.0 109.0 %copy-start.26 = (f32[1152]{0:T(1024)}, f32[1152]{0:T(1024)S(1)}, u32[]{:S(2)}) copy-start(f32[1152]{0:T(1024)S(1)} %fusion.60) | copy-start | bytes 13828
  231.0 46.7 %copy-start.9 = (bf16[1152,1024]{0,1:T(8,128)(2,1)S(1)}, bf16[1152,1024]{0,1:T(8,128)(2,1)}, u32[]{:S(2)}) copy-start(bf16[1152,1024]{0,1:T(8,128)(2,1)} %copy.94) | copy-start | bytes 7077892
  231.0 46.7 %copy-start.24 = (f32[1152]{0:T(1024)S(1)}, f32[1152]{0:T(1024)}, u32[]{:S(2)}) copy-start(f32[1152]{0:T(1024)} %compare_convert_fusion) | copy-start | bytes 13828
  340.0 5.2 copy-start.41
  349.3 223.6 %copy-start.29 = (f32[1152]{0:T(1024)S(1)}, f32[1152]{0:T(1024)}, u32[]{:S(2)}) copy-start(f32[1152]{0:T(1024)} %copy-done.28) | copy-start | bytes 13828
  349.7 8.8 copy-start.20
  349.7 8.8 copy-start.42
  387.4 11.5 %copy-start = (bf16[4,1152,1152]{1,2,0:T(8,128)(2,1)S(1)}, bf16[4,1152,1152]{1,2,0:T(8,128)(2,1)}, u32[]{:S(2)}) copy-start(bf16[4,1152,1152]{1,2,0:T(8,128)(2,1)} %multiply_convert_fusion.5) | copy-start | bytes 31850500 | tf_op jit(solution)/shard_map/while/body/eval_jaxpr/while
  387.5 11.5 %copy-start.4 = (bf16[1,1152,256]{1,2,0:T(8,128)(2,1)S(1)}, bf16[1,1152,256]{1,2,0:T(8,128)(2,1)}, u32[]{:S(2)}) copy-start(bf16[1,1152,256]{1,2,0:T(8,128)(2,1)} %get-tuple-element.433) | copy-start | bytes 1769476 | tf_op jit(solution)/shard_map/while/body/eval_jaxpr/while
  405.5 8.8 copy-start.20
  405.5 8.8 copy-start.42
  443.2 11.5 %copy-start = (bf16[4,1152,1152]{1,2,0:T(8,128)(2,1)S(1)}, bf16[4,1152,1152]{1,2,0:T(8,128)(2,1)}, u32[]{:S(2)}) copy-start(bf16[4,1152,1152]{1,2,0:T(8,128)(2,1)} %multiply_convert_fusion.5) | copy-start | bytes 31850500 | tf_op jit(solution)/shard_map/while/body/eval_jaxpr/while
  443.2 11.5 %copy-start.4 = (bf16[1,1152,256]{1,2,0:T(8,128)(2,1)S(1)}, bf16[1,1152,256]{1,2,0:T(8,128)(2,1)}, u32[]{:S(2)}) copy-start(bf16[1,1152,256]{1,2,0:T(8,128)(2,1)} %get-tuple-element.433) | copy-start | bytes 1769476 | tf_op jit(solution)/shard_map/while/body/eval_jaxpr/while
  461.3 8.8 copy-start.20
  461.3 8.8 copy-start.42
  499.0 11.5 %copy-start = (bf16[4,1152,1152]{1,2,0:T(8,128)(2,1)S(1)}, bf16[4,1152,1152]{1,2,0:T(8,128)(2,1)}, u32[]{:S(2)}) copy-start(bf16[4,1152,1152]{1,2,0:T(8,128)(2,1)} %multiply_convert_fusion.5) | copy-start | bytes 31850500 | tf_op jit(solution)/shard_map/while/body/eval_jaxpr/while
  499.0 11.5 %copy-start.4 = (bf16[1,1152,256]{1,2,0:T(8,128)(2,1)S(1)}, bf16[1,1152,256]{1,2,0:T(8,128)(2,1)}, u32[]{:S(2)}) copy-start(bf16[1,1152,256]{1,2,0:T(8,128)(2,1)} %get-tuple-element.433) | copy-start | bytes 1769476 | tf_op jit(solution)/shard_map/while/body/eval_jaxpr/while
  517.1 8.8 copy-start.20
  517.1 8.8 copy-start.42
  554.8 11.5 %copy-start = (bf16[4,1152,1152]{1,2,0:T(8,128)(2,1)S(1)}, bf16[4,1152,1152]{1,2,0:T(8,128)(2,1)}, u32[]{:S(2)}) copy-start(bf16[4,1152,1152]{1,2,0:T(8,128)(2,1)} %multiply_convert_fusion.5) | copy-start | bytes 31850500 | tf_op jit(solution)/shard_map/while/body/eval_jaxpr/while
  554.8 11.5 %copy-start.4 = (bf16[1,1152,256]{1,2,0:T(8,128)(2,1)S(1)}, bf16[1,1152,256]{1,2,0:T(8,128)(2,1)}, u32[]{:S(2)}) copy-start(bf16[1,1152,256]{1,2,0:T(8,128)(2,1)} %get-tuple-element.433) | copy-start | bytes 1769476 | tf_op jit(solution)/shard_map/while/body/eval_jaxpr/while
  568.1 4.8 copy-start.21
  572.9 14.7 %copy-start.32 = (bf16[1024,1]{0,1:T(2,128)(2,1)S(1)}, bf16[1024,1]{0,1:T(2,128)(2,1)}, u32[]{:S(2)}) copy-start(bf16[1024,1]{0,1:T(2,128)(2,1)} %stack.37) | copy-start | bytes 6148
  588.6 7.6 copy-start.10
  588.6 7.6 copy-start.25
  588.6 118.3 %reduce-scatter.21.cloned.1.call-start = ((), (), s32[]{:S(2)}) async-start(), calls=%async_computation.16 | async-start | bytes 2228224 | tf_op jit(solution)/shard_map/reduce_scatter | solution.py:284
  596.1 195.7 %reduce-scatter.27.cloned.1.call-start = ((), (), s32[]{:S(2)}) async-start(), calls=%async_computation.19 | async-start | bytes 6127616 | tf_op jit(solution)/shard_map/reduce_scatter | solution.py:290
  608.7 272.0 %reduce-scatter.17.cloned.1.call-start = ((), (), s32[]{:S(2)}) async-start(), calls=%async_computation.14 | async-start | bytes 6684672 | tf_op jit(solution)/shard_map/reduce_scatter | solution.py:281
  624.0 386.2 %reduce-scatter.25.cloned.1.call-start = ((), (), s32[]{:S(2)}) async-start(), calls=%async_computation.18 | async-start | bytes 12255232 | tf_op jit(solution)/shard_map/reduce_scatter | solution.py:287
  646.9 388.7 %reduce-scatter.35.cloned.1.call-start = ((), (), s32[]{:S(2)}) async-start(), calls=%async_computation.23 | async-start | bytes 24576
  647.5 389.7 %reduce-scatter.23.cloned.1.call-start = ((), (), s32[]{:S(2)}) async-start(), calls=%async_computation.17 | async-start | bytes 196608 | tf_op jit(solution)/shard_map/reduce_scatter | solution.py:301
  706.9 342.6 %reduce-scatter.29.cloned.1.call-start = ((), (), s32[]{:S(2)}) async-start(), calls=%async_computation.20 | async-start | bytes 540672 | tf_op jit(solution)/shard_map/reduce_scatter | solution.py:307
  791.9 273.1 %reduce-scatter.19.cloned.1.call-start = ((), (), s32[]{:S(2)}) async-start(), calls=%async_computation.15 | async-start | bytes 589824 | tf_op jit(solution)/shard_map/reduce_scatter | solution.py:298
  880.7 13.7 %copy-start.23 = (f32[1152]{0:T(1024)S(1)}, f32[1152]{0:T(1024)}, u32[]{:S(2)}) copy-start(f32[1152]{0:T(1024)} %copy-done.22) | copy-start | bytes 13828
  880.7 203.7 %reduce-scatter.31.cloned.1.call-start = ((), (), s32[]{:S(2)}) async-start(), calls=%async_computation.21 | async-start | bytes 1081344
  1029.4 7.2 copy-start.38
  1029.4 7.2 copy-start.39
  1029.4 7.2 copy-start.40
  1029.4 7.8 copy-start.17
  1029.4 7.8 copy-start.18
  1029.4 7.8 copy-start.19
  1029.4 20.1 %copy-start.14 = (f32[176,512]{1,0:T(8,128)S(1)}, f32[176,512]{1,0:T(8,128)}, u32[]{:S(2)}) copy-start(f32[176,512]{1,0:T(8,128)} %param.30) | copy-start | bytes 1081348
  1029.4 35.5 %copy-start.12 = (f32[3,64,512]{2,1,0:T(8,128)S(1)}, f32[3,64,512]{2,1,0:T(8,128)}, u32[]{:S(2)}) copy-start(f32[3,64,512]{2,1,0:T(8,128)} %param.27) | copy-start | bytes 1179652
  1035.6 51.8 %copy-start.11 = (f32[2,64,1408]{2,1,0:T(8,128)S(1)}, f32[2,64,1408]{2,1,0:T(8,128)}, u32[]{:S(2)}) copy-start(f32[2,64,1408]{2,1,0:T(8,128)} %param.29) | copy-start | bytes 2162692
  1035.6 51.8 %copy-start.15 = (f32[2,64,1408]{2,1,0:T(8,128)S(1)}, f32[2,64,1408]{2,1,0:T(8,128)}, u32[]{:S(2)}) copy-start(f32[2,64,1408]{2,1,0:T(8,128)} %param.39) | copy-start | bytes 2162692
  1035.6 51.8 %copy-start.16 = (f32[2,64,1408]{2,1,0:T(8,128)S(1)}, f32[2,64,1408]{2,1,0:T(8,128)}, u32[]{:S(2)}) copy-start(f32[2,64,1408]{2,1,0:T(8,128)} %param.34) | copy-start | bytes 2162692
  1036.6 52.6 %copy-start.36 = (f32[32,2]{0,1:T(2,128)}, f32[32,2]{0,1:T(2,128)S(1)}, u32[]{:S(2)}) copy-start(f32[32,2]{0,1:T(2,128)S(1)} %copy.132) | copy-start | bytes 772
  (24 other events, 76.1 us)
Sparse Core Ops, SparseCore 0:
  17.1 63.4 all-gather.6
  82.8 40.0 all-gather.8
  125.2 93.1 all-gather.10
  220.5 57.1 all-gather.12
  588.7 53.9 reduce-scatter.32
  646.2 60.5 reduce-scatter.20
  711.3 80.5 reduce-scatter.26
  796.3 84.3 reduce-scatter.16
  884.8 125.3 reduce-scatter.24
  1012.3 9.5 reduce-scatter.34
  1024.2 10.2 reduce-scatter.22
  1036.7 12.7 reduce-scatter.28
  1051.8 13.1 reduce-scatter.18
  1067.6 16.7 reduce-scatter.30
where the time goes:
time: 1110 us; the launch traced here: 1100 us
  waiting for transfers between devices  414 us (37%)
  matrix products  379 us (34%)
  local copies, waits for them, and re-layouts  110 us (10%)
  other arithmetic  107 us (10%)
  blocking collectives  55.1 us (5%)
  between operations  16.1 us (1%)
  loops' own time  14.2 us (1%)
    reduce_scatter x1, waiting for transfers between devices, local(): lax.psum_scatter(grad_ffin_rows.astype(jnp.bfloat16), 'dp', scatter_dimen...  116 us
    reduce_scatter x1, waiting for transfers between devices, local(): lax.psum_scatter(grad_qkv.astype(jnp.bfloat16), 'dp', scatter_dimension=0...  88.8 us
    reduce_scatter x1, waiting for transfers between devices, local(): lax.psum_scatter(grad_ffout.astype(jnp.bfloat16), 'dp', scatter_dimension...  84.9 us
    dot_general x8, matrix products, masked_scores(): jnp.einsum('qhd,khd->hqk', split_heads(query_cols), split_heads(key_cols)...  70.4 us
    reduce_scatter x1, waiting for transfers between devices, local(): lax.psum_scatter(grad_out.astype(jnp.bfloat16), 'dp', scatter_dimension=0...  59.3 us
    convert_element_type x4, other arithmetic, attend_backward(): grad_scores = (probs * (grad_probs - inner_sum)).astype(jnp.bfloat16)  53.2 us
    dot_general x4, matrix products, attend_backward(): jnp.einsum('hqk,qhd->khd', probs.astype(jnp.bfloat16), grad_heads, prefer...  46 us
    unnamed x81, local copies, waits for them, and re-layouts  43.2 us
  transfers between devices with their start and end apart: 14, of which 8 were waited for; matrix products, arithmetic and copies ran while one was open for 24% of the time, Pallas kernels for 0%

commit v1 on v0

v1 whole, which is shorter than its diff:
```python
import functools

import jax
import jax.numpy as jnp
from jax import lax
from jax.experimental import pallas as pl
from jax.experimental.pallas import tpu as pltpu
from jax.sharding import PartitionSpec as P

HEADS = 16
DK = 64
SHORT_PATCH = 256
STEP = 10
HD = 1024
SLOT = 384
LONG = 1152
LONG_PATCH = 1024

norm_eps = 1e-06
score_scale = 0.125
beta_one = 0.9
beta_two = 0.999
adam_eps = 1e-08
decay_rate = 0.01
rates = (0.08, 0.8, 0.08, 0.05, 0.6)

BF = jnp.bfloat16
F32 = jnp.float32
PAIRS = HD // 128
NN = (((1,), (0,)), ((), ()))
NT = (((1,), (1,)), ((), ()))
TN = (((0,), (0,)), ((), ()))
AXES = ("dp", "narrow")
VMEM_BYTES = 60 * 2**20
ROWS_GAIN = 16
FF_BLOCK = 256
QUERY_BLOCK = 384


def dot(left, right, dims=NN):
    return lax.dot_general(left, right, dims, preferred_element_type=F32)


def params():
    return pltpu.CompilerParams(vmem_limit_bytes=VMEM_BYTES)


def shape(dims, dtype):
    return jax.ShapeDtypeStruct(dims, dtype)


IN_VMEM = pl.BlockSpec(memory_space=pltpu.VMEM)
IN_HBM = pl.BlockSpec(memory_space=pl.ANY)
IN_SMEM = pl.BlockSpec(memory_space=pltpu.SMEM)


def exchange_perms():
    steps = []
    for kinds in (("z2", "z1"), ("z1", "z2"), ("x", "y"), ("y", "x"), ("core", "core")):
        perm = []
        for z in range(4):
            for x in range(2):
                for core in range(2):
                    for y in range(2):
                        kind = kinds[core]
                        to = [z, x, core, y]
                        if kind == "z2":
                            to[0] ^= 2
                        elif kind == "z1":
                            to[0] ^= 1
                        elif kind == "x":
                            to[1] ^= 1
                        elif kind == "y":
                            to[3] ^= 1
                        else:
                            to[2] ^= 1
                        perm.append(
                            (
                                ((z * 2 + x) * 2 + core) * 2 + y,
                                ((to[0] * 2 + to[1]) * 2 + to[2]) * 2 + to[3],
                            )
                        )
        steps.append(perm)
    return steps


def place_table(fast):
    if not fast:
        return jnp.zeros((1, 2), jnp.int32)
    dp = lax.axis_index("dp")
    narrow = lax.axis_index("narrow")
    z, x, core = dp // 4, (dp // 2) % 2, dp % 2
    rows = []
    for place in range(32):
        one, two, three, four, five = [(place >> bit) & 1 for bit in range(5)]
        core_of = core ^ five
        first = core_of == 0
        z_of = z ^ jnp.where(first, 2 * one + two, one + 2 * two)
        x_of = x ^ jnp.where(first, three, four)
        y_of = narrow ^ jnp.where(first, four, three)
        rows.append(jnp.stack(((z_of * 2 + x_of) * 2 + core_of, y_of)))
    return jnp.stack(rows).astype(jnp.int32)


def gather(piece, perms):
    held = piece[None]
    for perm in perms[:3]:
        held = jnp.concatenate((held, lax.ppermute(held, AXES, perm)), axis=0)
    more = lax.ppermute(held, AXES, perms[3])
    return (held, more, lax.ppermute(held, AXES, perms[4]), lax.ppermute(more, AXES, perms[4]))


def reduce_to_owner(blocks, perms):
    keep, pass_on, away, away_on = blocks
    other_on = lax.ppermute(away_on, AXES, perms[4])
    other = lax.ppermute(away, AXES, perms[4])
    sent = (pass_on.astype(F32) + other_on.astype(F32)).astype(BF)
    parts = [keep, other, lax.ppermute(sent, AXES, perms[3])]
    for perm, low, high in ((perms[2], 4, 8), (perms[1], 2, 4), (perms[0], 1, 2)):
        sent = sum(part[low:high].astype(F32) for part in parts).astype(BF)
        parts.append(lax.ppermute(sent, AXES, perm))
    return sum(part[0].astype(F32) for part in parts)


def place_of(index):
    return index // 8, index % 8


def each_place(table, sources, fast, body):
    if not fast:
        body(sources[0].at[0], 0, 0)
        return
    for index in range(32):
        array, slot = place_of(index)
        body(sources[array].at[slot], table[index, 0], table[index, 1])


def rows_of(start, size, unit):
    if isinstance(start, int):
        return pl.ds(start * size, size)
    return pl.ds(pl.multiple_of(start * size, unit), size)


def project_kernel(fast, row_piece, col_piece, table, x_ref, *refs):
    n_arrays = 4 if fast else 1
    arrays = refs[:n_arrays]
    out_ref, normed_t_ref, gains_ref, weight, gain_parts, normed, sem, gain_sem = refs[n_arrays:]
    step = pl.program_id(0)

    @pl.when(step == 0)
    def _():
        slots = 8 if fast else 1
        for index in range(n_arrays):
            pltpu.make_async_copy(
                arrays[index].at[:, pl.ds(row_piece, ROWS_GAIN), pl.ds(0, HD)],
                gain_parts.at[pl.ds(index * slots, slots)],
                gain_sem,
            ).start()

        def start(source, dp, narrow):
            pltpu.make_async_copy(
                source.at[pl.ds(0, row_piece)],
                weight.at[rows_of(dp, row_piece, 16), rows_of(narrow, col_piece, 128)],
                sem,
            ).start()

        each_place(table, arrays, fast, start)
        x = x_ref[...].astype(F32)
        scaled = x * lax.rsqrt(jnp.mean(x * x, axis=-1, keepdims=True) + norm_eps)
        pltpu.make_async_copy(gain_parts, gain_parts, gain_sem).wait()
        gains = jnp.sum(gain_parts[...].astype(F32), axis=0)
        gains_ref[...] = gains
        low = (scaled * gains[0:1]).astype(BF)
        normed[...] = low
        normed_t_ref[...] = low.T
        pltpu.make_async_copy(weight, weight, sem).wait()

    column = pl.multiple_of(step * 512, 512)
    out_ref[...] = dot(normed[...], weight[:, pl.ds(column, 512)]).astype(BF)


def project(tokens, arrays, table, fast, row_piece, col_piece):
    rows = tokens.shape[0]
    full = lambda dims: pl.BlockSpec(dims, lambda step: (0,) * len(dims))
    n_places = 32 if fast else 1
    return pl.pallas_call(
        functools.partial(project_kernel, fast, row_piece, col_piece),
        grid=(6,),
        in_specs=[IN_SMEM, full((rows, HD))] + [IN_HBM] * len(arrays),
        out_specs=[
            pl.BlockSpec((rows, 512), lambda step: (0, step)),
            full((HD, rows)),
            full((ROWS_GAIN, HD)),
        ],
        out_shape=[shape((rows, 3 * HD), BF), shape((HD, rows), BF), shape((ROWS_GAIN, HD), F32)],
        scratch_shapes=[
            pltpu.VMEM((HD, 3 * HD), BF),
            pltpu.VMEM((n_places, ROWS_GAIN, HD), BF),
            pltpu.VMEM((rows, HD), BF),
            pltpu.SemaphoreType.DMA(()),
            pltpu.SemaphoreType.DMA(()),
        ],
        compiler_params=params(),
        name="project",
    )(table, tokens, *arrays)


def three_parts(values):
    first = values.astype(BF)
    rest = values - first.astype(F32)
    second = rest.astype(BF)
    return first, second, (rest - second.astype(F32)).astype(BF)


def mask_operands(segments):
    kind = jnp.arange(64, dtype=jnp.int32)
    mine = segments[None, :] + 1 == kind[:, None]
    query_side = jnp.where(mine, -1e30, 0.0).astype(BF)
    key_side = jnp.where((kind[None, :] < 4) & ~mine.T, 1.0, 0.0).astype(BF)
    return (
        jnp.concatenate((query_side, query_side), axis=0),
        jnp.concatenate((key_side, key_side), axis=1),
    )


def attend_forward_kernel(q_ref, k_ref, v_ref, mask_q_ref, mask_k_ref, out_ref, extra_ref):
    queries_t = (q_ref[...].astype(F32) * score_scale).astype(BF).T
    keys = k_ref[...]
    values_t = v_ref[...].T
    mask_q = mask_q_ref[...]
    mask_k = mask_k_ref[...]
    lane = lax.broadcasted_iota(jnp.int32, (1, 128), 1)
    row = lax.broadcasted_iota(jnp.int32, (64, 1), 0)
    ones = jnp.ones((16, LONG), BF)
    outs = []
    extras = []
    for head in range(2):
        half = slice(64 * head, 64 * head + 64)
        if head == 0:
            key_side = jnp.where(lane < 64, keys, mask_k)
            query_side = jnp.concatenate((queries_t[half], mask_q[64:128]), axis=0)
        else:
            key_side = jnp.where(lane >= 64, keys, mask_k)
            query_side = jnp.concatenate((mask_q[0:64], queries_t[half]), axis=0)
        value_side = jnp.concatenate((values_t[half], ones), axis=0)
        out_blocks = []
        log_blocks = []
        for start in range(0, LONG, QUERY_BLOCK):
            scores = dot(key_side, query_side[:, start : start + QUERY_BLOCK])
            top = jnp.max(scores, axis=0, keepdims=True)
            expo = jnp.exp(scores - top).astype(BF)
            both = dot(value_side, expo)
            total = both[64:65]
            out_blocks.append((both[0:64] * (1.0 / total)).astype(BF))
            log_blocks.append(-(top + jnp.log(total)))
        outs.append(jnp.concatenate(out_blocks, axis=1))
        extra = mask_q[0:64].astype(F32)
        for index, part in enumerate(three_parts(jnp.concatenate(log_blocks, axis=1))):
            extra = jnp.where(row == 4 + index, part.astype(F32), extra)
        extras.append(extra.astype(BF))
    out_ref[...] = jnp.concatenate(outs, axis=0).T
    extra_ref[...] = jnp.concatenate((extras[1], extras[0]), axis=0).T


def tile_spec(rows, tiles_of, offset):
    return pl.BlockSpec(
        (rows, 128), lambda i: (0, (i // tiles_of) * 3 * tiles_of + offset * tiles_of + i % tiles_of)
    )


def attend_forward(projected, mask_q, mask_k, tiles_of):
    rows = projected.shape[0]
    tile = pl.BlockSpec((rows, 128), lambda i: (0, i))
    return pl.pallas_call(
        attend_forward_kernel,
        grid=(PAIRS,),
        in_specs=[
            tile_spec(rows, tiles_of, 0),
            tile_spec(rows, tiles_of, 1),
            tile_spec(rows, tiles_of, 2),
            pl.BlockSpec((128, rows), lambda i: (0, 0)),
            pl.BlockSpec((rows, 128), lambda i: (0, 0)),
        ],
        out_specs=[tile, tile],
        out_shape=[shape((rows, HD), BF), shape((rows, HD), BF)],
        compiler_params=params(),
        name="attend_forward",
    )(projected, projected, projected, mask_q, mask_k)


def attend_backward_kernel(
    q_ref, k_ref, v_ref, out_ref, grad_ref, extra_ref, mask_k_ref, grad_q_ref, grad_k_ref, grad_v_ref
):
    queries = (q_ref[...].astype(F32) * score_scale).astype(BF)
    queries_t = queries.T
    keys = k_ref[...]
    keys_t = keys.T
    values_t = v_ref[...].T
    grad = grad_ref[...]
    grad_t = grad.T
    extra = extra_ref[...]
    mask_k_t = mask_k_ref[...].T
    lane = lax.broadcasted_iota(jnp.int32, (1, 128), 1)
    row = lax.broadcasted_iota(jnp.int32, (64, 1), 0)
    product_t = (grad.astype(F32) * out_ref[...].astype(F32)).T
    inner = []
    for head in (1, 0):
        total = -jnp.sum(product_t[64 * head : 64 * head + 64], axis=0, keepdims=True)
        rows = jnp.zeros((64, LONG), F32)
        for index, part in enumerate(three_parts(total)):
            rows = jnp.where(row == index, part.astype(F32), rows)
        inner.append(rows.astype(BF))
    inner_cols = jnp.concatenate(inner, axis=0).T
    key_extra = jnp.where((row >= 4) & (row < 7), 1.0, mask_k_t[0:64].astype(F32)).astype(BF)
    value_extra = jnp.broadcast_to(jnp.where(row < 3, 1.0, 0.0).astype(BF), (64, LONG))
    grad_q = []
    grad_k = []
    grad_v = []
    for head in range(2):
        half = slice(64 * head, 64 * head + 64)
        own = (lane < 64) if head == 0 else (lane >= 64)
        query_side = jnp.where(own, queries, extra)
        grad_side = jnp.where(own, grad, inner_cols)
        if head == 0:
            key_side = jnp.concatenate((keys_t[half], key_extra), axis=0)
            value_side = jnp.concatenate((values_t[half], value_extra), axis=0)
        else:
            key_side = jnp.concatenate((key_extra, keys_t[half]), axis=0)
            value_side = jnp.concatenate((value_extra, values_t[half]), axis=0)
        q_blocks = []
        k_total = None
        v_total = None
        for start in range(0, LONG, QUERY_BLOCK):
            block = slice(start, start + QUERY_BLOCK)
            probs = jnp.exp(dot(query_side[block], key_side))
            grad_scores = (probs * dot(grad_side[block], value_side)).astype(BF)
            v_part = dot(grad_t[half, block], probs.astype(BF))
            k_part = dot(queries_t[half, block], grad_scores)
            v_total = v_part if v_total is None else v_total + v_part
            k_total = k_part if k_total is None else k_total + k_part
            q_blocks.append(dot(grad_scores, keys) * score_scale)
        grad_q.append(jnp.concatenate(q_blocks, axis=0))
        grad_k.append(k_total)
        grad_v.append(v_total)
    grad_q_ref[...] = jnp.where(lane < 64, grad_q[0], grad_q[1]).astype(BF)
    grad_k_ref[...] = jnp.concatenate(grad_k, axis=0).astype(BF).T
    grad_v_ref[...] = jnp.concatenate(grad_v, axis=0).astype(BF).T


def attend_backward(projected, attended, grad_attended, extra, mask_k, tiles_of):
    rows = projected.shape[0]
    tile = pl.BlockSpec((rows, 128), lambda i: (0, i))
    return pl.pallas_call(
        attend_backward_kernel,
        grid=(PAIRS,),
        in_specs=[
            tile_spec(rows, tiles_of, 0),
            tile_spec(rows, tiles_of, 1),
            tile_spec(rows, tiles_of, 2),
            tile,
            tile,
            tile,
            pl.BlockSpec((rows, 128), lambda i: (0, 0)),
        ],
        out_specs=[tile, tile, tile],
        out_shape=[shape((rows, HD), BF)] * 3,
        compiler_params=params(),
        name="attend_backward",
    )(projected, projected, projected, attended, grad_attended, extra, mask_k)


def middle_kernel(fast, sizes, table, x_ref, attended_ref, cotangent_ref, valid_ref, gains_ref, *refs):
    n_arrays = 4 if fast else 1
    row_d, row_f, col_d, col_f = sizes
    square, gates, ups = (refs[i * n_arrays : (i + 1) * n_arrays] for i in range(3))
    refs = refs[3 * n_arrays :]
    mixed_ref, grad_hidden_ref, grad_attended_ref = refs[:3]
    refs = refs[3:]
    grad_square, grad_gates, grad_ups = (refs[i * n_arrays : (i + 1) * n_arrays] for i in range(3))
    refs = refs[3 * n_arrays :]
    gain_grad_ref, w_out, w_gate, w_up, w_down, hidden, normed, normed_t, grad_mixed, grad_normed, sems, out_sem = refs

    def start(source, dp, narrow):
        pltpu.make_async_copy(
            source.at[pl.ds(0, row_d)], w_out.at[rows_of(dp, row_d, 16), rows_of(narrow, col_d, 128)], sems.at[0]
        ).start()

    each_place(table, square, fast, start)

    def start_gate(source, dp, narrow):
        pltpu.make_async_copy(
            source, w_gate.at[rows_of(dp, row_d, 16), rows_of(narrow, col_f, 128)], sems.at[1]
        ).start()

    each_place(table, gates, fast, start_gate)

    def start_up(source, dp, narrow):
        pltpu.make_async_copy(
            source, w_up.at[rows_of(dp, row_d, 16), rows_of(narrow, col_f, 128)], sems.at[2]
        ).start()

    each_place(table, ups, fast, start_up)

    def start_down(source, dp, narrow):
        pltpu.make_async_copy(
            source.at[pl.ds(row_d, row_f)],
            w_down.at[rows_of(dp, row_f, 16), rows_of(narrow, col_d, 128)],
            sems.at[3],
        ).start()

    each_place(table, square, fast, start_down)
    gain = gains_ref[1:2]
    pltpu.make_async_copy(w_out, w_out, sems.at[0]).wait()
    mixed_sum = grad_hidden_ref

    def before(index, carry):
        part = pl.ds(pl.multiple_of(index * QUERY_BLOCK, QUERY_BLOCK), QUERY_BLOCK)
        state = x_ref[part, :].astype(F32) + dot(attended_ref[part, :], w_out[...])
        hidden[part, :] = state
        mixed_sum[part, :] = state
        low = (state * lax.rsqrt(jnp.mean(state * state, axis=-1, keepdims=True) + norm_eps) * gain).astype(BF)
        normed[part, :] = low
        normed_t[:, part] = low.T
        grad_mixed[part, :] = (cotangent_ref[part, :].astype(F32) * valid_ref[part, :]).astype(BF)
        return carry

    lax.fori_loop(0, x_ref.shape[0] // QUERY_BLOCK, before, 0)
    grad_normed[...] = jnp.zeros_like(grad_normed)
    pltpu.make_async_copy(w_gate, w_gate, sems.at[1]).wait()
    pltpu.make_async_copy(w_up, w_up, sems.at[2]).wait()
    pltpu.make_async_copy(w_down, w_down, sems.at[3]).wait()

    def block(index, carry):
        cols = pl.ds(pl.multiple_of(index * FF_BLOCK, FF_BLOCK), FF_BLOCK)
        gate_w = w_gate[:, cols]
        up_w = w_up[:, cols]
        down_w = w_down[cols, :]
        gate = dot(normed[...], gate_w)
        upward = dot(normed[...], up_w)
        grad_inner = dot(grad_mixed[...], down_w, NT)
        square_gate = gate * gate
        curve = jnp.tanh(0.7978845608028654 * gate * (1.0 + 0.044715 * square_gate))
        half = 0.5 * (1.0 + curve)
        active = gate * half
        slope = half + (0.5 * gate) * (1.0 - curve * curve) * (
            0.7978845608028654 + (0.7978845608028654 * 3.0 * 0.044715) * square_gate
        )
        inner = (active * upward).astype(BF)
        grad_gate = (grad_inner * upward * slope).astype(BF)
        grad_up = (grad_inner * active).astype(BF)
        mixed_sum[...] += dot(inner, down_w)
        grad_normed[...] += dot(grad_gate, gate_w, NT) + dot(grad_up, up_w, NT)
        w_down[cols, :] = dot(inner.T, grad_mixed[...]).astype(BF)
        w_gate[:, cols] = dot(normed_t[...], grad_gate).astype(BF)
        w_up[:, cols] = dot(normed_t[...], grad_up).astype(BF)
        return carry

    lax.fori_loop(0, w_gate.shape[1] // FF_BLOCK, block, 0)

    def finish_gate(target, dp, narrow):
        pltpu.make_async_copy(
            w_gate.at[rows_of(dp, row_d, 16), rows_of(narrow, col_f, 128)], target, out_sem.at[0]
        ).start()

    def finish_up(target, dp, narrow):
        pltpu.make_async_copy(
            w_up.at[rows_of(dp, row_d, 16), rows_of(narrow, col_f, 128)], target, out_sem.at[1]
        ).start()

    def finish_down(target, dp, narrow):
        pltpu.make_async_copy(
            w_down.at[rows_of(dp, row_f, 16), rows_of(narrow, col_d, 128)],
            target.at[pl.ds(row_d, row_f)],
            out_sem.at[2],
        ).start()

    def finish_out(target, dp, narrow):
        pltpu.make_async_copy(
            w_out.at[rows_of(dp, row_d, 16), rows_of(narrow, col_d, 128)],
            target.at[pl.ds(0, row_d)],
            out_sem.at[3],
        ).start()

    each_place(table, grad_gates, fast, finish_gate)
    each_place(table, grad_ups, fast, finish_up)
    each_place(table, grad_square, fast, finish_down)
    gain_grad_ref[...] = jnp.zeros_like(gain_grad_ref)

    def after(index, carry):
        part = pl.ds(pl.multiple_of(index * QUERY_BLOCK, QUERY_BLOCK), QUERY_BLOCK)
        mixed_ref[part, :] = mixed_sum[part, :].astype(BF)
        state = hidden[part, :]
        scale = lax.rsqrt(jnp.mean(state * state, axis=-1, keepdims=True) + norm_eps)
        unit = state * scale
        through = grad_normed[part, :]
        gain_grad_ref[...] += jnp.sum(through * unit, axis=0, keepdims=True)
        through = through * gain
        result = grad_mixed[part, :].astype(F32) + scale * (
            through - unit * jnp.mean(through * unit, axis=-1, keepdims=True)
        )
        grad_hidden_ref[part, :] = result
        branch = result.astype(BF)
        normed[part, :] = branch
        grad_attended_ref[part, :] = dot(branch, w_out[...], NT).astype(BF)
        return carry

    lax.fori_loop(0, x_ref.shape[0] // QUERY_BLOCK, after, 0)
    branch = normed[...]
    w_out[...] = dot(attended_ref[...].T, branch).astype(BF)
    each_place(table, grad_square, fast, finish_out)
    pltpu.make_async_copy(w_gate, w_gate, out_sem.at[0]).wait()
    pltpu.make_async_copy(w_up, w_up, out_sem.at[1]).wait()
    pltpu.make_async_copy(w_down, w_down, out_sem.at[2]).wait()
    pltpu.make_async_copy(w_out, w_out, out_sem.at[3]).wait()


def middle(tokens, attended, cotangent, valid, gains, square, gates, ups, table, fast, sizes):
    rows = tokens.shape[0]
    ff = sizes[1] * (16 if fast else 1)
    n_arrays = len(square)
    outs = pl.pallas_call(
        functools.partial(middle_kernel, fast, sizes),
        in_specs=[IN_SMEM] + [IN_VMEM] * 5 + [IN_HBM] * (3 * n_arrays),
        out_specs=[IN_VMEM] * 3 + [IN_HBM] * (3 * n_arrays) + [IN_VMEM],
        out_shape=[shape((rows, HD), BF), shape((rows, HD), F32), shape((rows, HD), BF)]
        + [shape(array.shape, BF) for array in (*square, *gates, *ups)]
        + [shape((1, HD), F32)],
        scratch_shapes=[
            pltpu.VMEM((HD, HD), BF),
            pltpu.VMEM((HD, ff), BF),
            pltpu.VMEM((HD, ff), BF),
            pltpu.VMEM((ff, HD), BF),
            pltpu.VMEM((rows, HD), F32),
            pltpu.VMEM((rows, HD), BF),
            pltpu.VMEM((HD, rows), BF),
            pltpu.VMEM((rows, HD), BF),
            pltpu.VMEM((rows, HD), F32),
            pltpu.SemaphoreType.DMA((4,)),
            pltpu.SemaphoreType.DMA((4,)),
        ],
        compiler_params=params(),
        name="middle",
    )(table, tokens, attended, cotangent, valid, gains, *square, *gates, *ups)
    mixed, grad_hidden, grad_attended = outs[:3]
    grads = [outs[3 + i * n_arrays : 3 + (i + 1) * n_arrays] for i in range(3)]
    return mixed, grad_hidden, grad_attended, *grads, outs[-1]


def weight_grad_kernel(fast, row_piece, col_piece, table, normed_t_ref, q_ref, k_ref, v_ref, *refs):
    n_arrays = 4 if fast else 1
    targets = refs[:n_arrays]
    weight, sem = refs[n_arrays:]
    ny = HD * 3 // col_piece if fast else HD // 128
    width = HD // ny
    left = normed_t_ref[...]
    for narrow in range(ny):
        for index, ref in enumerate((q_ref, k_ref, v_ref)):
            start = narrow * 3 * width + index * width
            weight[:, start : start + width] = dot(left, ref[:, narrow * width : (narrow + 1) * width]).astype(BF)

    def finish(target, dp, narrow):
        pltpu.make_async_copy(
            weight.at[rows_of(dp, row_piece, 16), rows_of(narrow, col_piece, 128)], target, sem
        ).start()

    each_place(table, targets, fast, finish)
    pltpu.make_async_copy(weight, weight, sem).wait()


def weight_grad(normed_t, grads, table, fast, row_piece, col_piece):
    if fast:
        outs = [shape((8, row_piece, col_piece), BF)] * 4
    else:
        outs = [shape((1, row_piece, col_piece), BF)]
    return pl.pallas_call(
        functools.partial(weight_grad_kernel, fast, row_piece, col_piece),
        in_specs=[IN_SMEM] + [IN_VMEM] * 4,
        out_specs=[IN_HBM] * len(outs),
        out_shape=outs,
        scratch_shapes=[pltpu.VMEM((HD, 3 * HD), BF), pltpu.SemaphoreType.DMA(())],
        compiler_params=params(),
        name="weight_grad",
    )(table, normed_t, *grads)


def input_grad_kernel(
    fast, row_piece, col_piece, ny, table, x_ref, gains_ref, grad_hidden_ref, q_ref, k_ref, v_ref, *refs
):
    n_arrays = 4 if fast else 1
    arrays = refs[:n_arrays]
    out_ref, gain_grad_ref, weight, sem = refs[n_arrays:]

    def start(source, dp, narrow):
        pltpu.make_async_copy(
            source.at[pl.ds(0, row_piece)],
            weight.at[rows_of(dp, row_piece, 16), rows_of(narrow, col_piece, 128)],
            sem,
        ).start()

    each_place(table, arrays, fast, start)
    x = x_ref[...].astype(F32)
    scale = lax.rsqrt(jnp.mean(x * x, axis=-1, keepdims=True) + norm_eps)
    pltpu.make_async_copy(weight, weight, sem).wait()
    width = HD // ny
    through = None
    for narrow in range(ny):
        for index, ref in enumerate((q_ref, k_ref, v_ref)):
            begin = narrow * 3 * width + index * width
            part = dot(ref[:, narrow * width : (narrow + 1) * width], weight[:, begin : begin + width], NT)
            through = part if through is None else through + part
    unit = x * scale
    gain_grad_ref[...] = jnp.sum(through * unit, axis=0, keepdims=True)
    through = through * gains_ref[0:1]
    out_ref[...] = grad_hidden_ref[...] + scale * (
        through - unit * jnp.mean(through * unit, axis=-1, keepdims=True)
    )


def input_gradient(tokens, gains, grad_hidden, grads, arrays, table, fast, row_piece, col_piece, ny):
    rows = tokens.shape[0]
    return pl.pallas_call(
        functools.partial(input_grad_kernel, fast, row_piece, col_piece, ny),
        in_specs=[IN_SMEM] + [IN_VMEM] * 6 + [IN_HBM] * len(arrays),
        out_specs=[IN_VMEM] * 2,
        out_shape=[shape((rows, HD), F32), shape((1, HD), F32)],
        scratch_shapes=[pltpu.VMEM((HD, 3 * HD), BF), pltpu.SemaphoreType.DMA(())],
        compiler_params=params(),
        name="input_gradient",
    )(table, tokens, gains, grad_hidden, *grads, *arrays)


def segment_ids(bucket_one, text_one):
    position = jnp.arange(LONG, dtype=jnp.int32)
    slot_index = position // SLOT
    inside = position - slot_index * SLOT
    slot_length = SHORT_PATCH + jnp.where(
        slot_index == 0, text_one[0], jnp.where(slot_index == 1, text_one[1], text_one[2])
    )
    long_valid = position < LONG_PATCH + text_one[0]
    short_valid = inside < slot_length
    return jnp.where(
        bucket_one == 1, jnp.where(long_valid, 0, -1), jnp.where(short_valid, slot_index, -1)
    ).astype(jnp.int32)


def adamw(weight, grad_total, first, second, rate):
    first_new = beta_one * first + (1.0 - beta_one) * grad_total
    second_new = beta_two * second + (1.0 - beta_two) * grad_total * grad_total
    first_hat = first_new / (1.0 - beta_one**STEP)
    second_hat = second_new / (1.0 - beta_two**STEP)
    weight_new = weight - rate * (first_hat / (jnp.sqrt(second_hat) + adam_eps) + decay_rate * weight)
    return (grad_total, first_new, second_new, weight_new)


def rows_of_shards(array, n_narrow):
    count, rows, columns = array.shape
    width = columns // n_narrow
    return array.reshape(count, rows, n_narrow, width).transpose(1, 2, 0, 3).reshape(rows, -1)


def local(
    n_dp,
    n_narrow,
    tokens,
    cotangent,
    bucket,
    text_lengths,
    attn_qkv,
    attn_out,
    ffn_in,
    ffn_out,
    norm_gains,
    first_qkv,
    first_out,
    first_ffin,
    first_ffout,
    first_gains,
    second_qkv,
    second_out,
    second_ffin,
    second_ffout,
    second_gains,
):
    fast = (n_dp, n_narrow) == (16, 2)
    perms = exchange_perms() if fast else None
    table = place_table(fast)
    me = lax.axis_index("dp") * n_narrow + lax.axis_index("narrow")
    row_d, width = attn_out.shape
    row_f = ffn_out.shape[0]
    col_f = ffn_in.shape[2]
    own_gains = norm_gains.shape[1]
    low_gains = lax.dynamic_update_slice(
        jnp.zeros((ROWS_GAIN, HD), BF), norm_gains.astype(BF), (0, me * own_gains)
    )
    if fast:
        low_qkv = attn_qkv.astype(BF).transpose(1, 0, 2).reshape(row_d, 3 * width)
        piece = jnp.concatenate((low_qkv, jnp.pad(low_gains, ((0, 0), (0, 3 * width - HD)))), axis=0)
        qkv_arrays = gather(piece, perms)
        square = gather(jnp.concatenate((attn_out.astype(BF), ffn_out.astype(BF)), axis=0), perms)
        gates = gather(ffn_in[0].astype(BF), perms)
        ups = gather(ffn_in[1].astype(BF), perms)
        sizes = (row_d, row_f, width, col_f)
        qkv_size = (row_d, 3 * width)
    else:
        whole = lambda low, axis: lax.all_gather(
            lax.all_gather(low.astype(BF), "narrow", axis=axis + 1, tiled=True), "dp", axis=axis, tiled=True
        )
        full_qkv = rows_of_shards(whole(attn_qkv, 1), n_narrow)
        gains_rows = jnp.pad(lax.psum(low_gains, AXES), ((0, 0), (0, 2 * HD)))
        qkv_arrays = (jnp.concatenate((full_qkv, gains_rows), axis=0)[None],)
        square = (jnp.concatenate((whole(attn_out, 0), whole(ffn_out, 0)), axis=0)[None],)
        full_ffin = whole(ffn_in, 1)
        gates = (full_ffin[0][None],)
        ups = (full_ffin[1][None],)
        sizes = (HD, full_ffin.shape[2], HD, full_ffin.shape[2])
        qkv_size = (HD, 3 * HD)
    tiles_of = width // 128
    segments = segment_ids(bucket[0], text_lengths[0])
    valid = (segments >= 0).astype(F32)[:, None]
    mask_q, mask_k = mask_operands(segments)
    projected, normed_t, gains = project(tokens, qkv_arrays, table, fast, *qkv_size)
    attended, extra = attend_forward(projected, mask_q, mask_k, tiles_of)
    mixed, grad_hidden, grad_attended, grad_square, grad_gates, grad_ups, gain_two = middle(
        tokens, attended, cotangent, valid, gains, square, gates, ups, table, fast, sizes
    )
    grads = attend_backward(projected, attended, grad_attended, extra, mask_k, tiles_of)
    grad_qkv = weight_grad(normed_t, grads, table, fast, *qkv_size)
    input_grad, gain_one = input_gradient(
        tokens, gains, grad_hidden, grads, qkv_arrays, table, fast, *qkv_size, n_narrow
    )
    gain_sums = lax.psum(jnp.concatenate((gain_one, gain_two), axis=0), AXES)
    share_gains = lax.dynamic_slice(gain_sums, (0, me * own_gains), (2, own_gains))
    if fast:
        share_square = reduce_to_owner(grad_square, perms)
        share_gate = reduce_to_owner(grad_gates, perms)
        share_up = reduce_to_owner(grad_ups, perms)
        share_qkv = reduce_to_owner(grad_qkv, perms).reshape(row_d, 3, width).transpose(1, 0, 2)
        share_out, share_down = share_square[:row_d], share_square[row_d:]
        share_ffin = jnp.stack((share_gate, share_up))
    else:
        own = lambda grad, axis: lax.psum_scatter(
            lax.psum_scatter(grad, "dp", scatter_dimension=axis, tiled=True),
            "narrow",
            scatter_dimension=axis + 1,
            tiled=True,
        ).astype(F32)
        ordered = grad_qkv[0][0].reshape(HD, n_narrow, 3, width).transpose(2, 0, 1, 3).reshape(3, HD, HD)
        share_qkv = own(ordered, 1)
        share_out = own(grad_square[0][0, :HD], 0)
        share_down = own(grad_square[0][0, HD:], 0)
        share_ffin = own(jnp.stack((grad_gates[0][0], grad_ups[0][0])), 1)
    shares = (share_qkv, share_out, share_ffin, share_down, share_gains)
    masters = (attn_qkv, attn_out, ffn_in, ffn_out, norm_gains)
    firsts = (first_qkv, first_out, first_ffin, first_ffout, first_gains)
    seconds = (second_qkv, second_out, second_ffin, second_ffout, second_gains)
    results = [mixed, input_grad]
    for index in range(5):
        results.extend(adamw(masters[index], shares[index], firsts[index], seconds[index], rates[index]))
    return tuple(results)


def solution(mesh):
    rows = P(("dp", "narrow"), None)
    cube = P(None, "dp", "narrow")
    flat = P("dp", "narrow")
    gain = P(None, ("dp", "narrow"))
    weights = (cube, flat, cube, flat, gain)
    in_specs = (rows, rows, P(("dp", "narrow")), rows, *weights, *weights, *weights)
    out_specs = (rows, rows, *(spec for spec in weights for _ in range(4)))
    step = functools.partial(local, mesh.shape["dp"], mesh.shape["narrow"])
    return jax.shard_map(step, mesh=mesh, in_specs=in_specs, out_specs=out_specs, check_vma=False)
```

time: 1110 us -> 600 us (0.54)
  matrix products: 379 us -> 0 us
  Pallas kernels: 0 us -> 238 us
  waiting for transfers between devices: 414 us -> 198 us
  local copies, waits for them, and re-layouts: 110 us -> 10.5 us
  other arithmetic: 107 us -> 51.9 us
  starting transfers between devices: 0.57 us -> 51.4 us
  blocking collectives: 55.1 us -> 39.9 us
  loops' own time: 14.2 us -> 0 us
  between operations: 16.1 us -> 3.32 us
    dot_general x40 -> x0, matrix products: 379 us -> none  [the longest x8 70.4 us: masked_scores(): jnp.einsum('qhd,khd->hqk', split_heads(query_cols), split_heads(key_cols)...]
    reduce_scatter x7 -> x0, waiting for transfers between devices: 373 us -> none  [the longest x1 116 us: local(): lax.psum_scatter(grad_ffin_rows.astype(jnp.bfloat16), 'dp', scatter_dimen...]
    pallas_call x0 -> x6, Pallas kernels: none -> 238 us  [the longest x1 93.8 us: middle(): pl.pallas_call(functools.partial(middle_kernel, fast, sizes), in_specs=[I...]
    ppermute x0 -> x48, waiting for transfers between devices: none -> 198 us  [the longest x12 71.1 us: gather(): held = jnp.concatenate((held, lax.ppermute(held, AXES, perm)), axis=0)]
    all_gather x6 -> x0, blocking collectives: 55.1 us -> none  [the longest x1 21.6 us: local(): lax.all_gather(wide_rows[4], 'dp', axis=1, tiled=True)]
    ppermute x0 -> x48, starting transfers between devices: none -> 51.4 us  [the longest x12 20 us: gather(): held = jnp.concatenate((held, lax.ppermute(held, AXES, perm)), axis=0)]
    convert_element_type x9 -> x22, other arithmetic: 58.9 us -> 18.2 us  [the longest x12 6.77 us: reduce_to_owner(): sent = sum((part[low:high].astype(F32) for part in parts)).astype(BF)]
    psum x0 -> x1, blocking collectives: none -> 39.9 us  [local(): gain_sums = lax.psum(jnp.concatenate((gain_one, gain_two), axis=0), AXES)]
  transfers between devices with their start and end apart: 14 -> 48, of which waited for: 8 -> 20; matrix products, arithmetic and copies ran while one was open for 24% -> 9% of each run, Pallas kernels for 0% -> 24%
where the time goes in v1:
time: 600 us; the launch traced here: 594 us
  Pallas kernels  238 us (40%)
  waiting for transfers between devices  198 us (33%)
  other arithmetic  51.9 us (9%)
  starting transfers between devices  51.4 us (9%)
  blocking collectives  39.9 us (7%)
  local copies, waits for them, and re-layouts  10.5 us (2%)
    pallas_call x1, Pallas kernels, middle(): pl.pallas_call(functools.partial(middle_kernel, fast, sizes), in_specs=[I...  93.8 us
    ppermute x12, waiting for transfers between devices, gather(): held = jnp.concatenate((held, lax.ppermute(held, AXES, perm)), axis=0)  71.1 us
    ppermute x4, waiting for transfers between devices, reduce_to_owner(): parts = [keep, other, lax.ppermute(sent, AXES, perms[3])]  56.6 us
    pallas_call x1, Pallas kernels, attend_backward(): pl.pallas_call(attend_backward_kernel, grid=(PAIRS,), in_specs=[tile_spec...  54.7 us
    ppermute x12, waiting for transfers between devices, reduce_to_owner(): parts.append(lax.ppermute(sent, AXES, perm))  41.9 us
    pallas_call x1, Pallas kernels, attend_forward(): pl.pallas_call(attend_forward_kernel, grid=(PAIRS,), in_specs=[tile_spec(...  40.9 us
    psum x1, blocking collectives, local(): gain_sums = lax.psum(jnp.concatenate((gain_one, gain_two), axis=0), AXES)  39.9 us
    ppermute x4, waiting for transfers between devices, gather(): more = lax.ppermute(held, AXES, perms[3])  28.8 us
  transfers between devices with their start and end apart: 48, of which 20 were waited for; matrix products, arithmetic and copies ran while one was open for 9% of the time, Pallas kernels for 24%

profile of v1, /device:TPU:0, one launch (start us, length us, event | category | flops | bytes accessed | tf_op | source)
XLA Modules:
  0.0 593.6 jit_solution(8864010001985096886)
XLA Ops:
  2.8 4.1 collective-permute-start
  6.9 5.6 collective-permute-done
  12.6 2.4 collective-permute-start.1
  15.1 3.5 collective-permute-start.12
  18.6 12.2 %collective-permute-done.1 = bf16[2,80,1536]{2,1,0:T(8,128)(2,1)S(1)} collective-permute-done((bf16[2,80,1536]{2,1,0:T(8,128)(2,1)S(1)}, bf16[2,80,1536]{2,1,0:T(8,128)(2,1)S(1)}, u32[]{:S(2)}, u32[]{:S(2)}) %collective-permute-start.1) | collective-permute-done | bytes 491552 | tf_op jit(solution)/shard_map/ppermute | solution.py:108
  30.9 1.9 collective-permute-start.2
  33.1 1.7 collective-permute-start.13
  34.8 17.8 %collective-permute-done.6 = bf16[1,240,512]{2,1,0:T(8,128)(2,1)S(1)} collective-permute-done((bf16[1,240,512]{2,1,0:T(8,128)(2,1)S(1)}, bf16[1,240,512]{2,1,0:T(8,128)(2,1)S(1)}, u32[]{:S(2)}, u32[]{:S(2)}) %collective-permute-start.6) | collective-permute-done | bytes 245792 | tf_op jit(solution)/shard_map/ppermute | solution.py:108
  52.8 1.5 collective-permute-start.14
  55.0 1.9 collective-permute-start.18
  56.9 8.9 %collective-permute-done.7 = bf16[2,240,512]{2,1,0:T(8,128)(2,1)S(1)} collective-permute-done((bf16[2,240,512]{2,1,0:T(8,128)(2,1)S(1)}, bf16[2,240,512]{2,1,0:T(8,128)(2,1)S(1)}, u32[]{:S(2)}, u32[]{:S(2)}) %collective-permute-start.7) | collective-permute-done | bytes 491552 | tf_op jit(solution)/shard_map/ppermute | solution.py:108
  66.9 1.5 collective-permute-start.8
  69.3 2.7 collective-permute-done.14
  72.1 1.5 pad_maximum_fusion.2.refs_4_
  73.7 5.1 collective-permute-done.19
  78.8 1.9 pad_maximum_fusion.7
  80.7 1.4 collective-permute-start.20
  82.1 11.0 %collective-permute-done.8 = bf16[4,240,512]{2,1,0:T(8,128)(2,1)} collective-permute-done((bf16[4,240,512]{2,1,0:T(8,128)(2,1)}, bf16[4,240,512]{2,1,0:T(8,128)(2,1)}, u32[]{:S(2)}, u32[]{:S(2)}) %collective-permute-start.8) | collective-permute-done | bytes 983072 | tf_op jit(solution)/shard_map/ppermute | solution.py:108
  93.2 2.7 pad_maximum_fusion.1.refs_0_
  100.9 7.6 %collective-permute-done.20 = bf16[4,64,1408]{2,1,0:T(8,128)(2,1)} collective-permute-done((bf16[4,64,1408]{2,1,0:T(8,128)(2,1)}, bf16[4,64,1408]{2,1,0:T(8,128)(2,1)}, u32[]{:S(2)}, u32[]{:S(2)}) %collective-permute-start.20) | collective-permute-done | bytes 720928 | tf_op jit(solution)/shard_map/ppermute | solution.py:108
  111.6 2.6 pad_maximum_fusion.3.refs_8_
  114.2 1.2 collective-permute-start.21
  120.4 1.9 select_add_fusion
  122.3 13.9 %collective-permute-done.15.refs_5_ = bf16[8,64,1408]{2,1,0:T(8,128)(2,1)} collective-permute-done((bf16[8,64,1408]{2,1,0:T(8,128)(2,1)S(1)}, bf16[8,64,1408]{2,1,0:T(8,128)(2,1)}, u32[]{:S(2)}, u32[]{:S(2)}) %collective-permute-start.15) | collective-permute-done | bytes 1441824 | tf_op jit(solution)/shard_map/ppermute | solution.py:109
  136.8 14.9 %collective-permute-done.21.refs_9_ = bf16[8,64,1408]{2,1,0:T(8,128)(2,1)} collective-permute-done((bf16[8,64,1408]{2,1,0:T(8,128)(2,1)}, bf16[8,64,1408]{2,1,0:T(8,128)(2,1)}, u32[]{:S(2)}, u32[]{:S(2)}) %collective-permute-start.21) | collective-permute-done | bytes 1441824 | tf_op jit(solution)/shard_map/ppermute | solution.py:109
  152.5 5.3 stack.442.table
  160.4 3.0 fusion.7.valid_ref
  163.4 14.4 %project.1 = (bf16[1152,3072]{1,0:T(8,128)(2,1)}, bf16[1024,1152]{1,0:T(8,128)(2,1)}, f32[16,1024]{1,0:T(8,128)}) custom-call(s32[32,2]{1,0:T(8,128)} %stack.442.table, bf16[1152,1024]{1,0:T(8,128)(2,1)} %x_ref.5, bf16[8,80,1536]{2,1,0:T(8,128)(2,1)} %copy-done, bf16[8,80,1536]{2,1,0:T(8,128)(2,1)} %collective-permute-done.3.refs_1_, ...), custom_call_target="tpu_custom_call" | custom-call | tf_op jit(solution)/shard_map/project/pallas_call | solution.py:186
  177.9 40.9 %attend_forward.1 = (bf16[1152,1024]{1,0:T(8,128)(2,1)}, bf16[1152,1024]{1,0:T(8,128)(2,1)}) custom-call(bf16[1152,3072]{1,0:T(8,128)(2,1)} %get-tuple-element.52.q_ref.k_ref.v_ref, bf16[1152,3072]{1,0:T(8,128)(2,1)} %get-tuple-element.52.q_ref.k_ref.v_ref, bf16[1152,3072]{1,0:T(8,128)(2,1)} %get-tuple-element.52.q_ref.k_ref.v_ref, ...), custom_call_target="tpu_custom_call" | custom-call | tf_op jit(solution)/shard_map/attend_forward/pallas_call | solution.py:274
  220.4 93.8 %middle.1 = (bf16[1152,1024]{1,0:T(8,128)(2,1)}, f32[1152,1024]{1,0:T(8,128)}, bf16[1152,1024]{1,0:T(8,128)(2,1)}, bf16[8,240,512]{2,1,0:T(8,128)(2,1)}, bf16[8,...) custom-call(s32[32,2]{1,0:T(8,128)} %stack.442.table, ...), custom_call_target="tpu_custom_call" | custom-call | tf_op jit(solution)/shard_map/middle/pallas_call | solution.py:521
  314.8 54.7 %attend_backward.1 = (bf16[1152,1024]{1,0:T(8,128)(2,1)}, bf16[1152,1024]{1,0:T(8,128)(2,1)}, bf16[1152,1024]{1,0:T(8,128)(2,1)}) custom-call(bf16[1152,3072]{1,0:T(8,128)(2,1)} %get-tuple-element.52.q_ref.k_ref.v_ref, bf16[1152,3072]{1,0:T(8,128)(2,1)} %get-tuple-element.52.q_ref.k_ref.v_ref, bf16[1152,3072]{1,0:T(8,128)(2,1)} %get-tuple-element.52.q_ref.k_ref.v_ref, ...), custom_call_target="tpu_custom_call" | custom-call | tf_op jit(solution)/shard_map/attend_backward/pallas_call | solution.py:353
  369.5 14.7 %weight_grad.1 = (bf16[8,64,1536]{2,1,0:T(8,128)(2,1)}, bf16[8,64,1536]{2,1,0:T(8,128)(2,1)}, bf16[8,64,1536]{2,1,0:T(8,128)(2,1)}, bf16[8,64,1536]{2,1,0:T(8,128)(2,1)}) custom-call(s32[32,2]{1,0:T(8,128)} %stack.442.table, bf16[1024,1152]{1,0:T(8,128)(2,1)} %get-tuple-element.63.normed_t_ref, bf16[1152,1024]{1,0:T(8,128)(2,1)} %get-tuple-element.59.q_ref, ...), custom_call_target="tpu_custom_call" | custom-call | tf_op jit(solution)/shard_map/weight_grad/pallas_call | solution.py:575
  385.2 19.6 %input_gradient.1 = (f32[1152,1024]{1,0:T(8,128)}, f32[1,1024]{1,0:T(1,128)}) custom-call(s32[32,2]{1,0:T(8,128)} %stack.442.table, bf16[1152,1024]{1,0:T(8,128)(2,1)} %x_ref.5, f32[16,1024]{1,0:T(8,128)} %get-tuple-element.54.gains_ref, f32[1152,1024]{1,0:T(8,128)} %get-tuple-element.56.grad_hidden_ref, bf16[1152,1024]{1,0:T(8,128)(2,1)} %get-tuple-element.59.q_ref, ...), custom_call_target="tpu_custom_call" | custom-call | tf_op jit(solution)/shard_map/input_gradient/pallas_call | solution.py:621
  405.5 39.9 %psum.7 = f32[2,1024]{1,0:T(2,128)S(1)} all-reduce(f32[2,1024]{1,0:T(2,128)S(1)} %pad_maximum_fusion.15), channel_id=1, replica_groups=mesh['dp'=16,'narrow'=2] {'dp','narrow'}, use_global_device_ids=true, to_apply=%region_0.1 | all-reduce | flops 2048 | bytes 16384 | tf_op jit(solution)/shard_map/psum | solution.py:731
  446.6 2.2 add_convert_fusion.3
  448.9 2.4 collective-permute-start.38
  451.2 1.8 add_convert_fusion.2
  454.6 2.0 collective-permute-start.26
  457.2 2.3 add_convert_fusion
  459.5 8.7 %collective-permute-done.38 = bf16[8,64,1408]{2,1,0:T(8,128)(2,1)S(1)} collective-permute-done((bf16[8,64,1408]{2,1,0:T(8,128)(2,1)S(1)}, bf16[8,64,1408]{2,1,0:T(8,128)(2,1)S(1)}, u32[]{:S(2)}, u32[]{:S(2)}) %collective-permute-start.38) | collective-permute-done | bytes 1441824 | tf_op jit(solution)/shard_map/ppermute | solution.py:118
  468.2 1.4 add_convert_fusion.7
  469.6 2.1 collective-permute-start.32
  471.7 12.0 %collective-permute-done.44 = bf16[8,64,1408]{2,1,0:T(8,128)(2,1)S(1)} collective-permute-done((bf16[8,64,1408]{2,1,0:T(8,128)(2,1)S(1)}, bf16[8,64,1408]{2,1,0:T(8,128)(2,1)S(1)}, u32[]{:S(2)}, u32[]{:S(2)}) %collective-permute-start.44) | collective-permute-done | bytes 1441824 | tf_op jit(solution)/shard_map/ppermute | solution.py:118
  483.7 2.0 collective-permute-start.39
  486.0 29.8 %collective-permute-done.26 = bf16[8,64,1536]{2,1,0:T(8,128)(2,1)S(1)} collective-permute-done((bf16[8,64,1536]{2,1,0:T(8,128)(2,1)S(1)}, bf16[8,64,1536]{2,1,0:T(8,128)(2,1)S(1)}, u32[]{:S(2)}, u32[]{:S(2)}) %collective-permute-start.26) | collective-permute-done | bytes 1572896 | tf_op jit(solution)/shard_map/ppermute | solution.py:118
  516.1 2.4 collective-permute-start.27
  519.8 2.1 collective-permute-start.40
  522.1 14.9 %collective-permute-done.27 = bf16[4,64,1536]{2,1,0:T(8,128)(2,1)S(1)} collective-permute-done((bf16[4,64,1536]{2,1,0:T(8,128)(2,1)S(1)}, bf16[4,64,1536]{2,1,0:T(8,128)(2,1)S(1)}, u32[]{:S(2)}, u32[]{:S(2)}) %collective-permute-start.27) | collective-permute-done | bytes 786464 | tf_op jit(solution)/shard_map/ppermute | solution.py:121
  537.2 2.1 collective-permute-start.28
  539.3 6.1 %collective-permute-done.32 = bf16[8,240,512]{2,1,0:T(8,128)(2,1)S(1)} collective-permute-done((bf16[8,240,512]{2,1,0:T(8,128)(2,1)S(1)}, bf16[8,240,512]{2,1,0:T(8,128)(2,1)S(1)}, u32[]{:S(2)}, u32[]{:S(2)}) %collective-permute-start.32) | collective-permute-done | bytes 1966112 | tf_op jit(solution)/shard_map/ppermute | solution.py:118
  545.9 2.1 collective-permute-start.33
  549.0 2.9 collective-permute-start.41
  552.2 3.7 collective-permute-done.41
  557.0 4.7 collective-permute-done.47
  561.9 1.7 multiply_subtract_fusion
  564.1 2.4 collective-permute-start.34
  566.5 9.4 %collective-permute-done.29 = bf16[1,64,1536]{2,1,0:T(8,128)(2,1)S(1)} collective-permute-done((bf16[1,64,1536]{2,1,0:T(8,128)(2,1)S(1)}, bf16[1,64,1536]{2,1,0:T(8,128)(2,1)S(1)}, u32[]{:S(2)}, u32[]{:S(2)}) %collective-permute-start.29) | collective-permute-done | bytes 196640 | tf_op jit(solution)/shard_map/ppermute | solution.py:121
  576.4 2.2 collective-permute-done.34
  578.6 1.3 add_convert_fusion.12
  580.0 1.5 collective-permute-start.35
  581.4 1.3 multiply_subtract_fusion.1
  582.8 6.9 %collective-permute-done.35 = bf16[1,240,512]{2,1,0:T(8,128)(2,1)S(1)} collective-permute-done((bf16[1,240,512]{2,1,0:T(8,128)(2,1)S(1)}, bf16[1,240,512]{2,1,0:T(8,128)(2,1)S(1)}, u32[]{:S(2)}, u32[]{:S(2)}) %collective-permute-start.35) | collective-permute-done | bytes 245792 | tf_op jit(solution)/shard_map/ppermute | solution.py:121
  589.8 1.4 add_add_fusion
  592.0 1.2 multiply_subtract_fusion.2
  (214 shorter events, 35.1 us)
Async XLA Ops:
  2.8 9.7 %collective-permute-start = (bf16[1,80,1536]{2,1,0:T(8,128)(2,1)S(1)}, bf16[1,80,1536]{2,1,0:T(8,128)(2,1)S(1)}, u32[]{:S(2)}, u32[]{:S(2)}) collective-permute-start(bf16[1,80,1536]{2,1,0:T(8,128)(2,1)S(1)} %fusion.12), channel_id=1, source_target_pairs={{0,16},{1,17},{2,10},{3,11},{4,20},{5,21},{6,14},{7,15},{8,24},{9,... | collective-permute-start | bytes 737288 | tf_op jit(solution)/shard_map/ppermute | solution.py:108
  12.6 18.3 %collective-permute-start.1 = (bf16[2,80,1536]{2,1,0:T(8,128)(2,1)S(1)}, bf16[2,80,1536]{2,1,0:T(8,128)(2,1)S(1)}, u32[]{:S(2)}, u32[]{:S(2)}) collective-permute-start(bf16[2,80,1536]{2,1,0:T(8,128)(2,1)S(1)} %pad_maximum_fusion.9), channel_id=1, source_target_pairs={{0,8},{1,9},{2,18},{3,19},{4,12},{5,13},{6,22},{7,23},{8,0},{9,1},... | collective-permute-start | bytes 1474568 | tf_op jit(solution)/shard_map/ppermute | solution.py:108
  15.1 37.6 %copy-start.8 = (bf16[1,64,1408]{2,1,0:T(8,128)(2,1)}, bf16[1,64,1408]{2,1,0:T(8,128)(2,1)S(1)}, u32[]{:S(2)}) copy-start(bf16[1,64,1408]{2,1,0:T(8,128)(2,1)S(1)} %get-tuple-element.169) | copy-start | bytes 540676
  15.1 53.3 %copy-start.6 = (bf16[1,64,1408]{2,1,0:T(8,128)(2,1)}, bf16[1,64,1408]{2,1,0:T(8,128)(2,1)S(1)}, u32[]{:S(2)}) copy-start(bf16[1,64,1408]{2,1,0:T(8,128)(2,1)S(1)} %get-tuple-element.168) | copy-start | bytes 540676
  15.1 17.9 %collective-permute-start.12 = (bf16[1,64,1408]{2,1,0:T(8,128)(2,1)S(1)}, bf16[1,64,1408]{2,1,0:T(8,128)(2,1)S(1)}, u32[]{:S(2)}, u32[]{:S(2)}) collective-permute-start(bf16[1,64,1408]{2,1,0:T(8,128)(2,1)S(1)} %get-tuple-element.169), channel_id=1, source_target_pairs={{0,16},{1,17},{2,10},{3,11},{4,20},{5,21},{6,14},{7,15},{8,24},{9,... | collective-permute-start | bytes 540680 | tf_op jit(solution)/shard_map/ppermute | solution.py:108
  30.9 23.4 %collective-permute-start.2 = (bf16[4,80,1536]{2,1,0:T(8,128)(2,1)S(1)}, bf16[4,80,1536]{2,1,0:T(8,128)(2,1)S(1)}, u32[]{:S(2)}, u32[]{:S(2)}) collective-permute-start(bf16[4,80,1536]{2,1,0:T(8,128)(2,1)S(1)} %pad_maximum_fusion.4), channel_id=1, source_target_pairs={{0,4},{1,5},{2,3},{3,2},{4,0},{5,1},{6,7},{7,6},{8,12},{9,13},{10,... | collective-permute-start | bytes 2949128 | tf_op jit(solution)/shard_map/ppermute | solution.py:108
  32.9 32.9 %copy-start.2 = (bf16[1,240,512]{2,1,0:T(8,128)(2,1)}, bf16[1,240,512]{2,1,0:T(8,128)(2,1)S(1)}, u32[]{:S(2)}) copy-start(bf16[1,240,512]{2,1,0:T(8,128)(2,1)S(1)} %maximum_bitcast_fusion) | copy-start | bytes 737284
  32.9 19.6 %collective-permute-start.6 = (bf16[1,240,512]{2,1,0:T(8,128)(2,1)S(1)}, bf16[1,240,512]{2,1,0:T(8,128)(2,1)S(1)}, u32[]{:S(2)}, u32[]{:S(2)}) collective-permute-start(bf16[1,240,512]{2,1,0:T(8,128)(2,1)S(1)} %maximum_bitcast_fusion), channel_id=1, source_target_pairs={{0,16},{1,17},{2,10},{3,11},{4,20},{5,21},{6,14},{7,15},{8,24},{9,... | collective-permute-start | bytes 737288 | tf_op jit(solution)/shard_map/ppermute | solution.py:108
  33.0 19.8 %copy-start.19 = (bf16[1,64,1408]{2,1,0:T(8,128)(2,1)}, bf16[1,64,1408]{2,1,0:T(8,128)(2,1)S(1)}, u32[]{:S(2)}) copy-start(bf16[1,64,1408]{2,1,0:T(8,128)(2,1)S(1)} %collective-permute-done.12) | copy-start | bytes 540676
  33.1 19.6 %collective-permute-start.13 = (bf16[2,64,1408]{2,1,0:T(8,128)(2,1)S(1)}, bf16[2,64,1408]{2,1,0:T(8,128)(2,1)S(1)}, u32[]{:S(2)}, u32[]{:S(2)}) collective-permute-start(bf16[2,64,1408]{2,1,0:T(8,128)(2,1)S(1)} %pad_maximum_fusion.11), channel_id=1, source_target_pairs={{0,8},{1,9},{2,18},{3,19},{4,12},{5,13},{6,22},{7,23},{8,0},{9,1},... | collective-permute-start | bytes 1081352 | tf_op jit(solution)/shard_map/ppermute | solution.py:108
  52.6 13.2 %collective-permute-start.7 = (bf16[2,240,512]{2,1,0:T(8,128)(2,1)S(1)}, bf16[2,240,512]{2,1,0:T(8,128)(2,1)S(1)}, u32[]{:S(2)}, u32[]{:S(2)}) collective-permute-start(bf16[2,240,512]{2,1,0:T(8,128)(2,1)S(1)} %pad_maximum_fusion.10), channel_id=1, source_target_pairs={{0,8},{1,9},{2,18},{3,19},{4,12},{5,13},{6,22},{7,23},{8,0},{9,1},... | collective-permute-start | bytes 1474568 | tf_op jit(solution)/shard_map/ppermute | solution.py:108
  52.8 19.2 %collective-permute-start.14 = (bf16[4,64,1408]{2,1,0:T(8,128)(2,1)S(1)}, bf16[4,64,1408]{2,1,0:T(8,128)(2,1)}, u32[]{:S(2)}, u32[]{:S(2)}) collective-permute-start(bf16[4,64,1408]{2,1,0:T(8,128)(2,1)S(1)} %pad_maximum_fusion.6), channel_id=1, source_target_pairs={{0,4},{1,5},{2,3},{3,2},{4,0},{5,1},{6,7},{7,6},{8,12},{9,13},{10,... | collective-permute-start | bytes 2162696 | tf_op jit(solution)/shard_map/ppermute | solution.py:108
  54.6 54.0 %copy-start = (bf16[8,80,1536]{2,1,0:T(8,128)(2,1)}, bf16[8,80,1536]{2,1,0:T(8,128)(2,1)S(1)}, u32[]{:S(2)}) copy-start(bf16[8,80,1536]{2,1,0:T(8,128)(2,1)S(1)} %pad_maximum_fusion.refs_0_) | copy-start | bytes 5898244
  54.6 54.0 %collective-permute-start.3 = (bf16[8,80,1536]{2,1,0:T(8,128)(2,1)S(1)}, bf16[8,80,1536]{2,1,0:T(8,128)(2,1)}, u32[]{:S(2)}, u32[]{:S(2)}) collective-permute-start(bf16[8,80,1536]{2,1,0:T(8,128)(2,1)S(1)} %pad_maximum_fusion.refs_0_), channel_id=1, source_target_pairs={{0,1},{1,0},{2,6},{3,7},{4,5},{5,4},{6,2},{7,3},{8,9},{9,8},{10,14... | collective-permute-start | bytes 5898248 | tf_op jit(solution)/shard_map/ppermute | solution.py:109
  55.0 13.5 %collective-permute-start.18 = (bf16[1,64,1408]{2,1,0:T(8,128)(2,1)S(1)}, bf16[1,64,1408]{2,1,0:T(8,128)(2,1)S(1)}, u32[]{:S(2)}, u32[]{:S(2)}) collective-permute-start(bf16[1,64,1408]{2,1,0:T(8,128)(2,1)S(1)} %get-tuple-element.168), channel_id=1, source_target_pairs={{0,16},{1,17},{2,10},{3,11},{4,20},{5,21},{6,14},{7,15},{8,24},{9,... | collective-permute-start | bytes 540680 | tf_op jit(solution)/shard_map/ppermute | solution.py:108
  66.9 26.2 %collective-permute-start.8 = (bf16[4,240,512]{2,1,0:T(8,128)(2,1)}, bf16[4,240,512]{2,1,0:T(8,128)(2,1)}, u32[]{:S(2)}, u32[]{:S(2)}) collective-permute-start(bf16[4,240,512]{2,1,0:T(8,128)(2,1)} %pad_maximum_fusion.5), channel_id=1, source_target_pairs={{0,4},{1,5},{2,3},{3,2},{4,0},{5,1},{6,7},{7,6},{8,12},{9,13},{10,... | collective-permute-start | bytes 2949128 | tf_op jit(solution)/shard_map/ppermute | solution.py:108
  69.2 9.5 %collective-permute-start.19 = (bf16[2,64,1408]{2,1,0:T(8,128)(2,1)}, bf16[2,64,1408]{2,1,0:T(8,128)(2,1)}, u32[]{:S(2)}, u32[]{:S(2)}) collective-permute-start(bf16[2,64,1408]{2,1,0:T(8,128)(2,1)} %pad_maximum_fusion.12), channel_id=1, source_target_pairs={{0,8},{1,9},{2,18},{3,19},{4,12},{5,13},{6,22},{7,23},{8,0},{9,1},... | collective-permute-start | bytes 1081352 | tf_op jit(solution)/shard_map/ppermute | solution.py:108
  69.3 23.8 %copy-start.3 = (bf16[1,240,512]{2,1,0:T(8,128)(2,1)S(1)}, bf16[1,240,512]{2,1,0:T(8,128)(2,1)}, u32[]{:S(2)}) copy-start(bf16[1,240,512]{2,1,0:T(8,128)(2,1)} %copy-done.2) | copy-start | bytes 737284
  69.3 23.8 %copy-start.10 = (bf16[1,240,512]{2,1,0:T(8,128)(2,1)S(1)}, bf16[1,240,512]{2,1,0:T(8,128)(2,1)}, u32[]{:S(2)}) copy-start(bf16[1,240,512]{2,1,0:T(8,128)(2,1)} %copy-done.9) | copy-start | bytes 737284
  69.3 23.8 %copy-start.16 = (bf16[2,240,512]{2,1,0:T(8,128)(2,1)S(1)}, bf16[2,240,512]{2,1,0:T(8,128)(2,1)}, u32[]{:S(2)}) copy-start(bf16[2,240,512]{2,1,0:T(8,128)(2,1)} %copy-done.15) | copy-start | bytes 1474564
  73.6 26.6 %copy-start.1 = (bf16[8,64,1408]{2,1,0:T(8,128)(2,1)}, bf16[8,64,1408]{2,1,0:T(8,128)(2,1)S(1)}, u32[]{:S(2)}) copy-start(bf16[8,64,1408]{2,1,0:T(8,128)(2,1)S(1)} %pad_maximum_fusion.2.refs_4_) | copy-start | bytes 4325380
  73.6 40.6 %collective-permute-start.16 = (bf16[8,64,1408]{2,1,0:T(8,128)(2,1)S(1)}, bf16[8,64,1408]{2,1,0:T(8,128)(2,1)}, u32[]{:S(2)}, u32[]{:S(2)}) collective-permute-start(bf16[8,64,1408]{2,1,0:T(8,128)(2,1)S(1)} %pad_maximum_fusion.2.refs_4_), channel_id=1, source_target_pairs={{0,2},{1,3},{2,0},{3,1},{4,6},{5,7},{6,4},{7,5},{8,10},{9,11},{10,... | collective-permute-start | bytes 4325384 | tf_op jit(solution)/shard_map/ppermute | solution.py:110
  80.7 18.8 %copy-start.43 = (s32[1,3]{1,0:T(1,128)S(1)}, s32[1,3]{1,0:T(1,128)}, u32[]{:S(2)}) copy-start(s32[1,3]{1,0:T(1,128)} %param.22) | copy-start | bytes 40
  80.7 27.9 %collective-permute-start.20 = (bf16[4,64,1408]{2,1,0:T(8,128)(2,1)}, bf16[4,64,1408]{2,1,0:T(8,128)(2,1)}, u32[]{:S(2)}, u32[]{:S(2)}) collective-permute-start(bf16[4,64,1408]{2,1,0:T(8,128)(2,1)} %pad_maximum_fusion.7), channel_id=1, source_target_pairs={{0,4},{1,5},{2,3},{3,2},{4,0},{5,1},{6,7},{7,6},{8,12},{9,13},{10,... | collective-permute-start | bytes 2162696 | tf_op jit(solution)/shard_map/ppermute | solution.py:108
  95.9 40.6 %collective-permute-start.9 = (bf16[8,240,512]{2,1,0:T(8,128)(2,1)}, bf16[8,240,512]{2,1,0:T(8,128)(2,1)}, u32[]{:S(2)}, u32[]{:S(2)}) collective-permute-start(bf16[8,240,512]{2,1,0:T(8,128)(2,1)} %pad_maximum_fusion.1.refs_0_), channel_id=1, source_target_pairs={{0,1},{1,0},{2,6},{3,7},{4,5},{5,4},{6,2},{7,3},{8,9},{9,8},{10,14... | collective-permute-start | bytes 5898248 | tf_op jit(solution)/shard_map/ppermute | solution.py:109
  100.1 36.1 %collective-permute-start.15 = (bf16[8,64,1408]{2,1,0:T(8,128)(2,1)S(1)}, bf16[8,64,1408]{2,1,0:T(8,128)(2,1)}, u32[]{:S(2)}, u32[]{:S(2)}) collective-permute-start(bf16[8,64,1408]{2,1,0:T(8,128)(2,1)S(1)} %pad_maximum_fusion.2.refs_4_), channel_id=1, source_target_pairs={{0,1},{1,0},{2,6},{3,7},{4,5},{5,4},{6,2},{7,3},{8,9},{9,8},{10,14... | collective-permute-start | bytes 4325384 | tf_op jit(solution)/shard_map/ppermute | solution.py:109
  108.6 43.2 %collective-permute-start.4 = (bf16[8,80,1536]{2,1,0:T(8,128)(2,1)S(1)}, bf16[8,80,1536]{2,1,0:T(8,128)(2,1)}, u32[]{:S(2)}, u32[]{:S(2)}) collective-permute-start(bf16[8,80,1536]{2,1,0:T(8,128)(2,1)S(1)} %pad_maximum_fusion.refs_0_), channel_id=1, source_target_pairs={{0,2},{1,3},{2,0},{3,1},{4,6},{5,7},{6,4},{7,5},{8,10},{9,11},{10,... | collective-permute-start | bytes 5898248 | tf_op jit(solution)/shard_map/ppermute | solution.py:110
  108.6 43.6 %collective-permute-start.5 = (bf16[8,80,1536]{2,1,0:T(8,128)(2,1)}, bf16[8,80,1536]{2,1,0:T(8,128)(2,1)}, u32[]{:S(2)}, u32[]{:S(2)}) collective-permute-start(bf16[8,80,1536]{2,1,0:T(8,128)(2,1)} %collective-permute-done.3.refs_1_), channel_id=1, source_target_pairs={{0,2},{1,3},{2,0},{3,1},{4,6},{5,7},{6,4},{7,5},{8,10},{9,11},{10,... | collective-permute-start | bytes 5898248 | tf_op jit(solution)/shard_map/ppermute | solution.py:110
  114.2 37.5 %collective-permute-start.21 = (bf16[8,64,1408]{2,1,0:T(8,128)(2,1)}, bf16[8,64,1408]{2,1,0:T(8,128)(2,1)}, u32[]{:S(2)}, u32[]{:S(2)}) collective-permute-start(bf16[8,64,1408]{2,1,0:T(8,128)(2,1)} %pad_maximum_fusion.3.refs_8_), channel_id=1, source_target_pairs={{0,1},{1,0},{2,6},{3,7},{4,5},{5,4},{6,2},{7,3},{8,9},{9,8},{10,14... | collective-permute-start | bytes 4325384 | tf_op jit(solution)/shard_map/ppermute | solution.py:109
  122.3 29.5 %copy-start.42 = (s32[1152]{0:T(1024)}, s32[1152]{0:T(1024)S(1)}, u32[]{:S(2)}) copy-start(s32[1152]{0:T(1024)S(1)} %select_add_fusion) | copy-start | bytes 13828
  136.3 82.5 %collective-permute-start.10 = (bf16[8,240,512]{2,1,0:T(8,128)(2,1)}, bf16[8,240,512]{2,1,0:T(8,128)(2,1)}, u32[]{:S(2)}, u32[]{:S(2)}) collective-permute-start(bf16[8,240,512]{2,1,0:T(8,128)(2,1)} %pad_maximum_fusion.1.refs_0_), channel_id=1, source_target_pairs={{0,2},{1,3},{2,0},{3,1},{4,6},{5,7},{6,4},{7,5},{8,10},{9,11},{10,... | collective-permute-start | bytes 5898248 | tf_op jit(solution)/shard_map/ppermute | solution.py:110
  136.5 82.3 %collective-permute-start.11 = (bf16[8,240,512]{2,1,0:T(8,128)(2,1)}, bf16[8,240,512]{2,1,0:T(8,128)(2,1)}, u32[]{:S(2)}, u32[]{:S(2)}) collective-permute-start(bf16[8,240,512]{2,1,0:T(8,128)(2,1)} %collective-permute-done.9.refs_1_), channel_id=1, source_target_pairs={{0,2},{1,3},{2,0},{3,1},{4,6},{5,7},{6,4},{7,5},{8,10},{9,11},{10,... | collective-permute-start | bytes 5898248 | tf_op jit(solution)/shard_map/ppermute | solution.py:110
  151.7 67.1 %collective-permute-start.22 = (bf16[8,64,1408]{2,1,0:T(8,128)(2,1)}, bf16[8,64,1408]{2,1,0:T(8,128)(2,1)S(1)}, u32[]{:S(2)}, u32[]{:S(2)}) collective-permute-start(bf16[8,64,1408]{2,1,0:T(8,128)(2,1)} %pad_maximum_fusion.3.refs_8_), channel_id=1, source_target_pairs={{0,2},{1,3},{2,0},{3,1},{4,6},{5,7},{6,4},{7,5},{8,10},{9,11},{10,... | collective-permute-start | bytes 4325384 | tf_op jit(solution)/shard_map/ppermute | solution.py:110
  151.8 67.0 %collective-permute-start.17 = (bf16[8,64,1408]{2,1,0:T(8,128)(2,1)}, bf16[8,64,1408]{2,1,0:T(8,128)(2,1)S(1)}, u32[]{:S(2)}, u32[]{:S(2)}) collective-permute-start(bf16[8,64,1408]{2,1,0:T(8,128)(2,1)} %collective-permute-done.15.refs_5_), channel_id=1, source_target_pairs={{0,2},{1,3},{2,0},{3,1},{4,6},{5,7},{6,4},{7,5},{8,10},{9,11},{10,... | collective-permute-start | bytes 4325384 | tf_op jit(solution)/shard_map/ppermute | solution.py:110
  152.2 66.6 %collective-permute-start.23 = (bf16[8,64,1408]{2,1,0:T(8,128)(2,1)}, bf16[8,64,1408]{2,1,0:T(8,128)(2,1)}, u32[]{:S(2)}, u32[]{:S(2)}) collective-permute-start(bf16[8,64,1408]{2,1,0:T(8,128)(2,1)} %collective-permute-done.21.refs_9_), channel_id=1, source_target_pairs={{0,2},{1,3},{2,0},{3,1},{4,6},{5,7},{6,4},{7,5},{8,10},{9,11},{10,... | collective-permute-start | bytes 4325384 | tf_op jit(solution)/shard_map/ppermute | solution.py:110
  314.2 131.2 %collective-permute-start.37 = (bf16[8,64,1408]{2,1,0:T(8,128)(2,1)}, bf16[8,64,1408]{2,1,0:T(8,128)(2,1)S(1)}, u32[]{:S(2)}, u32[]{:S(2)}) collective-permute-start(bf16[8,64,1408]{2,1,0:T(8,128)(2,1)} %get-tuple-element.75), channel_id=1, source_target_pairs={{0,2},{1,3},{2,0},{3,1},{4,6},{5,7},{6,4},{7,5},{8,10},{9,11},{10,... | collective-permute-start | bytes 4325384 | tf_op jit(solution)/shard_map/ppermute | solution.py:115
  314.7 134.2 %collective-permute-start.43 = (bf16[8,64,1408]{2,1,0:T(8,128)(2,1)}, bf16[8,64,1408]{2,1,0:T(8,128)(2,1)}, u32[]{:S(2)}, u32[]{:S(2)}) collective-permute-start(bf16[8,64,1408]{2,1,0:T(8,128)(2,1)} %get-tuple-element.79), channel_id=1, source_target_pairs={{0,2},{1,3},{2,0},{3,1},{4,6},{5,7},{6,4},{7,5},{8,10},{9,11},{10,... | collective-permute-start | bytes 4325384 | tf_op jit(solution)/shard_map/ppermute | solution.py:115
  384.2 68.8 %collective-permute-start.25 = (bf16[8,64,1536]{2,1,0:T(8,128)(2,1)}, bf16[8,64,1536]{2,1,0:T(8,128)(2,1)S(1)}, u32[]{:S(2)}, u32[]{:S(2)}) collective-permute-start(bf16[8,64,1536]{2,1,0:T(8,128)(2,1)} %get-tuple-element.67), channel_id=1, source_target_pairs={{0,2},{1,3},{2,0},{3,1},{4,6},{5,7},{6,4},{7,5},{8,10},{9,11},{10,... | collective-permute-start | bytes 4718600 | tf_op jit(solution)/shard_map/ppermute | solution.py:115
  384.7 69.9 %collective-permute-start.31 = (bf16[8,240,512]{2,1,0:T(8,128)(2,1)}, bf16[8,240,512]{2,1,0:T(8,128)(2,1)}, u32[]{:S(2)}, u32[]{:S(2)}) collective-permute-start(bf16[8,240,512]{2,1,0:T(8,128)(2,1)} %get-tuple-element.71), channel_id=1, source_target_pairs={{0,2},{1,3},{2,0},{3,1},{4,6},{5,7},{6,4},{7,5},{8,10},{9,11},{10,... | collective-permute-start | bytes 5898248 | tf_op jit(solution)/shard_map/ppermute | solution.py:115
  384.8 68.8 %collective-permute-start.36 = (bf16[8,64,1408]{2,1,0:T(8,128)(2,1)}, bf16[8,64,1408]{2,1,0:T(8,128)(2,1)}, u32[]{:S(2)}, u32[]{:S(2)}) collective-permute-start(bf16[8,64,1408]{2,1,0:T(8,128)(2,1)} %get-tuple-element.73), channel_id=1, source_target_pairs={{0,2},{1,3},{2,0},{3,1},{4,6},{5,7},{6,4},{7,5},{8,10},{9,11},{10,... | collective-permute-start | bytes 4325384 | tf_op jit(solution)/shard_map/ppermute | solution.py:116
  385.2 19.6 %copy-start.44 = (f32[1,1024]{1,0:T(1,128)S(1)}, f32[1,1024]{1,0:T(1,128)}, u32[]{:S(2)}) copy-start(f32[1,1024]{1,0:T(1,128)} %get-tuple-element.81) | copy-start | bytes 12292
  445.4 24.2 %collective-permute-start.42 = (bf16[8,64,1408]{2,1,0:T(8,128)(2,1)}, bf16[8,64,1408]{2,1,0:T(8,128)(2,1)S(1)}, u32[]{:S(2)}, u32[]{:S(2)}) collective-permute-start(bf16[8,64,1408]{2,1,0:T(8,128)(2,1)} %get-tuple-element.77), channel_id=1, source_target_pairs={{0,2},{1,3},{2,0},{3,1},{4,6},{5,7},{6,4},{7,5},{8,10},{9,11},{10,... | collective-permute-start | bytes 4325384 | tf_op jit(solution)/shard_map/ppermute | solution.py:116
  448.9 19.4 %collective-permute-start.38 = (bf16[8,64,1408]{2,1,0:T(8,128)(2,1)S(1)}, bf16[8,64,1408]{2,1,0:T(8,128)(2,1)S(1)}, u32[]{:S(2)}, u32[]{:S(2)}) collective-permute-start(bf16[8,64,1408]{2,1,0:T(8,128)(2,1)S(1)} %add_convert_fusion.3), channel_id=1, source_target_pairs={{0,1},{1,0},{2,6},{3,7},{4,5},{5,4},{6,2},{7,3},{8,9},{9,8},{10,14... | collective-permute-start | bytes 4325384 | tf_op jit(solution)/shard_map/ppermute | solution.py:118
  453.1 30.6 %collective-permute-start.44 = (bf16[8,64,1408]{2,1,0:T(8,128)(2,1)S(1)}, bf16[8,64,1408]{2,1,0:T(8,128)(2,1)S(1)}, u32[]{:S(2)}, u32[]{:S(2)}) collective-permute-start(bf16[8,64,1408]{2,1,0:T(8,128)(2,1)S(1)} %add_convert_fusion.2), channel_id=1, source_target_pairs={{0,1},{1,0},{2,6},{3,7},{4,5},{5,4},{6,2},{7,3},{8,9},{9,8},{10,14... | collective-permute-start | bytes 4325384 | tf_op jit(solution)/shard_map/ppermute | solution.py:118
  454.6 31.4 %collective-permute-start.24 = (bf16[8,64,1536]{2,1,0:T(8,128)(2,1)S(1)}, bf16[8,64,1536]{2,1,0:T(8,128)(2,1)S(1)}, u32[]{:S(2)}, u32[]{:S(2)}) collective-permute-start(bf16[8,64,1536]{2,1,0:T(8,128)(2,1)S(1)} %copy-done.49), channel_id=1, source_target_pairs={{0,2},{1,3},{2,0},{3,1},{4,6},{5,7},{6,4},{7,5},{8,10},{9,11},{10,... | collective-permute-start | bytes 4718600 | tf_op jit(solution)/shard_map/ppermute | solution.py:116
  454.6 61.3 %collective-permute-start.26 = (bf16[8,64,1536]{2,1,0:T(8,128)(2,1)S(1)}, bf16[8,64,1536]{2,1,0:T(8,128)(2,1)S(1)}, u32[]{:S(2)}, u32[]{:S(2)}) collective-permute-start(bf16[8,64,1536]{2,1,0:T(8,128)(2,1)S(1)} %add_convert_fusion.1), channel_id=1, source_target_pairs={{0,1},{1,0},{2,6},{3,7},{4,5},{5,4},{6,2},{7,3},{8,9},{9,8},{10,14... | collective-permute-start | bytes 4718600 | tf_op jit(solution)/shard_map/ppermute | solution.py:118
  459.5 26.2 %copy-start.25 = (bf16[8,64,1408]{2,1,0:T(8,128)(2,1)S(1)}, bf16[8,64,1408]{2,1,0:T(8,128)(2,1)}, u32[]{:S(2)}) copy-start(bf16[8,64,1408]{2,1,0:T(8,128)(2,1)} %get-tuple-element.76) | copy-start | bytes 4325380
  468.2 71.1 %collective-permute-start.30 = (bf16[8,240,512]{2,1,0:T(8,128)(2,1)S(1)}, bf16[8,240,512]{2,1,0:T(8,128)(2,1)S(1)}, u32[]{:S(2)}, u32[]{:S(2)}) collective-permute-start(bf16[8,240,512]{2,1,0:T(8,128)(2,1)S(1)} %copy-done.48), channel_id=1, source_target_pairs={{0,2},{1,3},{2,0},{3,1},{4,6},{5,7},{6,4},{7,5},{8,10},{9,11},{10,... | collective-permute-start | bytes 5898248 | tf_op jit(solution)/shard_map/ppermute | solution.py:116
  469.6 46.2 %copy-start.21 = (bf16[8,64,1536]{2,1,0:T(8,128)(2,1)S(1)}, bf16[8,64,1536]{2,1,0:T(8,128)(2,1)}, u32[]{:S(2)}) copy-start(bf16[8,64,1536]{2,1,0:T(8,128)(2,1)} %get-tuple-element.64) | copy-start | bytes 4718596
  469.6 75.8 %collective-permute-start.32 = (bf16[8,240,512]{2,1,0:T(8,128)(2,1)S(1)}, bf16[8,240,512]{2,1,0:T(8,128)(2,1)S(1)}, u32[]{:S(2)}, u32[]{:S(2)}) collective-permute-start(bf16[8,240,512]{2,1,0:T(8,128)(2,1)S(1)} %add_convert_fusion), channel_id=1, source_target_pairs={{0,1},{1,0},{2,6},{3,7},{4,5},{5,4},{6,2},{7,3},{8,9},{9,8},{10,14... | collective-permute-start | bytes 5898248 | tf_op jit(solution)/shard_map/ppermute | solution.py:118
  483.7 34.9 %collective-permute-start.39 = (bf16[4,64,1408]{2,1,0:T(8,128)(2,1)S(1)}, bf16[4,64,1408]{2,1,0:T(8,128)(2,1)S(1)}, u32[]{:S(2)}, u32[]{:S(2)}) collective-permute-start(bf16[4,64,1408]{2,1,0:T(8,128)(2,1)S(1)} %add_convert_fusion.7), channel_id=1, source_target_pairs={{0,4},{1,5},{2,3},{3,2},{4,0},{5,1},{6,7},{7,6},{8,12},{9,13},{10,... | collective-permute-start | bytes 2162696 | tf_op jit(solution)/shard_map/ppermute | solution.py:121
  485.9 35.9 %collective-permute-start.45 = (bf16[4,64,1408]{2,1,0:T(8,128)(2,1)S(1)}, bf16[4,64,1408]{2,1,0:T(8,128)(2,1)S(1)}, u32[]{:S(2)}, u32[]{:S(2)}) collective-permute-start(bf16[4,64,1408]{2,1,0:T(8,128)(2,1)S(1)} %add_convert_fusion.6), channel_id=1, source_target_pairs={{0,4},{1,5},{2,3},{3,2},{4,0},{5,1},{6,7},{7,6},{8,12},{9,13},{10,... | collective-permute-start | bytes 2162696 | tf_op jit(solution)/shard_map/ppermute | solution.py:121
  516.1 20.9 %collective-permute-start.27 = (bf16[4,64,1536]{2,1,0:T(8,128)(2,1)S(1)}, bf16[4,64,1536]{2,1,0:T(8,128)(2,1)S(1)}, u32[]{:S(2)}, u32[]{:S(2)}) collective-permute-start(bf16[4,64,1536]{2,1,0:T(8,128)(2,1)S(1)} %add_convert_fusion.5), channel_id=1, source_target_pairs={{0,4},{1,5},{2,3},{3,2},{4,0},{5,1},{6,7},{7,6},{8,12},{9,13},{10,... | collective-permute-start | bytes 2359304 | tf_op jit(solution)/shard_map/ppermute | solution.py:121
  519.8 25.7 %copy-start.11 = (bf16[8,240,512]{2,1,0:T(8,128)(2,1)S(1)}, bf16[8,240,512]{2,1,0:T(8,128)(2,1)}, u32[]{:S(2)}) copy-start(bf16[8,240,512]{2,1,0:T(8,128)(2,1)} %get-tuple-element.68) | copy-start | bytes 5898244
  519.8 28.2 %collective-permute-start.40 = (bf16[2,64,1408]{2,1,0:T(8,128)(2,1)S(1)}, bf16[2,64,1408]{2,1,0:T(8,128)(2,1)S(1)}, u32[]{:S(2)}, u32[]{:S(2)}) collective-permute-start(bf16[2,64,1408]{2,1,0:T(8,128)(2,1)S(1)} %add_convert_fusion.11), channel_id=1, source_target_pairs={{0,8},{1,9},{2,18},{3,19},{4,12},{5,13},{6,22},{7,23},{8,0},{9,1},... | collective-permute-start | bytes 1081352 | tf_op jit(solution)/shard_map/ppermute | solution.py:121
  522.1 29.8 %collective-permute-start.46 = (bf16[2,64,1408]{2,1,0:T(8,128)(2,1)S(1)}, bf16[2,64,1408]{2,1,0:T(8,128)(2,1)S(1)}, u32[]{:S(2)}, u32[]{:S(2)}) collective-permute-start(bf16[2,64,1408]{2,1,0:T(8,128)(2,1)S(1)} %add_convert_fusion.10), channel_id=1, source_target_pairs={{0,8},{1,9},{2,18},{3,19},{4,12},{5,13},{6,22},{7,23},{8,0},{9,1},... | collective-permute-start | bytes 1081352 | tf_op jit(solution)/shard_map/ppermute | solution.py:121
  537.2 26.4 %collective-permute-start.28 = (bf16[2,64,1536]{2,1,0:T(8,128)(2,1)S(1)}, bf16[2,64,1536]{2,1,0:T(8,128)(2,1)S(1)}, u32[]{:S(2)}, u32[]{:S(2)}) collective-permute-start(bf16[2,64,1536]{2,1,0:T(8,128)(2,1)S(1)} %add_convert_fusion.9), channel_id=1, source_target_pairs={{0,8},{1,9},{2,18},{3,19},{4,12},{5,13},{6,22},{7,23},{8,0},{9,1},... | collective-permute-start | bytes 1179656 | tf_op jit(solution)/shard_map/ppermute | solution.py:121
  539.3 24.5 %copy-start.12 = (bf16[8,240,512]{2,1,0:T(8,128)(2,1)}, bf16[8,240,512]{2,1,0:T(8,128)(2,1)S(1)}, u32[]{:S(2)}) copy-start(bf16[8,240,512]{2,1,0:T(8,128)(2,1)S(1)} %collective-permute-done.30) | copy-start | bytes 5898244
  545.9 17.9 %collective-permute-start.33 = (bf16[4,240,512]{2,1,0:T(8,128)(2,1)S(1)}, bf16[4,240,512]{2,1,0:T(8,128)(2,1)S(1)}, u32[]{:S(2)}, u32[]{:S(2)}) collective-permute-start(bf16[4,240,512]{2,1,0:T(8,128)(2,1)S(1)} %add_convert_fusion.4), channel_id=1, source_target_pairs={{0,4},{1,5},{2,3},{3,2},{4,0},{5,1},{6,7},{7,6},{8,12},{9,13},{10,... | collective-permute-start | bytes 2949128 | tf_op jit(solution)/shard_map/ppermute | solution.py:121
  549.0 6.9 %collective-permute-start.41 = (bf16[1,64,1408]{2,1,0:T(8,128)(2,1)S(1)}, bf16[1,64,1408]{2,1,0:T(8,128)(2,1)S(1)}, u32[]{:S(2)}, u32[]{:S(2)}) collective-permute-start(bf16[1,64,1408]{2,1,0:T(8,128)(2,1)S(1)} %add_convert_fusion.15), channel_id=1, source_target_pairs={{0,16},{1,17},{2,10},{3,11},{4,20},{5,21},{6,14},{7,15},{8,24},{9,... | collective-permute-start | bytes 540680 | tf_op jit(solution)/shard_map/ppermute | solution.py:121
  552.1 9.6 %collective-permute-start.47 = (bf16[1,64,1408]{2,1,0:T(8,128)(2,1)S(1)}, bf16[1,64,1408]{2,1,0:T(8,128)(2,1)S(1)}, u32[]{:S(2)}, u32[]{:S(2)}) collective-permute-start(bf16[1,64,1408]{2,1,0:T(8,128)(2,1)S(1)} %add_convert_fusion.14), channel_id=1, source_target_pairs={{0,16},{1,17},{2,10},{3,11},{4,20},{5,21},{6,14},{7,15},{8,24},{9,... | collective-permute-start | bytes 540680 | tf_op jit(solution)/shard_map/ppermute | solution.py:121
  563.7 12.2 %collective-permute-start.29 = (bf16[1,64,1536]{2,1,0:T(8,128)(2,1)S(1)}, bf16[1,64,1536]{2,1,0:T(8,128)(2,1)S(1)}, u32[]{:S(2)}, u32[]{:S(2)}) collective-permute-start(bf16[1,64,1536]{2,1,0:T(8,128)(2,1)S(1)} %add_convert_fusion.13), channel_id=1, source_target_pairs={{0,16},{1,17},{2,10},{3,11},{4,20},{5,21},{6,14},{7,15},{8,24},{9,... | collective-permute-start | bytes 589832 | tf_op jit(solution)/shard_map/ppermute | solution.py:121
  564.1 14.5 %collective-permute-start.34 = (bf16[2,240,512]{2,1,0:T(8,128)(2,1)S(1)}, bf16[2,240,512]{2,1,0:T(8,128)(2,1)S(1)}, u32[]{:S(2)}, u32[]{:S(2)}) collective-permute-start(bf16[2,240,512]{2,1,0:T(8,128)(2,1)S(1)} %add_convert_fusion.8), channel_id=1, source_target_pairs={{0,8},{1,9},{2,18},{3,19},{4,12},{5,13},{6,22},{7,23},{8,0},{9,1},... | collective-permute-start | bytes 1474568 | tf_op jit(solution)/shard_map/ppermute | solution.py:121
  580.0 9.8 %collective-permute-start.35 = (bf16[1,240,512]{2,1,0:T(8,128)(2,1)S(1)}, bf16[1,240,512]{2,1,0:T(8,128)(2,1)S(1)}, u32[]{:S(2)}, u32[]{:S(2)}) collective-permute-start(bf16[1,240,512]{2,1,0:T(8,128)(2,1)S(1)} %add_convert_fusion.12), channel_id=1, source_target_pairs={{0,16},{1,17},{2,10},{3,11},{4,20},{5,21},{6,14},{7,15},{8,24},{9,... | collective-permute-start | bytes 737288 | tf_op jit(solution)/shard_map/ppermute | solution.py:121
  (34 other events, 251.8 us)

commit v2 on v1

v2 whole, which is shorter than its diff:
```python
import functools

import jax
import jax.numpy as jnp
from jax import lax
from jax.experimental import pallas as pl
from jax.experimental.pallas import tpu as pltpu
from jax.sharding import PartitionSpec as P

HEADS = 16
DK = 64
SHORT_PATCH = 256
STEP = 10
HD = 1024
SLOT = 384
LONG = 1152
LONG_PATCH = 1024

norm_eps = 1e-06
score_scale = 0.125
beta_one = 0.9
beta_two = 0.999
adam_eps = 1e-08
decay_rate = 0.01
rates = (0.08, 0.8, 0.08, 0.05, 0.6)

BF = jnp.bfloat16
F32 = jnp.float32
NN = (((1,), (0,)), ((), ()))
NT = (((1,), (1,)), ((), ()))
TN = (((0,), (0,)), ((), ()))
AXES = ("dp", "narrow")
VMEM_BYTES = 60 * 2**20
ROWS_GAIN = 16
GAIN_COLS = 512
PART = 6 * 128
HALF = 2 * PART
FF_BLOCK = 256
QUERY_BLOCK = 384
ROW_PARTS = (slice(0, 512), slice(512, LONG))


def dot(left, right, dims=NN):
    return lax.dot_general(left, right, dims, preferred_element_type=F32)


def params():
    return pltpu.CompilerParams(vmem_limit_bytes=VMEM_BYTES)


def shape(dims, dtype):
    return jax.ShapeDtypeStruct(dims, dtype)


IN_VMEM = pl.BlockSpec(memory_space=pltpu.VMEM)
IN_HBM = pl.BlockSpec(memory_space=pl.ANY)
IN_SMEM = pl.BlockSpec(memory_space=pltpu.SMEM)


BY_Z = (("z2", "z1"), ("z1", "z2"), ("x", "y"), ("y", "x"), ("core", "core"))
BY_PLANE = (("x", "y"), ("y", "x"), ("z2", "z1"), ("z1", "z2"), ("core", "core"))
BIT = {"y": 1, "core": 2, "x": 4, "z1": 8, "z2": 16}


def partners(kinds):
    return [(me, me ^ BIT[kinds[(me >> 1) & 1]]) for me in range(32)]


def swap(array, kinds):
    return lax.ppermute(array, AXES, partners(kinds))


def owner_of(me, index, order):
    flips = [0, 0]
    for step in range(4):
        if (index >> step) & 1:
            for core in range(2):
                flips[core] ^= BIT[order[step][core]]
    own = me ^ 2 if index >> 4 else me
    device = own ^ jnp.where((own >> 1) & 1 == 1, flips[1], flips[0])
    return device >> 1, device & 1


def tie(*values):
    return lax.optimization_barrier(values)


def total(*parts):
    return sum(part.astype(F32) for part in parts)


def joined(held, arrived):
    return jnp.concatenate((held, arrived), axis=0)


def add_low(parts, low, high):
    return total(*(part[low:high] for part in parts)).astype(BF)


def each_place(me_ref, arrays, order, body):
    if order is None:
        body(arrays[0].at[0], 0, 0)
        return
    me = me_ref[0]
    for index in range(32):
        dp, narrow = owner_of(me, index, order)
        body(arrays[index // 8].at[index % 8], dp, narrow)


def span(start, size, unit):
    if isinstance(start, int):
        return pl.ds(start * size, size)
    return pl.ds(pl.multiple_of(start * size, unit), size)


def head_rows(dp, fast):
    return (dp & 4) * 2 + (dp >> 3) * 4 + (dp & 3) if fast else 0


def load_half(me_ref, arrays, order, rows_piece, weight, sem):
    cols = PART if order else HALF

    def start(source, dp, narrow):
        pltpu.make_async_copy(
            source.at[pl.ds(0, rows_piece), pl.ds(0, cols)],
            weight.at[span(dp, rows_piece, 16), span(narrow, cols, 128)],
            sem,
        ).start()

    each_place(me_ref, arrays, order, start)


def first_project_kernel(order, rows_piece, me_ref, x_ref, *refs):
    n_arrays = 4 if order else 1
    arrays = refs[:n_arrays]
    out_ref, normed_ref, normed_t_ref, gains_ref, weight, gain_parts, sem, gain_sem = refs[n_arrays:]
    step = pl.program_id(0)

    @pl.when(step == 0)
    def _():
        slots = 8 if order else 1
        for index in range(n_arrays):
            pltpu.make_async_copy(
                arrays[index].at[:, pl.ds(rows_piece, ROWS_GAIN), pl.ds(0, GAIN_COLS)],
                gain_parts.at[pl.ds(index * slots, slots)],
                gain_sem,
            ).start()
        load_half(me_ref, arrays, order, rows_piece, weight, sem)
        x = x_ref[...].astype(F32)
        scaled = x * lax.rsqrt(jnp.mean(x * x, axis=-1, keepdims=True) + norm_eps)
        pltpu.make_async_copy(gain_parts, gain_parts, gain_sem).wait()
        parts = jnp.sum(gain_parts[...].astype(F32), axis=0)
        one = jnp.concatenate((parts[0:1], parts[1:2]), axis=1)
        gains_ref[...] = jnp.concatenate((one, jnp.concatenate((parts[2:3], parts[3:4]), axis=1)), axis=0)
        low = (scaled * one).astype(BF)
        normed_ref[...] = low
        normed_t_ref[...] = low.T
        pltpu.make_async_copy(weight, weight, sem).wait()

    column = pl.multiple_of(step * PART, PART)
    out_ref[...] = dot(normed_ref[...], weight[:, pl.ds(column, PART)]).astype(BF)


def first_project(me, tokens, arrays, order, rows_piece):
    rows = tokens.shape[0]
    full = lambda dims: pl.BlockSpec(dims, lambda step: (0,) * len(dims))
    return pl.pallas_call(
        functools.partial(first_project_kernel, order, rows_piece),
        grid=(2,),
        in_specs=[IN_SMEM, full((rows, HD))] + [IN_HBM] * len(arrays),
        out_specs=[
            pl.BlockSpec((rows, PART), lambda step: (0, step)),
            full((rows, HD)),
            full((HD, rows)),
            full((2, HD)),
        ],
        out_shape=[shape((rows, HALF), BF), shape((rows, HD), BF), shape((HD, rows), BF), shape((2, HD), F32)],
        scratch_shapes=[
            pltpu.VMEM((HD, HALF), BF),
            pltpu.VMEM((32 if order else 1, ROWS_GAIN, GAIN_COLS), BF),
            pltpu.SemaphoreType.DMA(()),
            pltpu.SemaphoreType.DMA(()),
        ],
        compiler_params=params(),
        name="first_project",
    )(me, tokens, *arrays)


def second_project_kernel(order, rows_piece, me_ref, normed_ref, *refs):
    n_arrays = 4 if order else 1
    arrays = refs[:n_arrays]
    out_ref, weight, sem = refs[n_arrays:]
    step = pl.program_id(0)

    @pl.when(step == 0)
    def _():
        load_half(me_ref, arrays, order, rows_piece, weight, sem)
        pltpu.make_async_copy(weight, weight, sem).wait()

    column = pl.multiple_of(step * PART, PART)
    out_ref[...] = dot(normed_ref[...], weight[:, pl.ds(column, PART)]).astype(BF)


def second_project(me, normed, arrays, order, rows_piece):
    rows = normed.shape[0]
    return pl.pallas_call(
        functools.partial(second_project_kernel, order, rows_piece),
        grid=(2,),
        in_specs=[IN_SMEM, pl.BlockSpec((rows, HD), lambda step: (0, 0))] + [IN_HBM] * len(arrays),
        out_specs=pl.BlockSpec((rows, PART), lambda step: (0, step)),
        out_shape=shape((rows, HALF), BF),
        scratch_shapes=[pltpu.VMEM((HD, HALF), BF), pltpu.SemaphoreType.DMA(())],
        compiler_params=params(),
        name="second_project",
    )(me, normed, *arrays)


def three_parts(values):
    first = values.astype(BF)
    rest = values - first.astype(F32)
    second = rest.astype(BF)
    return first, second, (rest - second.astype(F32)).astype(BF)


def mask_operands(segments):
    kind = jnp.arange(64, dtype=jnp.int32)
    mine = segments[None, :] + 1 == kind[:, None]
    query_side = jnp.where(mine, -1e30, 0.0).astype(BF)
    key_side = jnp.where((kind[None, :] < 4) & ~mine.T, 1.0, 0.0).astype(BF)
    return (
        jnp.concatenate((query_side, query_side), axis=0),
        jnp.concatenate((key_side, key_side), axis=1),
    )


def attend_forward_kernel(q_ref, k_ref, v_ref, mask_q_ref, mask_k_ref, out_ref, extra_ref):
    queries_t = (q_ref[...].astype(F32) * score_scale).astype(BF).T
    keys = k_ref[...]
    values_t = v_ref[...].T
    mask_q = mask_q_ref[...]
    mask_k = mask_k_ref[...]
    lane = lax.broadcasted_iota(jnp.int32, (1, 128), 1)
    row = lax.broadcasted_iota(jnp.int32, (64, 1), 0)
    ones = jnp.ones((16, LONG), BF)
    key_sides = (jnp.where(lane < 64, keys, mask_k), jnp.where(lane >= 64, keys, mask_k))
    query_sides = (
        jnp.concatenate((queries_t[0:64], mask_q[64:128]), axis=0),
        jnp.concatenate((mask_q[0:64], queries_t[64:128]), axis=0),
    )
    value_sides = [jnp.concatenate((values_t[64 * head : 64 * head + 64], ones), axis=0) for head in range(2)]
    out_blocks = ([], [])
    log_blocks = ([], [])

    def score(head, start):
        return dot(key_sides[head], query_sides[head][:, start : start + QUERY_BLOCK])

    def finish(head, top, expo):
        both = dot(value_sides[head], expo)
        sums = both[64:65]
        out_blocks[head].append((both[0:64] * (1.0 / sums)).astype(BF))
        log_blocks[head].append(-(top + jnp.log(sums)))

    jobs = [(head, start) for head in range(2) for start in range(0, LONG, QUERY_BLOCK)]
    scores = score(*jobs[0])
    waiting = None
    for index, job in enumerate(jobs):
        later = score(*jobs[index + 1]) if index + 1 < len(jobs) else None
        top = jnp.max(scores, axis=0, keepdims=True)
        expo = jnp.exp(scores - top).astype(BF)
        if waiting is not None:
            finish(*waiting)
        waiting = (job[0], top, expo)
        scores = later
    finish(*waiting)
    outs = [jnp.concatenate(blocks, axis=1) for blocks in out_blocks]
    extras = []
    for head in range(2):
        extra = mask_q[0:64].astype(F32)
        for index, part in enumerate(three_parts(jnp.concatenate(log_blocks[head], axis=1))):
            extra = jnp.where(row == 4 + index, part.astype(F32), extra)
        extras.append(extra.astype(BF))
    out_ref[...] = jnp.concatenate(outs, axis=0).T
    extra_ref[...] = jnp.concatenate((extras[1], extras[0]), axis=0).T


def tile_specs(rows, narrow, first):
    return [pl.BlockSpec((rows, 128), lambda i, c=c: (0, narrow * 6 + (first + i) * 3 + c)) for c in range(3)]


def attend_forward(projected, narrow, mask_q, mask_k):
    rows = projected.shape[0]
    tile = pl.BlockSpec((rows, 128), lambda i: (0, i))
    return pl.pallas_call(
        attend_forward_kernel,
        grid=(2,),
        in_specs=tile_specs(rows, narrow, 0)
        + [pl.BlockSpec((128, rows), lambda i: (0, 0)), pl.BlockSpec((rows, 128), lambda i: (0, 0))],
        out_specs=[tile, tile],
        out_shape=[shape((rows, 256), BF), shape((rows, 256), BF)],
        compiler_params=params(),
        name="attend_forward",
    )(projected, projected, projected, mask_q, mask_k)


def attend_backward_kernel(
    q_ref, k_ref, v_ref, out_ref, grad_ref, extra_ref, mask_k_ref, result_ref
):
    queries = (q_ref[...].astype(F32) * score_scale).astype(BF)
    queries_t = queries.T
    keys = k_ref[...]
    keys_t = keys.T
    values_t = v_ref[...].T
    grad = grad_ref[...]
    grad_t = grad.T
    extra = extra_ref[...]
    mask_k_t = mask_k_ref[...].T
    lane = lax.broadcasted_iota(jnp.int32, (1, 128), 1)
    row = lax.broadcasted_iota(jnp.int32, (64, 1), 0)
    product_t = (grad.astype(F32) * out_ref[...].astype(F32)).T
    inner = []
    for head in (1, 0):
        total = -jnp.sum(product_t[64 * head : 64 * head + 64], axis=0, keepdims=True)
        rows = jnp.zeros((64, LONG), F32)
        for index, part in enumerate(three_parts(total)):
            rows = jnp.where(row == index, part.astype(F32), rows)
        inner.append(rows.astype(BF))
    inner_cols = jnp.concatenate(inner, axis=0).T
    key_extra = jnp.where((row >= 4) & (row < 7), 1.0, mask_k_t[0:64].astype(F32)).astype(BF)
    value_extra = jnp.broadcast_to(jnp.where(row < 3, 1.0, 0.0).astype(BF), (64, LONG))
    grad_q = []
    grad_k = []
    grad_v = []
    for head in range(2):
        half = slice(64 * head, 64 * head + 64)
        own = (lane < 64) if head == 0 else (lane >= 64)
        query_side = jnp.where(own, queries, extra)
        grad_side = jnp.where(own, grad, inner_cols)
        if head == 0:
            key_side = jnp.concatenate((keys_t[half], key_extra), axis=0)
            value_side = jnp.concatenate((values_t[half], value_extra), axis=0)
        else:
            key_side = jnp.concatenate((key_extra, keys_t[half]), axis=0)
            value_side = jnp.concatenate((value_extra, values_t[half]), axis=0)
        q_blocks = []
        k_total = None
        v_total = None
        for start in range(0, LONG, QUERY_BLOCK):
            block = slice(start, start + QUERY_BLOCK)
            probs = jnp.exp(dot(query_side[block], key_side))
            grad_scores = (probs * dot(grad_side[block], value_side)).astype(BF)
            v_part = dot(grad_t[half, block], probs.astype(BF))
            k_part = dot(queries_t[half, block], grad_scores)
            v_total = v_part if v_total is None else v_total + v_part
            k_total = k_part if k_total is None else k_total + k_part
            q_blocks.append(dot(grad_scores, keys) * score_scale)
        grad_q.append(jnp.concatenate(q_blocks, axis=0))
        grad_k.append(k_total)
        grad_v.append(v_total)
    result_ref[:, 0:128] = jnp.where(lane < 64, grad_q[0], grad_q[1]).astype(BF)
    result_ref[:, 128:256] = jnp.concatenate(grad_k, axis=0).astype(BF).T
    result_ref[:, 256:384] = jnp.concatenate(grad_v, axis=0).astype(BF).T


def attend_backward(projected, attended, grad_attended, extra, mask_k, half, narrow, first, count):
    rows = projected.shape[0]
    own = pl.BlockSpec((rows, 128), lambda i: (0, first + i))
    return pl.pallas_call(
        attend_backward_kernel,
        grid=(count,),
        in_specs=tile_specs(rows, narrow, first)
        + [
            own,
            pl.BlockSpec((rows, 128), lambda i: (0, half * 4 + narrow * 2 + first + i)),
            own,
            pl.BlockSpec((rows, 128), lambda i: (0, 0)),
        ],
        out_specs=pl.BlockSpec((rows, 384), lambda i: (0, i)),
        out_shape=shape((rows, 384 * count), BF),
        compiler_params=params(),
        name="attend_backward",
    )(projected, projected, projected, attended, grad_attended, extra, mask_k)


def one_buffer(dims):
    return pl.BlockSpec(dims, lambda step: (0,) * len(dims), pipeline_mode=pl.Buffered(buffer_count=1))


def load_out(me_ref, arrays, order, rows_piece, w_out, sem):
    cols, at = (GAIN_COLS, PART) if order else (HD, HALF)

    def start(source, dp, narrow):
        pltpu.make_async_copy(
            source.at[pl.ds(0, rows_piece), pl.ds(at, cols)],
            w_out.at[span(head_rows(dp, order is not None), rows_piece, 16), span(narrow, cols, 128)],
            sem,
        ).start()

    each_place(me_ref, arrays, order, start)


def load_wide(me_ref, arrays, order, rows_piece, targets, sems):
    cols = targets[0].shape[1] // (2 if order else 1)

    def start(source, dp, narrow):
        for index, target in enumerate(targets):
            pltpu.make_async_copy(
                source.at[pl.ds(index * rows_piece, rows_piece)],
                target.at[span(dp, rows_piece, 16), span(narrow, cols, 128)],
                sems[index],
            ).start()

    each_place(me_ref, arrays, order, start)


def load_wide_by_half(me_ref, arrays, order, rows_piece, targets, sems):
    whole = targets[0].shape[1]
    if order is None:
        for index, target in enumerate(targets):
            for half in range(2):
                cols = pl.ds(half * (whole // 2), whole // 2)
                pltpu.make_async_copy(
                    arrays[0].at[0, pl.ds(index * rows_piece, rows_piece), cols], target.at[:, cols], sems.at[index, half]
                ).start()
        return
    for half in range(2):

        def start(source, dp, narrow, half=half):
            @pl.when(narrow == half)
            def _():
                for index, target in enumerate(targets):
                    pltpu.make_async_copy(
                        source.at[pl.ds(index * rows_piece, rows_piece)],
                        target.at[span(dp, rows_piece, 16), pl.ds(half * (whole // 2), whole // 2)],
                        sems.at[index, half],
                    ).start()

        each_place(me_ref, arrays, order, start)


def wait_half(targets, sems, half):
    whole = targets[0].shape[1]
    for index, target in enumerate(targets):
        part = target.at[:, pl.ds(half * (whole // 2), whole // 2)]
        pltpu.make_async_copy(part, part, sems.at[index, half]).wait()


def load_down(me_ref, arrays, order, w_down, sem):
    rows, cols = arrays[0].shape[1:]

    def start(source, dp, narrow):
        pltpu.make_async_copy(source, w_down.at[span(dp, rows, 16), span(narrow, cols, 128)], sem).start()

    each_place(me_ref, arrays, order, start)


N_GROUPS = 4


def load_down_by_group(me_ref, arrays, order, w_down, sems):
    rows, cols = arrays[0].shape[1:]
    if order is None:
        rows = rows // N_GROUPS
        for group in range(N_GROUPS):
            part = pl.ds(group * rows, rows)
            pltpu.make_async_copy(arrays[0].at[0, part], w_down.at[part], sems.at[group]).start()
        return

    def start(source, dp, narrow):
        pltpu.make_async_copy(
            source, w_down.at[span(dp, rows, 16), span(narrow, cols, 128)], sems.at[dp >> 2]
        ).start()

    each_place(me_ref, arrays, order, start)


def wait_group(w_down, sems, group):
    rows = w_down.shape[0] // N_GROUPS
    part = w_down.at[pl.ds(group * rows, rows)]
    pltpu.make_async_copy(part, part, sems.at[group]).wait()


def at_step(step, wanted, body):
    pl.when(step == wanted)(body)


def last_step_of(rows):
    return -(-rows // FF_BLOCK) - 1


def all_of(ref, sem):
    pltpu.make_async_copy(ref, ref, sem).wait()


def gelu_parts(gate):
    square = gate * gate
    curve = jnp.tanh(0.7978845608028654 * gate * (1.0 + 0.044715 * square))
    half = 0.5 * (1.0 + curve)
    slope = half + (0.5 * gate) * (1.0 - curve * curve) * (
        0.7978845608028654 + (0.7978845608028654 * 3.0 * 0.044715) * square
    )
    return gate * half, slope


def feed_in_kernel(orders, rows_piece, me_ref, x_ref, att_a, att_b, att_c, att_d, cotangent_ref, valid_ref, gains_ref, *refs):
    square_order, wide_order, down_order = orders
    n_arrays = 4 if wide_order else 1
    square, wide = (refs[i * n_arrays : (i + 1) * n_arrays] for i in range(2))
    refs = refs[2 * n_arrays :]
    active_ref, sloped_ref, inner_ref, hidden_out, normed_t_out, grad_mixed_out = refs[:6]
    grad_down = refs[6 : 6 + n_arrays]
    w_out, w_gate, w_up, w_down, hidden, normed, normed_t, grad_mixed, sem, wide_sems, out_sems, down_sems = refs[6 + n_arrays :]
    step = pl.program_id(0)

    @pl.when(step == 0)
    def _():
        load_out(me_ref, square, square_order, rows_piece, w_out, sem)
        load_wide_by_half(me_ref, wide, wide_order, rows_piece, (w_gate, w_up), wide_sems)
        gain = gains_ref[1:2]
        all_of(w_out, sem)

        def before(index, carry):
            part = pl.ds(pl.multiple_of(index * QUERY_BLOCK, QUERY_BLOCK), QUERY_BLOCK)
            left = jnp.concatenate([ref[part, :] for ref in (att_a, att_b, att_c, att_d)], axis=1)
            state = x_ref[part, :].astype(F32) + dot(left, w_out[...])
            hidden[part, :] = state
            low = (state * lax.rsqrt(jnp.mean(state * state, axis=-1, keepdims=True) + norm_eps) * gain).astype(BF)
            normed[part, :] = low
            normed_t[:, part] = low.T
            grad_mixed[part, :] = (cotangent_ref[part, :].astype(F32) * valid_ref[part, :]).astype(BF)
            return carry

        lax.fori_loop(0, x_ref.shape[0] // QUERY_BLOCK, before, 0)
        pltpu.make_async_copy(hidden, hidden_out, out_sems.at[0]).start()
        pltpu.make_async_copy(normed_t, normed_t_out, out_sems.at[1]).start()
        pltpu.make_async_copy(grad_mixed, grad_mixed_out, out_sems.at[2]).start()
        wait_half((w_gate, w_up), wide_sems, 0)

    at_step(step, w_gate.shape[1] // 2 // FF_BLOCK, lambda: wait_half((w_gate, w_up), wide_sems, 1))
    cols = pl.ds(pl.multiple_of(step * FF_BLOCK, FF_BLOCK), FF_BLOCK)
    gate_w = w_gate[:, cols]
    up_w = w_up[:, cols]
    found = [(dot(normed[part, :], gate_w), dot(normed[part, :], up_w)) for part in ROW_PARTS]
    down_sum = None
    for part, (gate, upward) in zip(ROW_PARTS, found):
        active, slope = gelu_parts(gate)
        active_ref[part, :] = active.astype(BF)
        sloped_ref[part, :] = (upward * slope).astype(BF)
        inner = (active * upward).astype(BF)
        inner_ref[part, :] = inner
        down_part = dot(inner.T, grad_mixed[part, :])
        down_sum = down_part if down_sum is None else down_sum + down_part
    w_down[cols, :] = down_sum.astype(BF)

    ff = w_down.shape[0]
    for group in range(N_GROUPS):

        def store_group(group=group):
            if down_order is None:
                part = pl.ds(group * (ff // N_GROUPS), ff // N_GROUPS)
                pltpu.make_async_copy(w_down.at[part], grad_down[0].at[0, part], down_sems.at[group]).start()
                return

            def finish(target, dp, narrow):
                rows, width = target.shape

                @pl.when(dp >> 2 == group)
                def _():
                    pltpu.make_async_copy(
                        w_down.at[span(dp, rows, 16), span(narrow, width, 128)], target, down_sems.at[group]
                    ).start()

            each_place(me_ref, grad_down, down_order, finish)

        at_step(step, last_step_of((group + 1) * (ff // N_GROUPS)), store_group)

    @pl.when(step == pl.num_programs(0) - 1)
    def _():
        pltpu.make_async_copy(hidden, hidden_out, out_sems.at[0]).wait()
        pltpu.make_async_copy(normed_t, normed_t_out, out_sems.at[1]).wait()
        pltpu.make_async_copy(grad_mixed, grad_mixed_out, out_sems.at[2]).wait()
        for group in range(N_GROUPS):
            wait_group(w_down, down_sems, group)


def feed_in(me, tokens, attended, cotangent, valid, gains, square, wide, orders, rows_piece, ff, down_shape):
    rows = tokens.shape[0]
    n_arrays = len(square)
    tile = pl.BlockSpec((rows, FF_BLOCK), lambda step: (0, step))
    outs = pl.pallas_call(
        functools.partial(feed_in_kernel, orders, rows_piece),
        grid=(ff // FF_BLOCK,),
        in_specs=[IN_SMEM]
        + [one_buffer(array.shape) for array in (tokens, *attended, cotangent, valid, gains)]
        + [IN_HBM] * (2 * n_arrays),
        out_specs=[tile] * 3 + [IN_HBM] * (3 + n_arrays),
        out_shape=[
            shape((rows, ff), BF),
            shape((rows, ff), BF),
            shape((rows, ff), BF),
            shape((rows, HD), F32),
            shape((HD, rows), BF),
            shape((rows, HD), BF),
        ]
        + [shape(down_shape, BF)] * n_arrays,
        scratch_shapes=[
            pltpu.VMEM((HD, HD), BF),
            pltpu.VMEM((HD, ff), BF),
            pltpu.VMEM((HD, ff), BF),
            pltpu.VMEM((ff, HD), BF),
            pltpu.VMEM((rows, HD), F32),
            pltpu.VMEM((rows, HD), BF),
            pltpu.VMEM((HD, rows), BF),
            pltpu.VMEM((rows, HD), BF),
            pltpu.SemaphoreType.DMA(()),
            pltpu.SemaphoreType.DMA((2, 2)),
            pltpu.SemaphoreType.DMA((3,)),
            pltpu.SemaphoreType.DMA((N_GROUPS,)),
        ],
        compiler_params=params(),
        name="feed_in",
    )(me, tokens, *attended, cotangent, valid, gains, *square, *wide)
    return (*outs[:6], outs[6:])


def feed_grad_kernel(orders, rows_piece, me_ref, active_ref, sloped_ref, grad_mixed_ref, normed_t_ref, *refs):
    wide_order, down_order = orders
    n_arrays = 4 if wide_order else 1
    down = refs[:n_arrays]
    grad_gate_ref, grad_up_ref = refs[n_arrays : n_arrays + 2]
    grad_wide = refs[n_arrays + 2 : 2 * n_arrays + 2]
    w_down, w_gate, w_up, down_sems, out_sems = refs[2 * n_arrays + 2 :]
    step = pl.program_id(0)

    @pl.when(step == 0)
    def _():
        load_down_by_group(me_ref, down, down_order, w_down, down_sems)

    ff = w_down.shape[0]
    for group in range(N_GROUPS):
        at_step(step, group * (ff // N_GROUPS) // FF_BLOCK, lambda group=group: wait_group(w_down, down_sems, group))

    cols = pl.ds(pl.multiple_of(step * FF_BLOCK, FF_BLOCK), FF_BLOCK)
    grad_inner = dot(grad_mixed_ref[...], w_down[cols, :], NT)
    grad_gate = (grad_inner * sloped_ref[...].astype(F32)).astype(BF)
    grad_up = (grad_inner * active_ref[...].astype(F32)).astype(BF)
    grad_gate_ref[...] = grad_gate
    grad_up_ref[...] = grad_up
    w_gate[:, cols] = dot(normed_t_ref[...], grad_gate).astype(BF)
    w_up[:, cols] = dot(normed_t_ref[...], grad_up).astype(BF)

    ends = (ff // 2, ff // 2 + 3 * FF_BLOCK + FF_BLOCK // 2, ff)
    width = ff // 2 if wide_order else ff
    for place, (begin, end) in enumerate(zip((0, *ends), ends)):

        def store(place=place, begin=begin, end=end):
            count = end - begin

            def finish(target, dp, narrow):
                def copies():
                    for index, source in enumerate((w_gate, w_up)):
                        pltpu.make_async_copy(
                            source.at[span(dp, rows_piece, 16), pl.ds(begin, count)],
                            target.at[pl.ds(index * rows_piece, rows_piece), pl.ds(begin % width, count)],
                            out_sems.at[index, place],
                        ).start()

                if wide_order is None:
                    copies()
                else:
                    pl.when(narrow == begin // width)(copies)

            each_place(me_ref, grad_wide, wide_order, finish)

        at_step(step, last_step_of(end), store)

    @pl.when(step == pl.num_programs(0) - 1)
    def _():
        for index, source in enumerate((w_gate, w_up)):
            for place, (begin, end) in enumerate(zip((0, *ends), ends)):
                part = source.at[:, pl.ds(begin, end - begin)]
                pltpu.make_async_copy(part, part, out_sems.at[index, place]).wait()


def feed_grad(me, active, sloped, grad_mixed, normed_t, down, orders, rows_piece, wide_shape):
    rows, ff = active.shape
    n_arrays = len(down)
    tile = pl.BlockSpec((rows, FF_BLOCK), lambda step: (0, step))
    outs = pl.pallas_call(
        functools.partial(feed_grad_kernel, orders, rows_piece),
        grid=(ff // FF_BLOCK,),
        in_specs=[IN_SMEM, tile, tile, one_buffer((rows, HD)), one_buffer((HD, rows))] + [IN_HBM] * n_arrays,
        out_specs=[tile, tile] + [IN_HBM] * n_arrays,
        out_shape=[shape((rows, ff), BF)] * 2 + [shape(wide_shape, BF)] * n_arrays,
        scratch_shapes=[
            pltpu.VMEM((ff, HD), BF),
            pltpu.VMEM((HD, ff), BF),
            pltpu.VMEM((HD, ff), BF),
            pltpu.SemaphoreType.DMA((N_GROUPS,)),
            pltpu.SemaphoreType.DMA((2, 3)),
        ],
        compiler_params=params(),
        name="feed_grad",
    )(me, active, sloped, grad_mixed, normed_t, *down)
    return outs[0], outs[1], outs[2:]


def feed_out_kernel(orders, rows_piece, me_ref, inner_ref, grad_gate_ref, grad_up_ref, hidden_ref, grad_mixed_ref, gains_ref, *refs):
    square_order, wide_order, down_order = orders
    n_arrays = 4 if wide_order else 1
    square, wide, down = (refs[i * n_arrays : (i + 1) * n_arrays] for i in range(3))
    mixed_ref, grad_hidden_ref, grad_attended_ref, gain_grad_ref = refs[3 * n_arrays : 3 * n_arrays + 4]
    w_out, w_gate, w_up, w_down, sems = refs[3 * n_arrays + 4 :]
    step = pl.program_id(0)

    @pl.when(step == 0)
    def _():
        load_down(me_ref, down, down_order, w_down, sems.at[3])
        load_wide(me_ref, wide, wide_order, rows_piece, (w_gate, w_up), (sems.at[1], sems.at[2]))
        load_out(me_ref, square, square_order, rows_piece, w_out, sems.at[0])
        gain_grad_ref[...] = jnp.zeros_like(gain_grad_ref)
        all_of(w_down, sems.at[3])

    @pl.when(step < pl.num_programs(0) // 2)
    def _():
        mixed_ref[...] = (hidden_ref[...] + dot(inner_ref[...], w_down[...])).astype(BF)

    @pl.when(step == pl.num_programs(0) // 2)
    def _():
        all_of(w_gate, sems.at[1])
        all_of(w_up, sems.at[2])
        all_of(w_out, sems.at[0])

    @pl.when(step >= pl.num_programs(0) // 2)
    def _():
        state = hidden_ref[...]
        through = dot(grad_gate_ref[...], w_gate[...], NT) + dot(grad_up_ref[...], w_up[...], NT)
        scale = lax.rsqrt(jnp.mean(state * state, axis=-1, keepdims=True) + norm_eps)
        unit = state * scale
        gain_grad_ref[...] += jnp.sum(through * unit, axis=0, keepdims=True)
        through = through * gains_ref[1:2]
        result = grad_mixed_ref[...].astype(F32) + scale * (
            through - unit * jnp.mean(through * unit, axis=-1, keepdims=True)
        )
        grad_hidden_ref[...] = result
        grad_attended_ref[...] = dot(result.astype(BF), w_out[...], NT).astype(BF)


def feed_out(me, inner, grad_gate, grad_up, hidden, grad_mixed, gains, square, wide, down, orders, rows_piece):
    rows, ff = inner.shape
    n_arrays = len(down)
    count = rows // QUERY_BLOCK
    early = lambda cols: pl.BlockSpec((QUERY_BLOCK, cols), lambda step: (jnp.minimum(step, count - 1), 0))
    late = lambda cols: pl.BlockSpec((QUERY_BLOCK, cols), lambda step: (jnp.maximum(step - count, 0), 0))
    both = pl.BlockSpec((QUERY_BLOCK, HD), lambda step: (step % count, 0))
    return pl.pallas_call(
        functools.partial(feed_out_kernel, orders, rows_piece),
        grid=(2 * count,),
        in_specs=[IN_SMEM, early(ff), late(ff), late(ff), both, late(HD), one_buffer((2, HD))]
        + [IN_HBM] * (3 * n_arrays),
        out_specs=[early(HD), late(HD), late(HD), pl.BlockSpec((1, HD), lambda step: (0, 0))],
        out_shape=[shape((rows, HD), BF), shape((rows, HD), F32), shape((rows, HD), BF), shape((1, HD), F32)],
        scratch_shapes=[
            pltpu.VMEM((HD, HD), BF),
            pltpu.VMEM((HD, ff), BF),
            pltpu.VMEM((HD, ff), BF),
            pltpu.VMEM((ff, HD), BF),
            pltpu.SemaphoreType.DMA((4,)),
        ],
        compiler_params=params(),
        name="feed_out",
    )(me, inner, grad_gate, grad_up, hidden, grad_mixed, gains, *square, *wide, *down)


def half_of_grads(refs):
    wide = []
    held = []
    for ref in refs:
        held.append(ref)
        if sum(part.shape[1] for part in held) == PART:
            wide.append(held)
            held = []
    return wide


def fetch(sources, targets, sems):
    copies = [pltpu.make_async_copy(*triple) for triple in zip(sources, targets, sems)]
    for copy in copies:
        copy.start()

    def get(index):
        copies[index].wait()
        return targets[index][...]

    return get


def fetched(arrays):
    return [pltpu.VMEM(array.shape, array.dtype) for array in arrays] + [pltpu.SemaphoreType.DMA((len(arrays),))]


def weight_grad_kernel(order, rows_piece, n_grads, with_out, me_ref, *refs):
    n_arrays = 4 if order else 1
    fast = order is not None
    n_in = 1 + n_grads + (5 if with_out else 0)
    sources, targets, own = refs[:n_in], refs[n_in : n_in + n_arrays], refs[n_in + n_arrays :]
    held, in_sems = own[:n_in], own[n_in]
    weight, sems = own[n_in + 1 : n_in + 3]
    get = fetch(sources, held, [in_sems.at[index] for index in range(n_in)])
    cols = PART if fast else HALF
    left = get(0)
    begin = 1
    for index, group in enumerate(half_of_grads(sources[1 : 1 + n_grads])):
        right = [get(begin + place) for place in range(len(group))]
        begin += len(group)
        right = right[0] if len(right) == 1 else jnp.concatenate(right, axis=1)
        part = pl.ds(index * PART, PART)
        weight[:, part] = dot(left, right).astype(BF)

        def finish(target, dp, narrow, index=index, part=part):
            copy = pltpu.make_async_copy(
                weight.at[span(dp, rows_piece, 16), part],
                target.at[pl.ds(0, rows_piece), pl.ds(0 if fast else index * PART, PART)],
                sems.at[index],
            )
            if fast:
                pl.when(narrow == index)(copy.start)
            else:
                copy.start()

        each_place(me_ref, targets, order, finish)
    if with_out:
        w_out, out_sem = own[n_in + 3 :]
        col_d = GAIN_COLS if fast else HD
        attended = [get(1 + n_grads + index) for index in range(4)]
        branch = get(n_in - 1).astype(BF)
        for index in range(4):
            w_out[index * 256 : (index + 1) * 256, :] = dot(attended[index].T, branch).astype(BF)

        def finish_out(target, dp, narrow):
            pltpu.make_async_copy(
                w_out.at[span(head_rows(dp, fast), rows_piece, 16), span(narrow, col_d, 128)],
                target.at[pl.ds(0, rows_piece), pl.ds(cols, col_d)],
                out_sem,
            ).start()

        each_place(me_ref, targets, order, finish_out)
        all_of(w_out, out_sem)
    for index in range(2):
        part = weight.at[:, pl.ds(index * PART, PART)]
        pltpu.make_async_copy(part, part, sems.at[index]).wait()


def weight_grad(me, normed_t, grads, order, rows_piece, attended=(), grad_hidden=None):
    with_out = grad_hidden is not None
    cols = (PART if order else HALF) + ((GAIN_COLS if order else HD) if with_out else 0)
    outs = [shape((8 if order else 1, rows_piece, cols), BF)] * (4 if order else 1)
    more = [*attended, grad_hidden] if with_out else []
    given = [normed_t, *grads, *more]
    scratch = fetched(given) + [pltpu.VMEM((HD, HALF), BF), pltpu.SemaphoreType.DMA((2,))]
    if with_out:
        scratch += [pltpu.VMEM((HD, HD), BF), pltpu.SemaphoreType.DMA(())]
    return pl.pallas_call(
        functools.partial(weight_grad_kernel, order, rows_piece, len(grads), with_out),
        in_specs=[IN_SMEM] + [IN_HBM] * len(given),
        out_specs=[IN_HBM] * len(outs),
        out_shape=outs,
        scratch_shapes=scratch,
        compiler_params=params(),
        name="weight_grad",
    )(me, *given)


def input_grad_kernel(order, rows_piece, n_grads, last, me_ref, *refs):
    n_arrays = 4 if order else 1
    n_in = n_grads + (3 if last else 0)
    arrays, sources = refs[:n_arrays], refs[n_arrays : n_arrays + n_in]
    refs = refs[n_arrays + n_in :]
    if last:
        gains_ref, out_ref, gain_grad_ref = refs[:3]
        refs = refs[3:]
    else:
        out_ref = refs[0]
        refs = refs[1:]
    held, in_sems, weight, sem = refs[:n_in], refs[n_in], refs[n_in + 1], refs[n_in + 2]
    load_half(me_ref, arrays, order, rows_piece, weight, sem)
    get = fetch(sources, held, [in_sems.at[index] for index in range(n_in)])
    left = jnp.concatenate([get(index) for index in range(n_grads)], axis=1)
    all_of(weight, sem)
    if not last:
        out_ref[...] = dot(left, weight[...], NT)
        return
    out_ref[...] = dot(left, weight[...], NT)
    through = get(n_grads) + out_ref[...]
    x = get(n_grads + 1).astype(F32)
    scale = lax.rsqrt(jnp.mean(x * x, axis=-1, keepdims=True) + norm_eps)
    unit = x * scale
    gain_grad_ref[...] = jnp.sum(through * unit, axis=0, keepdims=True)
    through = through * gains_ref[0:1]
    out_ref[...] = get(n_grads + 2) + scale * (through - unit * jnp.mean(through * unit, axis=-1, keepdims=True))


def input_gradient(me, grads, arrays, order, rows_piece, more=(), gains=None):
    rows = grads[0].shape[0]
    last = gains is not None
    given = [*grads, *more]
    outs = [shape((rows, HD), F32)] + ([shape((1, HD), F32)] if last else [])
    return pl.pallas_call(
        functools.partial(input_grad_kernel, order, rows_piece, len(grads), last),
        in_specs=[IN_SMEM] + [IN_HBM] * (len(arrays) + len(given)) + ([IN_VMEM] if last else []),
        out_specs=[IN_VMEM] * len(outs),
        out_shape=outs,
        scratch_shapes=fetched(given) + [pltpu.VMEM((HD, HALF), BF), pltpu.SemaphoreType.DMA(())],
        compiler_params=params(),
        name="input_gradient",
    )(me, *arrays, *given, *([gains] if last else []))


def segment_ids(bucket_one, text_one):
    position = jnp.arange(LONG, dtype=jnp.int32)
    slot_index = position // SLOT
    inside = position - slot_index * SLOT
    slot_length = SHORT_PATCH + jnp.where(
        slot_index == 0, text_one[0], jnp.where(slot_index == 1, text_one[1], text_one[2])
    )
    long_valid = position < LONG_PATCH + text_one[0]
    short_valid = inside < slot_length
    return jnp.where(
        bucket_one == 1, jnp.where(long_valid, 0, -1), jnp.where(short_valid, slot_index, -1)
    ).astype(jnp.int32)


def adamw(weight, grad_total, first, second, rate):
    first_new = beta_one * first + (1.0 - beta_one) * grad_total
    second_new = beta_two * second + (1.0 - beta_two) * grad_total * grad_total
    first_hat = first_new / (1.0 - beta_one**STEP)
    second_hat = second_new / (1.0 - beta_two**STEP)
    weight_new = weight - rate * (first_hat / (jnp.sqrt(second_hat) + adam_eps) + decay_rate * weight)
    return (grad_total, first_new, second_new, weight_new)


def heads_first(array):
    rows = array.shape[1]
    return array.reshape(3, rows, 2, 2, 2, 128).transpose(3, 1, 2, 4, 0, 5).reshape(2, rows, HALF)


def heads_back(first, second):
    rows = first.shape[0]
    stacked = jnp.stack((first, second)).reshape(2, rows, 2, 2, 3, 128)
    return stacked.transpose(4, 1, 2, 0, 3, 5).reshape(3, rows, HD)


def gain_block(low_gains, cols):
    return jnp.pad(low_gains.reshape(4, GAIN_COLS), ((0, ROWS_GAIN - 4), (0, cols - GAIN_COLS)))


def local(n_dp, n_narrow, tokens, cotangent, bucket, text_lengths, *weights):
    attn_qkv, attn_out, ffn_in, ffn_out, norm_gains = weights[:5]
    masters, firsts, seconds = weights[:5], weights[5:10], weights[10:]
    run = local_fast if (n_dp, n_narrow) == (16, 2) else local_any
    linear = lax.axis_index("dp") * n_narrow + lax.axis_index("narrow")
    me = linear.astype(jnp.int32)[None]
    own = norm_gains.shape[1]
    low_gains = lax.dynamic_update_slice(jnp.zeros((2, HD), BF), norm_gains.astype(BF), (0, linear * own))
    segments = segment_ids(bucket[0], text_lengths[0])
    valid = (segments >= 0).astype(F32)[:, None]
    masks = mask_operands(segments)
    mixed, input_grad, shares, gain_sums = run(
        me, tokens, cotangent, valid, masks, attn_qkv, attn_out, ffn_in, ffn_out, low_gains
    )
    shares = (*shares, lax.dynamic_slice(gain_sums, (0, linear * own), (2, own)))
    results = [mixed, input_grad]
    for index in range(5):
        results.extend(adamw(masters[index], shares[index], firsts[index], seconds[index], rates[index]))
    return tuple(results)


def local_fast(me, tokens, cotangent, valid, masks, attn_qkv, attn_out, ffn_in, ffn_out, low_gains):
    mask_q, mask_k = masks
    row_d, width = attn_out.shape
    row_f, col_f = ffn_out.shape[0], ffn_in.shape[2]
    low_qkv = attn_qkv.astype(BF).reshape(3, row_d, 2, 2, 128).transpose(2, 1, 3, 0, 4).reshape(2, row_d, PART)
    one = joined(low_qkv[0], gain_block(low_gains, PART))[None]
    two = jnp.concatenate((low_qkv[1], attn_out.astype(BF)), axis=1)[None]
    wide = ffn_in.astype(BF).reshape(1, 2 * row_d, col_f)
    down = ffn_out.astype(BF)[None]
    z_a, z_b, z_c, z_d, core = BY_Z
    p_a, p_b, p_c, p_d, _ = BY_PLANE

    one_in, down_in, two, wide = tie(swap(one, z_a), swap(down, p_a), two, wide)
    one, down = joined(one, one_in), joined(down, down_in)
    one_in, down_in, two, wide = tie(swap(one, z_b), swap(down, p_b), two, wide)
    one, down = joined(one, one_in), joined(down, down_in)
    one_in, two_in, down, wide, valid = tie(swap(one, z_c), swap(two, z_a), down, wide, valid)
    one, two = joined(one, one_in), joined(two, two_in)
    one_more, one_away, two_in, wide, down, mask_q, mask_k = tie(
        swap(one, z_d), swap(one, core), swap(two, z_b), wide, down, mask_q, mask_k
    )
    one_last = swap(one_more, core)
    two = joined(two, two_in)
    one_last, two, cotangent = tie(one_last, two, cotangent)
    two_in = swap(two, z_c)
    wide_in = swap(wide, z_a)
    ones = (one, one_more, one_away, one_last)
    first, normed, normed_t, gains = first_project(me, tokens, ones, BY_Z, row_d)
    first, two_in, wide_in, down = tie(first, two_in, wide_in, down)
    two = joined(two, two_in)
    wide = joined(wide, wide_in)
    two_more = swap(two, z_d)
    wide_in = swap(wide, z_b)
    two_away = swap(two, core)
    att_a, extra_a = attend_forward(first, 0, mask_q, mask_k)
    first, att_a, two_more, two_away, wide_in, down = tie(first, att_a, two_more, two_away, wide_in, down)
    wide = joined(wide, wide_in)
    two_last = swap(two_more, core)
    wide_in = swap(wide, z_c)
    down_in = swap(down, p_c)
    att_b, extra_b = attend_forward(first, 1, mask_q, mask_k)
    normed, att_b, two_last, wide_in, down_in = tie(normed, att_b, two_last, wide_in, down_in)
    wide = joined(wide, wide_in)
    down = joined(down, down_in)
    twos = (two, two_more, two_away, two_last)
    wide_more = swap(wide, z_d)
    wide_away = swap(wide, core)
    down_more = swap(down, p_d)
    second = second_project(me, normed, twos, BY_Z, row_d)
    second, wide_away, down_next = tie(second, wide_away, down)
    att_c, extra_c = attend_forward(second, 0, mask_q, mask_k)
    second, att_c, down_next = tie(second, att_c, down_next)
    down_away = swap(down_next, core)
    att_d, extra_d = attend_forward(second, 1, mask_q, mask_k)
    att_d, down_away, wide_more, down_more = tie(att_d, down_away, wide_more, down_more)
    wide_last = swap(wide_more, core)
    wide_last, down_more = tie(wide_last, down_more)
    wides = (wide, wide_more, wide_away, wide_last)
    attended = (att_a, att_b, att_c, att_d)
    extras = (extra_a, extra_b, extra_c, extra_d)
    down_last = swap(down_more, core)
    active, sloped, inner, hidden, normed_two_t, grad_mixed, g_down = feed_in(
        me, tokens, attended, cotangent, valid, gains, twos, wides, (BY_Z, BY_Z, BY_PLANE), row_d, 2 * col_f,
        (8, row_f, width),
    )
    grad_mixed, g_down, down_last = tie(grad_mixed, g_down, down_last)
    downs = (down, down_more, down_away, down_last)

    def back(half, narrow, start, count, grad_now):
        place = half * 2 + narrow
        return attend_backward(
            (first, second)[half], attended[place], grad_now, extras[place], mask_k, half, narrow, start, count
        )

    d_on = swap(g_down[3], core)
    d_other = swap(g_down[2], core)
    grad_gate, grad_up, g_wide = feed_grad(
        me, active, sloped, grad_mixed, normed_two_t, downs, (BY_Z, BY_PLANE), row_d, (8, 2 * row_d, col_f)
    )
    grad_gate, g_wide, d_on, d_other = tie(grad_gate, g_wide, d_on, d_other)
    d_in = swap(add_low((g_down[1], d_on), 0, 8), p_d)
    w_on = swap(g_wide[3], core)
    w_other = swap(g_wide[2], core)
    mixed, grad_hidden, grad_att, gain_two = feed_out(
        me, inner, grad_gate, grad_up, hidden, grad_mixed, gains, twos, wides, downs, (BY_Z, BY_Z, BY_PLANE), row_d
    )
    grad_att, d_in, w_on, w_other = tie(grad_att, d_in, w_on, w_other)
    w_in = swap(add_low((g_wide[1], w_on), 0, 8), z_d)
    d_parts = [g_down[0], d_other, d_in]
    d_next = swap(add_low(d_parts, 4, 8), p_c)
    back_a = back(0, 0, 0, 2, grad_att)
    grad_att, back_a, d_next = tie(grad_att, back_a, d_next)
    d_parts.append(d_next)
    d_next = swap(add_low(d_parts, 2, 4), p_b)
    back_c = back(0, 1, 0, 2, grad_att)
    normed_t, back_c, w_in, d_next = tie(normed_t, back_c, w_in, d_next)
    d_parts.append(d_next)
    d_next = swap(add_low(d_parts, 1, 2), p_a)
    w_parts = [g_wide[0], w_other, w_in]
    w_next = swap(add_low(w_parts, 4, 8), z_c)
    g_one = weight_grad(me, normed_t, (back_a, back_c), BY_Z, row_d, attended, grad_hidden)
    grad_att, g_one, w_next, d_next = tie(grad_att, g_one, w_next, d_next)
    d_parts.append(d_next)
    w_parts.append(w_next)
    o_on = swap(g_one[3], core)
    o_other = swap(g_one[2], core)
    w_next = swap(add_low(w_parts, 2, 4), z_b)
    back_d = back(1, 0, 0, 1, grad_att)
    grad_att, back_d, o_on, o_other = tie(grad_att, back_d, o_on, o_other)
    o_in = swap(add_low((g_one[1], o_on), 0, 8), z_d)
    back_e = back(1, 0, 1, 1, grad_att)
    grad_att, back_e, w_next, o_in = tie(grad_att, back_e, w_next, o_in)
    w_parts.append(w_next)
    o_parts = [g_one[0], o_other, o_in]
    w_next = swap(add_low(w_parts, 1, 2), z_a)
    o_next = swap(add_low(o_parts, 4, 8), z_c)
    back_f = back(1, 1, 0, 2, grad_att)
    back_f, normed_t, w_next, o_next = tie(back_f, normed_t, w_next, o_next)
    w_parts.append(w_next)
    o_parts.append(o_next)
    o_next = swap(add_low(o_parts, 2, 4), z_b)
    g_two = weight_grad(me, normed_t, (back_d, back_e, back_f), BY_Z, row_d)
    g_two, o_next = tie(g_two, o_next)
    o_parts.append(o_next)
    t_on = swap(g_two[3], core)
    t_other = swap(g_two[2], core)
    tokens, t_on, t_other = tie(tokens, t_on, t_other)
    t_in = swap(add_low((g_two[1], t_on), 0, 8), z_d)
    o_next = swap(add_low(o_parts, 1, 2), z_a)
    (through,) = input_gradient(me, (back_a, back_c), ones, BY_Z, row_d)
    through, t_in, o_next = tie(through, t_in, o_next)
    o_parts.append(o_next)
    t_parts = [g_two[0], t_other, t_in]
    t_next = swap(add_low(t_parts, 4, 8), z_c)
    input_grad, gain_one = input_gradient(
        me, (back_d, back_e, back_f), twos, BY_Z, row_d, (through, tokens, grad_hidden), gains
    )
    gain_one, t_next = tie(gain_one, t_next)
    gain_sums = jnp.concatenate((gain_one, gain_two), axis=0)
    t_parts.append(t_next)
    t_next = swap(add_low(t_parts, 2, 4), z_b)
    gain_in = swap(gain_sums, z_c)
    share_ffin = total(*(part[0] for part in w_parts)).reshape(2, row_d, col_f)
    share_down = total(*(part[0] for part in d_parts))
    t_next, gain_in = tie(t_next, gain_in)
    t_parts.append(t_next)
    gain_sums = gain_sums + gain_in
    t_next = swap(add_low(t_parts, 1, 2), z_a)
    gain_sums = gain_sums + swap(gain_sums, z_b)
    gain_sums = gain_sums + swap(gain_sums, z_a)
    gain_sums = gain_sums + swap(gain_sums, z_d)
    gain_sums = gain_sums + swap(gain_sums, core)
    t_parts.append(t_next)
    share_one = total(*(part[0] for part in o_parts))
    share_two = total(*(part[0] for part in t_parts))
    share_qkv = jnp.stack((share_one[:, :PART], share_two)).reshape(2, row_d, 2, 3, 128)
    share_qkv = share_qkv.transpose(3, 1, 0, 2, 4).reshape(3, row_d, width)
    return mixed, input_grad, (share_qkv, share_one[:, PART:], share_ffin, share_down), gain_sums


def local_any(me, tokens, cotangent, valid, masks, attn_qkv, attn_out, ffn_in, ffn_out, low_gains):
    mask_q, mask_k = masks

    def whole(array, axis):
        wide = lax.all_gather(array.astype(BF), "narrow", axis=axis + 1, tiled=True)
        return lax.all_gather(wide, "dp", axis=axis, tiled=True)

    def own(grad, axis):
        rows = lax.psum_scatter(grad, "dp", scatter_dimension=axis, tiled=True)
        return lax.psum_scatter(rows, "narrow", scatter_dimension=axis + 1, tiled=True).astype(F32)

    halves = heads_first(whole(attn_qkv, 1))
    full_gains = lax.psum(low_gains, AXES)
    full_out = whole(attn_out, 0).reshape(2, 2, 256, HD).transpose(1, 0, 2, 3).reshape(HD, HD)
    full_ffin = whole(ffn_in, 1)
    ff = full_ffin.shape[2]
    ones = (joined(halves[0], gain_block(full_gains, HALF))[None],)
    twos = (jnp.concatenate((halves[1], full_out), axis=1)[None],)
    wides = (full_ffin.reshape(1, 2 * HD, ff),)
    downs = (whole(ffn_out, 0)[None],)
    first, normed, normed_t, gains = first_project(me, tokens, ones, None, HD)
    second = second_project(me, normed, twos, None, HD)
    projected = (first, first, second, second)
    found = [attend_forward(projected[i], i % 2, mask_q, mask_k) for i in range(4)]
    attended = tuple(pair[0] for pair in found)
    active, sloped, inner, hidden, normed_two_t, grad_mixed, g_down = feed_in(
        me, tokens, attended, cotangent, valid, gains, twos, wides, (None,) * 3, HD, ff, (1, ff, HD)
    )
    grad_gate, grad_up, g_wide = feed_grad(
        me, active, sloped, grad_mixed, normed_two_t, downs, (None,) * 2, HD, (1, 2 * HD, ff)
    )
    mixed, grad_hidden, grad_att, gain_two = feed_out(
        me, inner, grad_gate, grad_up, hidden, grad_mixed, gains, twos, wides, downs, (None,) * 3, HD
    )
    grads = [
        attend_backward(projected[i], attended[i], grad_att, found[i][1], mask_k, i // 2, i % 2, 0, 2)
        for i in range(4)
    ]
    g_one = weight_grad(me, normed_t, grads[:2], None, HD, attended, grad_hidden)[0][0]
    g_two = weight_grad(me, normed_t, grads[2:], None, HD)[0][0]
    (through,) = input_gradient(me, grads[:2], ones, None, HD)
    input_grad, gain_one = input_gradient(me, grads[2:], twos, None, HD, (through, tokens, grad_hidden), gains)
    gain_sums = lax.psum(jnp.concatenate((gain_one, gain_two), axis=0), AXES)
    grad_out = g_one[:, HALF:].reshape(2, 2, 256, HD).transpose(1, 0, 2, 3).reshape(HD, HD)
    shares = (
        own(heads_back(g_one[:, :HALF], g_two), 1),
        own(grad_out, 0),
        own(g_wide[0].reshape(2, HD, ff), 1),
        own(g_down[0][0], 0),
    )
    return mixed, input_grad, shares, gain_sums


def solution(mesh):
    rows = P(("dp", "narrow"), None)
    cube = P(None, "dp", "narrow")
    flat = P("dp", "narrow")
    gain = P(None, ("dp", "narrow"))
    weights = (cube, flat, cube, flat, gain)
    in_specs = (rows, rows, P(("dp", "narrow")), rows, *weights, *weights, *weights)
    out_specs = (rows, rows, *(spec for spec in weights for _ in range(4)))
    step = functools.partial(local, mesh.shape["dp"], mesh.shape["narrow"])
    return jax.shard_map(step, mesh=mesh, in_specs=in_specs, out_specs=out_specs, check_vma=False)
```

time: 600 us -> 498 us (0.83)
  waiting for transfers between devices: 198 us -> 82.9 us
  Pallas kernels: 238 us -> 278 us
  blocking collectives: 39.9 us -> 0 us
  other arithmetic: 51.9 us -> 63.8 us
  starting transfers between devices: 51.4 us -> 43 us
  local copies, waits for them, and re-layouts: 10.5 us -> 17.2 us
    ppermute x48 -> x53, waiting for transfers between devices: 198 us -> 82.9 us  [swap(): return lax.ppermute(array, AXES, partners(kinds))]
    psum x1 -> x0, blocking collectives: 39.9 us -> none  [local(): gain_sums = lax.psum(jnp.concatenate((gain_one, gain_two), axis=0), AXES)]
    pallas_call x6 -> x18, Pallas kernels: 238 us -> 278 us  [the longest x5 65.6 us: attend_backward(): pl.pallas_call(attend_backward_kernel, grid=(count,), in_specs=tile_specs...]
    convert_element_type x18 -> x19, other arithmetic: 13.5 us -> 35.5 us  [the longest x16 34.4 us: add_low(): return total(*(part[low:high] for part in parts)).astype(BF)]
    another operation x17 -> x0, other arithmetic: 8.81 us -> none  [the longest x16 8.77 us: place_table(): return jnp.stack(rows).astype(jnp.int32)]
    ppermute x48 -> x53, starting transfers between devices: 51.4 us -> 43 us  [swap(): return lax.ppermute(array, AXES, partners(kinds))]
    unnamed x100 -> x115, local copies, waits for them, and re-layouts: 3.85 us -> 9.86 us
  transfers between devices with their start and end apart: 48 -> 53, of which waited for: 20 -> 22; matrix products, arithmetic and copies ran while one was open for 9% -> 10% of each run, Pallas kernels for 24% -> 57%
where the time goes in v2:
time: 498 us; the launch traced here: 488 us
  Pallas kernels  278 us (56%)
  waiting for transfers between devices  82.9 us (17%)
  other arithmetic  63.8 us (13%)
  starting transfers between devices  43 us (9%)
  local copies, waits for them, and re-layouts  17.2 us (3%)
    ppermute x53, waiting for transfers between devices, swap(): return lax.ppermute(array, AXES, partners(kinds))  82.9 us
    pallas_call x5, Pallas kernels, attend_backward(): pl.pallas_call(attend_backward_kernel, grid=(count,), in_specs=tile_specs...  65.6 us
    pallas_call x1, Pallas kernels, feed_in(): pl.pallas_call(functools.partial(feed_in_kernel, orders, rows_piece), gri...  43.6 us
    ppermute x53, starting transfers between devices, swap(): return lax.ppermute(array, AXES, partners(kinds))  43 us
    pallas_call x4, Pallas kernels, attend_forward(): pl.pallas_call(attend_forward_kernel, grid=(2,), in_specs=tile_specs(rows...  37.1 us
    convert_element_type x16, other arithmetic, add_low(): return total(*(part[low:high] for part in parts)).astype(BF)  34.4 us
    pallas_call x1, Pallas kernels, feed_out(): pl.pallas_call(functools.partial(feed_out_kernel, orders, rows_piece), gr...  34.4 us
    pallas_call x1, Pallas kernels, feed_grad(): pl.pallas_call(functools.partial(feed_grad_kernel, orders, rows_piece), g...  33 us
  transfers between devices with their start and end apart: 53, of which 22 were waited for; matrix products, arithmetic and copies ran while one was open for 10% of the time, Pallas kernels for 57%

profile of v2, /device:TPU:0, one launch (start us, length us, event | category | flops | bytes accessed | tf_op | source)
XLA Modules:
  0.0 488.2 jit_solution(10179255015358849083)
XLA Ops:
  1.7 3.0 collective-permute-start.1
  7.2 2.7 collective-permute-start
  10.1 4.3 collective-permute-done
  14.4 1.7 collective-permute-start.3
  18.8 2.0 select_add_fusion
  20.7 4.1 collective-permute-done.2
  26.0 3.1 fusion.7.valid_ref
  30.1 2.9 collective-permute-done.5
  35.8 8.2 %collective-permute-done.8 = bf16[2,64,1280]{2,1,0:T(8,128)(2,1)S(1)} collective-permute-done((bf16[2,64,1280]{2,1,0:T(8,128)(2,1)S(1)}, bf16[2,64,1280]{2,1,0:T(8,128)(2,1)S(1)}, u32[]{:S(2)}, u32[]{:S(2)}) %collective-permute-start.8) | collective-permute-done | bytes 327712 | tf_op jit(solution)/shard_map/ppermute | solution.py:70
  43.9 4.2 collective-permute-done.6.refs_1_
  49.1 1.6 collective-permute-done.9.refs_3_
  51.6 9.2 %first_project.1 = (bf16[1152,1536]{1,0:T(8,128)(2,1)}, bf16[1152,1024]{1,0:T(8,128)(2,1)}, bf16[1024,1152]{1,0:T(8,128)(2,1)}, f32[2,1024]{1,0:T(2,128)}) custom-call(s32[1]{0:T(128)} %bitcast.me_ref, bf16[1152,1024]{1,0:T(8,128)(2,1)} %refs_8_, bf16[8,80,768]{2,1,0:T(8,128)(2,1)} %copy-done.6, bf16[8,80,768]{2,1,0:T(8,128)(2,1)} %copy-done.11, ...), custom_call_target="tpu_custom_call" | custom-call | tf_op jit(solution)/shard_map/first_project/pallas_call | solution.py:167
  64.7 2.0 pad_maximum_fusion.3
  68.3 9.1 %attend_forward.4 = (bf16[1152,256]{1,0:T(8,128)(2,1)}, bf16[1152,256]{1,0:T(8,128)(2,1)}) custom-call(bf16[1152,1536]{1,0:T(8,128)(2,1)} %get-tuple-element.201.q_ref.k_ref.v_ref, bf16[1152,1536]{1,0:T(8,128)(2,1)} %get-tuple-element.201.q_ref.k_ref.v_ref, bf16[1152,1536]{1,0:T(8,128)(2,1)} %get-tuple-element.201.q_ref.k_ref.v_ref, ...), custom_call_target="tpu_custom_call" | custom-call | tf_op jit(solution)/shard_map/attend_forward/pallas_call | solution.py:293
  77.4 8.3 %collective-permute-done.14 = bf16[2,128,1408]{2,1,0:T(8,128)(2,1)} collective-permute-done((bf16[2,128,1408]{2,1,0:T(8,128)(2,1)}, bf16[2,128,1408]{2,1,0:T(8,128)(2,1)}, u32[]{:S(2)}, u32[]{:S(2)}) %collective-permute-start.14) | collective-permute-done | bytes 720928 | tf_op jit(solution)/shard_map/ppermute | solution.py:70
  85.7 3.5 pad_maximum_fusion
  89.2 1.9 collective-permute-start.16
  94.0 9.3 %attend_forward.5 = (bf16[1152,256]{1,0:T(8,128)(2,1)}, bf16[1152,256]{1,0:T(8,128)(2,1)}) custom-call(bf16[1152,1536]{1,0:T(8,128)(2,1)} %get-tuple-element.201.q_ref.k_ref.v_ref, bf16[1152,1536]{1,0:T(8,128)(2,1)} %get-tuple-element.201.q_ref.k_ref.v_ref, bf16[1152,1536]{1,0:T(8,128)(2,1)} %get-tuple-element.201.q_ref.k_ref.v_ref, ...), custom_call_target="tpu_custom_call" | custom-call | tf_op jit(solution)/shard_map/attend_forward/pallas_call | solution.py:293
  103.4 2.0 constant_dynamic-update-slice_fusion.3
  105.4 5.9 %collective-permute-done.17 = bf16[4,176,512]{2,1,0:T(8,128)(2,1)S(1)} collective-permute-done((bf16[4,176,512]{2,1,0:T(8,128)(2,1)}, bf16[4,176,512]{2,1,0:T(8,128)(2,1)S(1)}, u32[]{:S(2)}, u32[]{:S(2)}) %collective-permute-start.17) | collective-permute-done | bytes 720928 | tf_op jit(solution)/shard_map/ppermute | solution.py:70
  111.3 3.1 constant_dynamic-update-slice_fusion.2.refs_4_
  115.0 2.0 constant_dynamic-update-slice_fusion.7
  118.2 8.9 %second_project.1.q_ref.k_ref.v_ref = bf16[1152,1536]{1,0:T(8,128)(2,1)} custom-call(s32[1]{0:T(128)} %bitcast.me_ref, bf16[1152,1024]{1,0:T(8,128)(2,1)} %get-tuple-element.207.normed_ref, bf16[8,64,1280]{2,1,0:T(8,128)(2,1)} %copy-done, bf16[8,64,1280]{2,1,0:T(8,128)(2,1)} %copy-done.2, bf16[8,64,1280]{2,1,0:T(8,128)(2,1)} %copy-done.1, ...), custom_call_target="tpu_custom_call" | custom-call | tf_op jit(solution)/shard_map/second_project/pallas_call | solution.py:206
  127.1 9.1 %attend_forward.6 = (bf16[1152,256]{1,0:T(8,128)(2,1)}, bf16[1152,256]{1,0:T(8,128)(2,1)}) custom-call(bf16[1152,1536]{1,0:T(8,128)(2,1)} %second_project.1.q_ref.k_ref.v_ref, bf16[1152,1536]{1,0:T(8,128)(2,1)} %second_project.1.q_ref.k_ref.v_ref, bf16[1152,1536]{1,0:T(8,128)(2,1)} %second_project.1.q_ref.k_ref.v_ref, ...), custom_call_target="tpu_custom_call" | custom-call | tf_op jit(solution)/shard_map/attend_forward/pallas_call | solution.py:293
  136.7 9.6 %attend_forward.7 = (bf16[1152,256]{1,0:T(8,128)(2,1)}, bf16[1152,256]{1,0:T(8,128)(2,1)}) custom-call(bf16[1152,1536]{1,0:T(8,128)(2,1)} %second_project.1.q_ref.k_ref.v_ref, bf16[1152,1536]{1,0:T(8,128)(2,1)} %second_project.1.q_ref.k_ref.v_ref, bf16[1152,1536]{1,0:T(8,128)(2,1)} %second_project.1.q_ref.k_ref.v_ref, ...), custom_call_target="tpu_custom_call" | custom-call | tf_op jit(solution)/shard_map/attend_forward/pallas_call | solution.py:293
  146.2 6.4 %collective-permute-done.21.refs_1_.refs_9_ = bf16[8,176,512]{2,1,0:T(8,128)(2,1)} collective-permute-done((bf16[8,176,512]{2,1,0:T(8,128)(2,1)}, bf16[8,176,512]{2,1,0:T(8,128)(2,1)}, u32[]{:S(2)}, u32[]{:S(2)}) %collective-permute-start.21) | collective-permute-done | bytes 1441824 | tf_op jit(solution)/shard_map/ppermute | solution.py:70
  152.8 5.3 %collective-permute-done.22.refs_7_ = bf16[8,128,1408]{2,1,0:T(8,128)(2,1)S(1)} collective-permute-done((bf16[8,128,1408]{2,1,0:T(8,128)(2,1)S(1)}, bf16[8,128,1408]{2,1,0:T(8,128)(2,1)S(1)}, u32[]{:S(2)}, u32[]{:S(2)}) %collective-permute-start.22) | collective-permute-done | bytes 2883616 | tf_op jit(solution)/shard_map/ppermute | solution.py:70
  159.7 43.6 %feed_in.1 = (bf16[1152,2816]{1,0:T(8,128)(2,1)}, bf16[1152,2816]{1,0:T(8,128)(2,1)}, bf16[1152,2816]{1,0:T(8,128)(2,1)}, f32[1152,1024]{1,0:T(8,128)}, bf16[102...) custom-call(s32[1]{0:T(128)} %bitcast.me_ref, ...), custom_call_target="tpu_custom_call" | custom-call | tf_op jit(solution)/shard_map/feed_in/pallas_call | solution.py:589
  203.9 33.0 %feed_grad.1 = (bf16[1152,2816]{1,0:T(8,128)(2,1)}, bf16[1152,2816]{1,0:T(8,128)(2,1)}, bf16[8,128,1408]{2,1,0:T(8,128)(2,1)}, bf16[8,128,1408]{2,1,0:T(8,128)(2...) custom-call(s32[1]{0:T(128)} %bitcast.me_ref, bf16[1152,2816]{1,0:T(8,128)(2,1)} %get-tuple-element.228.active_ref, ...), custom_call_target="tpu_custom_call" | custom-call | tf_op jit(solution)/shard_map/feed_grad/pallas_call | solution.py:688
  237.5 2.9 add_convert_fusion.2
  240.7 34.4 %feed_out.1 = (bf16[1152,1024]{1,0:T(8,128)(2,1)}, f32[1152,1024]{1,0:T(8,128)}, bf16[1152,1024]{1,0:T(8,128)(2,1)}, f32[1,1024]{1,0:T(1,128)}) custom-call(s32[1]{0:T(128)} %bitcast.me_ref, bf16[1152,2816]{1,0:T(8,128)(2,1)} %get-tuple-element.227.inner_ref, bf16[1152,2816]{1,0:T(8,128)(2,1)} %get-tuple-element.247.grad_gate_ref, ...), custom_call_target="tpu_custom_call" | custom-call | tf_op jit(solution)/shard_map/feed_out/pallas_call | solution.py:755
  275.1 4.2 add_convert_fusion
  282.0 3.2 collective-permute-start.29
  285.2 15.8 %attend_backward.5.refs_1_.refs_4_ = bf16[1152,768]{1,0:T(8,128)(2,1)} custom-call(bf16[1152,1536]{1,0:T(8,128)(2,1)} %get-tuple-element.201.q_ref.k_ref.v_ref, bf16[1152,1536]{1,0:T(8,128)(2,1)} %get-tuple-element.201.q_ref.k_ref.v_ref, bf16[1152,1536]{1,0:T(8,128)(2,1)} %get-tuple-element.201.q_ref.k_ref.v_ref, ...), custom_call_target="tpu_custom_call" | custom-call | tf_op jit(solution)/shard_map/attend_backward/pallas_call | solution.py:367
  302.2 2.4 add_convert_fusion.10
  305.5 16.2 %attend_backward.6.refs_2_.refs_5_ = bf16[1152,768]{1,0:T(8,128)(2,1)} custom-call(bf16[1152,1536]{1,0:T(8,128)(2,1)} %get-tuple-element.201.q_ref.k_ref.v_ref, bf16[1152,1536]{1,0:T(8,128)(2,1)} %get-tuple-element.201.q_ref.k_ref.v_ref, bf16[1152,1536]{1,0:T(8,128)(2,1)} %get-tuple-element.201.q_ref.k_ref.v_ref, ...), custom_call_target="tpu_custom_call" | custom-call | tf_op jit(solution)/shard_map/attend_backward/pallas_call | solution.py:367
  321.7 3.5 add_convert_fusion.1
  325.3 1.9 add_convert_fusion.13
  327.2 2.0 collective-permute-start.33
  329.2 12.6 %weight_grad.2 = (bf16[8,64,1280]{2,1,0:T(8,128)(2,1)}, bf16[8,64,1280]{2,1,0:T(8,128)(2,1)}, bf16[8,64,1280]{2,1,0:T(8,128)(2,1)}, bf16[8,64,1280]{2,1,0:T(8,128)(2,1)}) custom-call(s32[1]{0:T(128)} %bitcast.me_ref, bf16[1024,1152]{1,0:T(8,128)(2,1)} %get-tuple-element.296.refs_0_, bf16[1152,768]{1,0:T(8,128)(2,1)} %attend_backward.5.refs_1_.refs_4_, ...), custom_call_target="tpu_custom_call" | custom-call | tf_op jit(solution)/shard_map/weight_grad/pallas_call | solution.py:862
  341.9 4.6 collective-permute-done.33
  347.0 9.1 %attend_backward.7.refs_1_.refs_4_ = bf16[1152,384]{1,0:T(8,128)(2,1)} custom-call(bf16[1152,1536]{1,0:T(8,128)(2,1)} %second_project.1.q_ref.k_ref.v_ref, bf16[1152,1536]{1,0:T(8,128)(2,1)} %second_project.1.q_ref.k_ref.v_ref, bf16[1152,1536]{1,0:T(8,128)(2,1)} %second_project.1.q_ref.k_ref.v_ref, ...), custom_call_target="tpu_custom_call" | custom-call | tf_op jit(solution)/shard_map/attend_backward/pallas_call | solution.py:367
  356.0 3.1 add_convert_fusion.3
  360.2 1.9 add_convert_fusion.5
  362.7 8.8 %attend_backward.8.refs_2_.refs_5_ = bf16[1152,384]{1,0:T(8,128)(2,1)} custom-call(bf16[1152,1536]{1,0:T(8,128)(2,1)} %second_project.1.q_ref.k_ref.v_ref, bf16[1152,1536]{1,0:T(8,128)(2,1)} %second_project.1.q_ref.k_ref.v_ref, bf16[1152,1536]{1,0:T(8,128)(2,1)} %second_project.1.q_ref.k_ref.v_ref, ...), custom_call_target="tpu_custom_call" | custom-call | tf_op jit(solution)/shard_map/attend_backward/pallas_call | solution.py:367
  371.6 8.8 %collective-permute-done.36 = bf16[2,128,1408]{2,1,0:T(8,128)(2,1)} collective-permute-done((bf16[2,128,1408]{2,1,0:T(8,128)(2,1)S(1)}, bf16[2,128,1408]{2,1,0:T(8,128)(2,1)}, u32[]{:S(2)}, u32[]{:S(2)}) %collective-permute-start.36) | collective-permute-done | bytes 720928 | tf_op jit(solution)/shard_map/ppermute | solution.py:70
  380.3 1.7 add_convert_fusion.7
  382.7 2.3 add_convert_fusion.9
  385.0 1.7 collective-permute-start.38
  386.7 15.8 %attend_backward.9.refs_3_.refs_6_ = bf16[1152,768]{1,0:T(8,128)(2,1)} custom-call(bf16[1152,1536]{1,0:T(8,128)(2,1)} %second_project.1.q_ref.k_ref.v_ref, bf16[1152,1536]{1,0:T(8,128)(2,1)} %second_project.1.q_ref.k_ref.v_ref, bf16[1152,1536]{1,0:T(8,128)(2,1)} %second_project.1.q_ref.k_ref.v_ref, ...), custom_call_target="tpu_custom_call" | custom-call | tf_op jit(solution)/shard_map/attend_backward/pallas_call | solution.py:367
  402.5 1.6 add_convert_fusion.11
  405.4 9.1 %weight_grad.3 = (bf16[8,64,768]{2,1,0:T(8,128)(2,1)}, bf16[8,64,768]{2,1,0:T(8,128)(2,1)}, bf16[8,64,768]{2,1,0:T(8,128)(2,1)}, bf16[8,64,768]{2,1,0:T(8,128)(2,1)}) custom-call(s32[1]{0:T(128)} %bitcast.me_ref, bf16[1024,1152]{1,0:T(8,128)(2,1)} %get-tuple-element.296.refs_0_, bf16[1152,384]{1,0:T(8,128)(2,1)} %attend_backward.7.refs_1_.refs_4_, ...), custom_call_target="tpu_custom_call" | custom-call | tf_op jit(solution)/shard_map/weight_grad/pallas_call | solution.py:862
  415.1 2.3 collective-permute-done.41
  418.3 2.2 add_convert_fusion.4
  424.1 9.4 %input_gradient.2.refs_7_ = f32[1152,1024]{1,0:T(8,128)} custom-call(s32[1]{0:T(128)} %bitcast.me_ref, bf16[8,80,768]{2,1,0:T(8,128)(2,1)} %copy-done.6, bf16[8,80,768]{2,1,0:T(8,128)(2,1)} %copy-done.11, bf16[8,80,768]{2,1,0:T(8,128)(2,1)} %copy-done.10, bf16[8,80,768]{2,1,0:T(8,128)(2,1)} %copy-done.12, bf16[1152,768]{1,0:T(8,128)(2,1)} %attend_backward.5.refs_1_.refs_4_, ...), custom_call_target="tpu_custom_call" | custom-call | tf_op jit(solution)/shard_map/input_gradient/pallas_call | solution.py:907
  434.2 2.0 add_convert_fusion.8
  437.3 2.5 multiply_subtract_fusion.2
  439.8 15.0 %input_gradient.3 = (f32[1152,1024]{1,0:T(8,128)}, f32[1,1024]{1,0:T(1,128)}) custom-call(s32[1]{0:T(128)} %bitcast.me_ref, bf16[8,64,1280]{2,1,0:T(8,128)(2,1)} %copy-done, bf16[8,64,1280]{2,1,0:T(8,128)(2,1)} %copy-done.2, bf16[8,64,1280]{2,1,0:T(8,128)(2,1)} %copy-done.1, bf16[8,64,1280]{2,1,0:T(8,128)(2,1)} %copy-done.3, ...), custom_call_target="tpu_custom_call" | custom-call | tf_op jit(solution)/shard_map/input_gradient/pallas_call | solution.py:907
  459.3 1.7 add_add_fusion
  461.0 3.5 collective-permute-done.46
  465.2 1.7 multiply_subtract_fusion
  468.2 1.8 collective-permute-start.50
  477.6 1.8 collective-permute-start.48
  480.0 4.2 collective-permute-done.48
  (245 shorter events, 59.5 us)
Async XLA Ops:
  1.7 12.6 %collective-permute-start.1 = (bf16[1,176,512]{2,1,0:T(8,128)(2,1)S(1)}, bf16[1,176,512]{2,1,0:T(8,128)(2,1)S(1)}, u32[]{:S(2)}, u32[]{:S(2)}) collective-permute-start(bf16[1,176,512]{2,1,0:T(8,128)(2,1)S(1)} %convert_bitcast_fusion), channel_id=1, source_target_pairs={{0,4},{1,5},{2,3},{3,2},{4,0},{5,1},{6,7},{7,6},{8,12},{9,13},{10,... | collective-permute-start | bytes 540680 | tf_op jit(solution)/shard_map/ppermute | solution.py:70
  7.2 7.2 %collective-permute-start = (bf16[1,80,768]{2,1,0:T(8,128)(2,1)S(1)}, bf16[1,80,768]{2,1,0:T(8,128)(2,1)S(1)}, u32[]{:S(2)}, u32[]{:S(2)}) collective-permute-start(bf16[1,80,768]{2,1,0:T(8,128)(2,1)S(1)} %fusion.13), channel_id=1, source_target_pairs={{0,16},{1,17},{2,10},{3,11},{4,20},{5,21},{6,14},{7,15},{8,24},{9,... | collective-permute-start | bytes 368648 | tf_op jit(solution)/shard_map/ppermute | solution.py:70
  10.0 41.4 %copy-start.7 = (bf16[2,64,1408]{2,1,0:T(8,128)(2,1)}, bf16[2,64,1408]{2,1,0:T(8,128)(2,1)S(1)}, u32[]{:S(2)}) copy-start(bf16[2,64,1408]{2,1,0:T(8,128)(2,1)S(1)} %convert_element_type.367) | copy-start | bytes 1081348
  14.4 10.4 %collective-permute-start.3 = (bf16[2,176,512]{2,1,0:T(8,128)(2,1)S(1)}, bf16[2,176,512]{2,1,0:T(8,128)(2,1)S(1)}, u32[]{:S(2)}, u32[]{:S(2)}) collective-permute-start(bf16[2,176,512]{2,1,0:T(8,128)(2,1)S(1)} %pad_maximum_fusion.6), channel_id=1, source_target_pairs={{0,1},{1,0},{2,6},{3,7},{4,5},{5,4},{6,2},{7,3},{8,9},{9,8},{10,14... | collective-permute-start | bytes 1081352 | tf_op jit(solution)/shard_map/ppermute | solution.py:70
  16.1 8.7 %collective-permute-start.2 = (bf16[2,80,768]{2,1,0:T(8,128)(2,1)S(1)}, bf16[2,80,768]{2,1,0:T(8,128)(2,1)S(1)}, u32[]{:S(2)}, u32[]{:S(2)}) collective-permute-start(bf16[2,80,768]{2,1,0:T(8,128)(2,1)S(1)} %pad_maximum_fusion.10), channel_id=1, source_target_pairs={{0,8},{1,9},{2,18},{3,19},{4,12},{5,13},{6,22},{7,23},{8,0},{9,1},... | collective-permute-start | bytes 737288 | tf_op jit(solution)/shard_map/ppermute | solution.py:70
  24.8 8.9 %collective-permute-start.4 = (bf16[4,80,768]{2,1,0:T(8,128)(2,1)S(1)}, bf16[4,80,768]{2,1,0:T(8,128)(2,1)S(1)}, u32[]{:S(2)}, u32[]{:S(2)}) collective-permute-start(bf16[4,80,768]{2,1,0:T(8,128)(2,1)S(1)} %pad_maximum_fusion.5), channel_id=1, source_target_pairs={{0,4},{1,5},{2,3},{3,2},{4,0},{5,1},{6,7},{7,6},{8,12},{9,13},{10,... | collective-permute-start | bytes 1474568 | tf_op jit(solution)/shard_map/ppermute | solution.py:70
  25.4 7.5 %collective-permute-start.5 = (bf16[1,64,1280]{2,1,0:T(8,128)(2,1)S(1)}, bf16[1,64,1280]{2,1,0:T(8,128)(2,1)S(1)}, u32[]{:S(2)}, u32[]{:S(2)}) collective-permute-start(bf16[1,64,1280]{2,1,0:T(8,128)(2,1)S(1)} %maximum_bitcast_fusion.1), channel_id=1, source_target_pairs={{0,16},{1,17},{2,10},{3,11},{4,20},{5,21},{6,14},{7,15},{8,24},{9,... | collective-permute-start | bytes 491528 | tf_op jit(solution)/shard_map/ppermute | solution.py:70
  33.8 15.2 %copy-start.6 = (bf16[8,80,768]{2,1,0:T(8,128)(2,1)}, bf16[8,80,768]{2,1,0:T(8,128)(2,1)S(1)}, u32[]{:S(2)}) copy-start(bf16[8,80,768]{2,1,0:T(8,128)(2,1)S(1)} %pad_maximum_fusion.1.refs_0_) | copy-start | bytes 2949124
  33.9 10.1 %collective-permute-start.7 = (bf16[8,80,768]{2,1,0:T(8,128)(2,1)S(1)}, bf16[8,80,768]{2,1,0:T(8,128)(2,1)S(1)}, u32[]{:S(2)}, u32[]{:S(2)}) collective-permute-start(bf16[8,80,768]{2,1,0:T(8,128)(2,1)S(1)} %pad_maximum_fusion.1.refs_0_), channel_id=1, source_target_pairs={{0,2},{1,3},{2,0},{3,1},{4,6},{5,7},{6,4},{7,5},{8,10},{9,11},{10,... | collective-permute-start | bytes 2949128 | tf_op jit(solution)/shard_map/ppermute | solution.py:70
  33.9 14.2 %collective-permute-start.6 = (bf16[8,80,768]{2,1,0:T(8,128)(2,1)S(1)}, bf16[8,80,768]{2,1,0:T(8,128)(2,1)S(1)}, u32[]{:S(2)}, u32[]{:S(2)}) collective-permute-start(bf16[8,80,768]{2,1,0:T(8,128)(2,1)S(1)} %pad_maximum_fusion.1.refs_0_), channel_id=1, source_target_pairs={{0,1},{1,0},{2,6},{3,7},{4,5},{5,4},{6,2},{7,3},{8,9},{9,8},{10,14... | collective-permute-start | bytes 2949128 | tf_op jit(solution)/shard_map/ppermute | solution.py:70
  34.1 9.8 %collective-permute-start.8 = (bf16[2,64,1280]{2,1,0:T(8,128)(2,1)S(1)}, bf16[2,64,1280]{2,1,0:T(8,128)(2,1)S(1)}, u32[]{:S(2)}, u32[]{:S(2)}) collective-permute-start(bf16[2,64,1280]{2,1,0:T(8,128)(2,1)S(1)} %pad_maximum_fusion.7), channel_id=1, source_target_pairs={{0,8},{1,9},{2,18},{3,19},{4,12},{5,13},{6,22},{7,23},{8,0},{9,1},... | collective-permute-start | bytes 983048 | tf_op jit(solution)/shard_map/ppermute | solution.py:70
  48.1 2.6 collective-permute-start.9
  50.7 12.5 %collective-permute-start.10 = (bf16[4,64,1280]{2,1,0:T(8,128)(2,1)}, bf16[4,64,1280]{2,1,0:T(8,128)(2,1)}, u32[]{:S(2)}, u32[]{:S(2)}) collective-permute-start(bf16[4,64,1280]{2,1,0:T(8,128)(2,1)} %pad_maximum_fusion.4), channel_id=1, source_target_pairs={{0,4},{1,5},{2,3},{3,2},{4,0},{5,1},{6,7},{7,6},{8,12},{9,13},{10,... | collective-permute-start | bytes 1966088 | tf_op jit(solution)/shard_map/ppermute | solution.py:70
  51.4 11.7 %collective-permute-start.11 = (bf16[1,128,1408]{2,1,0:T(8,128)(2,1)S(1)}, bf16[1,128,1408]{2,1,0:T(8,128)(2,1)S(1)}, u32[]{:S(2)}, u32[]{:S(2)}) collective-permute-start(bf16[1,128,1408]{2,1,0:T(8,128)(2,1)S(1)} %bitcast.23), channel_id=1, source_target_pairs={{0,16},{1,17},{2,10},{3,11},{4,20},{5,21},{6,14},{7,15},{8,24},{9,... | collective-permute-start | bytes 1081352 | tf_op jit(solution)/shard_map/ppermute | solution.py:70
  64.4 13.0 %copy-start = (bf16[8,64,1280]{2,1,0:T(8,128)(2,1)}, bf16[8,64,1280]{2,1,0:T(8,128)(2,1)S(1)}, u32[]{:S(2)}) copy-start(bf16[8,64,1280]{2,1,0:T(8,128)(2,1)S(1)} %constant_dynamic-update-slice_fusion.refs_0_) | copy-start | bytes 3932164
  64.4 21.2 %collective-permute-start.13 = (bf16[8,64,1280]{2,1,0:T(8,128)(2,1)S(1)}, bf16[8,64,1280]{2,1,0:T(8,128)(2,1)S(1)}, u32[]{:S(2)}, u32[]{:S(2)}) collective-permute-start(bf16[8,64,1280]{2,1,0:T(8,128)(2,1)S(1)} %constant_dynamic-update-slice_fusion.refs_0_), channel_id=1, source_target_pairs={{0,2},{1,3},{2,0},{3,1},{4,6},{5,7},{6,4},{7,5},{8,10},{9,11},{10,... | collective-permute-start | bytes 3932168 | tf_op jit(solution)/shard_map/ppermute | solution.py:70
  64.5 21.2 %collective-permute-start.12 = (bf16[8,64,1280]{2,1,0:T(8,128)(2,1)S(1)}, bf16[8,64,1280]{2,1,0:T(8,128)(2,1)S(1)}, u32[]{:S(2)}, u32[]{:S(2)}) collective-permute-start(bf16[8,64,1280]{2,1,0:T(8,128)(2,1)S(1)} %constant_dynamic-update-slice_fusion.refs_0_), channel_id=1, source_target_pairs={{0,1},{1,0},{2,6},{3,7},{4,5},{5,4},{6,2},{7,3},{8,9},{9,8},{10,14... | collective-permute-start | bytes 3932168 | tf_op jit(solution)/shard_map/ppermute | solution.py:70
  66.8 18.9 %collective-permute-start.14 = (bf16[2,128,1408]{2,1,0:T(8,128)(2,1)}, bf16[2,128,1408]{2,1,0:T(8,128)(2,1)}, u32[]{:S(2)}, u32[]{:S(2)}) collective-permute-start(bf16[2,128,1408]{2,1,0:T(8,128)(2,1)} %pad_maximum_fusion.3), channel_id=1, source_target_pairs={{0,8},{1,9},{2,18},{3,19},{4,12},{5,13},{6,22},{7,23},{8,0},{9,1},... | collective-permute-start | bytes 2162696 | tf_op jit(solution)/shard_map/ppermute | solution.py:70
  89.2 22.0 %collective-permute-start.16 = (bf16[4,128,1408]{2,1,0:T(8,128)(2,1)}, bf16[4,128,1408]{2,1,0:T(8,128)(2,1)}, u32[]{:S(2)}, u32[]{:S(2)}) collective-permute-start(bf16[4,128,1408]{2,1,0:T(8,128)(2,1)} %pad_maximum_fusion), channel_id=1, source_target_pairs={{0,4},{1,5},{2,3},{3,2},{4,0},{5,1},{6,7},{7,6},{8,12},{9,13},{10,... | collective-permute-start | bytes 4325384 | tf_op jit(solution)/shard_map/ppermute | solution.py:70
  91.1 20.1 %collective-permute-start.15 = (bf16[8,64,1280]{2,1,0:T(8,128)(2,1)S(1)}, bf16[8,64,1280]{2,1,0:T(8,128)(2,1)S(1)}, u32[]{:S(2)}, u32[]{:S(2)}) collective-permute-start(bf16[8,64,1280]{2,1,0:T(8,128)(2,1)S(1)} %collective-permute-done.12.refs_1_), channel_id=1, source_target_pairs={{0,2},{1,3},{2,0},{3,1},{4,6},{5,7},{6,4},{7,5},{8,10},{9,11},{10,... | collective-permute-start | bytes 3932168 | tf_op jit(solution)/shard_map/ppermute | solution.py:70
  91.1 20.1 %collective-permute-start.17 = (bf16[4,176,512]{2,1,0:T(8,128)(2,1)}, bf16[4,176,512]{2,1,0:T(8,128)(2,1)S(1)}, u32[]{:S(2)}, u32[]{:S(2)}) collective-permute-start(bf16[4,176,512]{2,1,0:T(8,128)(2,1)} %pad_maximum_fusion.2), channel_id=1, source_target_pairs={{0,16},{1,17},{2,10},{3,11},{4,20},{5,21},{6,14},{7,15},{8,24},{9,... | collective-permute-start | bytes 2162696 | tf_op jit(solution)/shard_map/ppermute | solution.py:70
  114.4 12.7 %collective-permute-start.18 = (bf16[8,128,1408]{2,1,0:T(8,128)(2,1)}, bf16[8,128,1408]{2,1,0:T(8,128)(2,1)}, u32[]{:S(2)}, u32[]{:S(2)}) collective-permute-start(bf16[8,128,1408]{2,1,0:T(8,128)(2,1)} %constant_dynamic-update-slice_fusion.2.refs_4_), channel_id=1, source_target_pairs={{0,2},{1,3},{2,0},{3,1},{4,6},{5,7},{6,4},{7,5},{8,10},{9,11},{10,... | collective-permute-start | bytes 8650760 | tf_op jit(solution)/shard_map/ppermute | solution.py:70
  114.4 38.3 %collective-permute-start.20 = (bf16[8,128,1408]{2,1,0:T(8,128)(2,1)}, bf16[8,128,1408]{2,1,0:T(8,128)(2,1)S(1)}, u32[]{:S(2)}, u32[]{:S(2)}) collective-permute-start(bf16[8,128,1408]{2,1,0:T(8,128)(2,1)} %constant_dynamic-update-slice_fusion.2.refs_4_), channel_id=1, source_target_pairs={{0,1},{1,0},{2,6},{3,7},{4,5},{5,4},{6,2},{7,3},{8,9},{9,8},{10,14... | collective-permute-start | bytes 8650760 | tf_op jit(solution)/shard_map/ppermute | solution.py:70
  117.9 34.8 %collective-permute-start.21 = (bf16[8,176,512]{2,1,0:T(8,128)(2,1)}, bf16[8,176,512]{2,1,0:T(8,128)(2,1)}, u32[]{:S(2)}, u32[]{:S(2)}) collective-permute-start(bf16[8,176,512]{2,1,0:T(8,128)(2,1)} %constant_dynamic-update-slice_fusion.6.refs_0_.refs_8_), channel_id=1, source_target_pairs={{0,8},{1,9},{2,18},{3,19},{4,12},{5,13},{6,22},{7,23},{8,0},{9,1},... | collective-permute-start | bytes 4325384 | tf_op jit(solution)/shard_map/ppermute | solution.py:70
  136.2 16.5 %collective-permute-start.19 = (bf16[8,176,512]{2,1,0:T(8,128)(2,1)}, bf16[8,176,512]{2,1,0:T(8,128)(2,1)}, u32[]{:S(2)}, u32[]{:S(2)}) collective-permute-start(bf16[8,176,512]{2,1,0:T(8,128)(2,1)} %constant_dynamic-update-slice_fusion.6.refs_0_.refs_8_), channel_id=1, source_target_pairs={{0,2},{1,3},{2,0},{3,1},{4,6},{5,7},{6,4},{7,5},{8,10},{9,11},{10,... | collective-permute-start | bytes 4325384 | tf_op jit(solution)/shard_map/ppermute | solution.py:70
  152.7 5.3 %collective-permute-start.22 = (bf16[8,128,1408]{2,1,0:T(8,128)(2,1)S(1)}, bf16[8,128,1408]{2,1,0:T(8,128)(2,1)S(1)}, u32[]{:S(2)}, u32[]{:S(2)}) collective-permute-start(bf16[8,128,1408]{2,1,0:T(8,128)(2,1)S(1)} %collective-permute-done.20.refs_5_), channel_id=1, source_target_pairs={{0,2},{1,3},{2,0},{3,1},{4,6},{5,7},{6,4},{7,5},{8,10},{9,11},{10,... | collective-permute-start | bytes 8650760 | tf_op jit(solution)/shard_map/ppermute | solution.py:70
  159.6 43.8 %collective-permute-start.23 = (bf16[8,176,512]{2,1,0:T(8,128)(2,1)}, bf16[8,176,512]{2,1,0:T(8,128)(2,1)}, u32[]{:S(2)}, u32[]{:S(2)}) collective-permute-start(bf16[8,176,512]{2,1,0:T(8,128)(2,1)} %collective-permute-done.21.refs_1_.refs_9_), channel_id=1, source_target_pairs={{0,2},{1,3},{2,0},{3,1},{4,6},{5,7},{6,4},{7,5},{8,10},{9,11},{10,... | collective-permute-start | bytes 4325384 | tf_op jit(solution)/shard_map/ppermute | solution.py:70
  203.4 33.6 %collective-permute-start.24 = (bf16[8,176,512]{2,1,0:T(8,128)(2,1)}, bf16[8,176,512]{2,1,0:T(8,128)(2,1)}, u32[]{:S(2)}, u32[]{:S(2)}) collective-permute-start(bf16[8,176,512]{2,1,0:T(8,128)(2,1)} %get-tuple-element.245), channel_id=1, source_target_pairs={{0,2},{1,3},{2,0},{3,1},{4,6},{5,7},{6,4},{7,5},{8,10},{9,11},{10,... | collective-permute-start | bytes 4325384 | tf_op jit(solution)/shard_map/ppermute | solution.py:70
  203.8 33.2 %collective-permute-start.25 = (bf16[8,176,512]{2,1,0:T(8,128)(2,1)}, bf16[8,176,512]{2,1,0:T(8,128)(2,1)S(1)}, u32[]{:S(2)}, u32[]{:S(2)}) collective-permute-start(bf16[8,176,512]{2,1,0:T(8,128)(2,1)} %get-tuple-element.246), channel_id=1, source_target_pairs={{0,2},{1,3},{2,0},{3,1},{4,6},{5,7},{6,4},{7,5},{8,10},{9,11},{10,... | collective-permute-start | bytes 4325384 | tf_op jit(solution)/shard_map/ppermute | solution.py:70
  203.9 33.6 %copy-start.26 = (bf16[8,176,512]{2,1,0:T(8,128)(2,1)S(1)}, bf16[8,176,512]{2,1,0:T(8,128)(2,1)}, u32[]{:S(2)}) copy-start(bf16[8,176,512]{2,1,0:T(8,128)(2,1)} %get-tuple-element.252) | copy-start | bytes 4325380
  237.0 38.1 %collective-permute-start.27 = (bf16[8,128,1408]{2,1,0:T(8,128)(2,1)}, bf16[8,128,1408]{2,1,0:T(8,128)(2,1)}, u32[]{:S(2)}, u32[]{:S(2)}) collective-permute-start(bf16[8,128,1408]{2,1,0:T(8,128)(2,1)} %get-tuple-element.254), channel_id=1, source_target_pairs={{0,2},{1,3},{2,0},{3,1},{4,6},{5,7},{6,4},{7,5},{8,10},{9,11},{10,... | collective-permute-start | bytes 8650760 | tf_op jit(solution)/shard_map/ppermute | solution.py:70
  237.3 37.8 %collective-permute-start.28 = (bf16[8,128,1408]{2,1,0:T(8,128)(2,1)}, bf16[8,128,1408]{2,1,0:T(8,128)(2,1)}, u32[]{:S(2)}, u32[]{:S(2)}) collective-permute-start(bf16[8,128,1408]{2,1,0:T(8,128)(2,1)} %get-tuple-element.255), channel_id=1, source_target_pairs={{0,2},{1,3},{2,0},{3,1},{4,6},{5,7},{6,4},{7,5},{8,10},{9,11},{10,... | collective-permute-start | bytes 8650760 | tf_op jit(solution)/shard_map/ppermute | solution.py:70
  240.4 34.7 %collective-permute-start.26 = (bf16[8,176,512]{2,1,0:T(8,128)(2,1)}, bf16[8,176,512]{2,1,0:T(8,128)(2,1)}, u32[]{:S(2)}, u32[]{:S(2)}) collective-permute-start(bf16[8,176,512]{2,1,0:T(8,128)(2,1)} %add_convert_fusion.2), channel_id=1, source_target_pairs={{0,8},{1,9},{2,18},{3,19},{4,12},{5,13},{6,22},{7,23},{8,0},{9,1},... | collective-permute-start | bytes 4325384 | tf_op jit(solution)/shard_map/ppermute | solution.py:70
  240.7 34.5 %copy-start.18 = (bf16[8,128,1408]{2,1,0:T(8,128)(2,1)S(1)}, bf16[8,128,1408]{2,1,0:T(8,128)(2,1)}, u32[]{:S(2)}) copy-start(bf16[8,128,1408]{2,1,0:T(8,128)(2,1)} %get-tuple-element.264) | copy-start | bytes 8650756
  279.4 42.3 %collective-permute-start.30 = (bf16[8,128,1408]{2,1,0:T(8,128)(2,1)}, bf16[8,128,1408]{2,1,0:T(8,128)(2,1)}, u32[]{:S(2)}, u32[]{:S(2)}) collective-permute-start(bf16[8,128,1408]{2,1,0:T(8,128)(2,1)} %add_convert_fusion), channel_id=1, source_target_pairs={{0,1},{1,0},{2,6},{3,7},{4,5},{5,4},{6,2},{7,3},{8,9},{9,8},{10,14... | collective-permute-start | bytes 8650760 | tf_op jit(solution)/shard_map/ppermute | solution.py:70
  282.0 20.2 %collective-permute-start.29 = (bf16[4,176,512]{2,1,0:T(8,128)(2,1)S(1)}, bf16[4,176,512]{2,1,0:T(8,128)(2,1)S(1)}, u32[]{:S(2)}, u32[]{:S(2)}) collective-permute-start(bf16[4,176,512]{2,1,0:T(8,128)(2,1)S(1)} %add_convert_fusion.6), channel_id=1, source_target_pairs={{0,16},{1,17},{2,10},{3,11},{4,20},{5,21},{6,14},{7,15},{8,24},{9,... | collective-permute-start | bytes 2162696 | tf_op jit(solution)/shard_map/ppermute | solution.py:70
  302.2 23.1 %copy-start.30 = (bf16[4,176,512]{2,1,0:T(8,128)(2,1)}, bf16[4,176,512]{2,1,0:T(8,128)(2,1)S(1)}, u32[]{:S(2)}) copy-start(bf16[4,176,512]{2,1,0:T(8,128)(2,1)S(1)} %collective-permute-done.29) | copy-start | bytes 2162692
  304.6 17.1 %collective-permute-start.31 = (bf16[2,176,512]{2,1,0:T(8,128)(2,1)}, bf16[2,176,512]{2,1,0:T(8,128)(2,1)S(1)}, u32[]{:S(2)}, u32[]{:S(2)}) collective-permute-start(bf16[2,176,512]{2,1,0:T(8,128)(2,1)} %add_convert_fusion.10), channel_id=1, source_target_pairs={{0,1},{1,0},{2,6},{3,7},{4,5},{5,4},{6,2},{7,3},{8,9},{9,8},{10,14... | collective-permute-start | bytes 1081352 | tf_op jit(solution)/shard_map/ppermute | solution.py:70
  305.5 16.2 %copy-start.19 = (bf16[8,128,1408]{2,1,0:T(8,128)(2,1)S(1)}, bf16[8,128,1408]{2,1,0:T(8,128)(2,1)}, u32[]{:S(2)}) copy-start(bf16[8,128,1408]{2,1,0:T(8,128)(2,1)} %get-tuple-element.275) | copy-start | bytes 8650756
  325.3 21.2 %collective-permute-start.32 = (bf16[4,128,1408]{2,1,0:T(8,128)(2,1)}, bf16[4,128,1408]{2,1,0:T(8,128)(2,1)}, u32[]{:S(2)}, u32[]{:S(2)}) collective-permute-start(bf16[4,128,1408]{2,1,0:T(8,128)(2,1)} %add_convert_fusion.1), channel_id=1, source_target_pairs={{0,4},{1,5},{2,3},{3,2},{4,0},{5,1},{6,7},{7,6},{8,12},{9,13},{10,... | collective-permute-start | bytes 4325384 | tf_op jit(solution)/shard_map/ppermute | solution.py:70
  327.2 19.3 %collective-permute-start.33 = (bf16[1,176,512]{2,1,0:T(8,128)(2,1)}, bf16[1,176,512]{2,1,0:T(8,128)(2,1)S(1)}, u32[]{:S(2)}, u32[]{:S(2)}) collective-permute-start(bf16[1,176,512]{2,1,0:T(8,128)(2,1)} %add_convert_fusion.13), channel_id=1, source_target_pairs={{0,4},{1,5},{2,3},{3,2},{4,0},{5,1},{6,7},{7,6},{8,12},{9,13},{10,... | collective-permute-start | bytes 540680 | tf_op jit(solution)/shard_map/ppermute | solution.py:70
  346.4 9.6 %copy-start.44 = (bf16[1,176,512]{2,1,0:T(8,128)(2,1)}, bf16[1,176,512]{2,1,0:T(8,128)(2,1)S(1)}, u32[]{:S(2)}) copy-start(bf16[1,176,512]{2,1,0:T(8,128)(2,1)S(1)} %collective-permute-done.33) | copy-start | bytes 540676
  346.4 9.6 %collective-permute-start.34 = (bf16[8,64,1280]{2,1,0:T(8,128)(2,1)}, bf16[8,64,1280]{2,1,0:T(8,128)(2,1)}, u32[]{:S(2)}, u32[]{:S(2)}) collective-permute-start(bf16[8,64,1280]{2,1,0:T(8,128)(2,1)} %get-tuple-element.281), channel_id=1, source_target_pairs={{0,2},{1,3},{2,0},{3,1},{4,6},{5,7},{6,4},{7,5},{8,10},{9,11},{10,... | collective-permute-start | bytes 3932168 | tf_op jit(solution)/shard_map/ppermute | solution.py:70
  346.4 9.6 %collective-permute-start.35 = (bf16[8,64,1280]{2,1,0:T(8,128)(2,1)}, bf16[8,64,1280]{2,1,0:T(8,128)(2,1)}, u32[]{:S(2)}, u32[]{:S(2)}) collective-permute-start(bf16[8,64,1280]{2,1,0:T(8,128)(2,1)} %get-tuple-element.282), channel_id=1, source_target_pairs={{0,2},{1,3},{2,0},{3,1},{4,6},{5,7},{6,4},{7,5},{8,10},{9,11},{10,... | collective-permute-start | bytes 3932168 | tf_op jit(solution)/shard_map/ppermute | solution.py:70
  359.1 21.2 %collective-permute-start.37 = (bf16[8,64,1280]{2,1,0:T(8,128)(2,1)}, bf16[8,64,1280]{2,1,0:T(8,128)(2,1)}, u32[]{:S(2)}, u32[]{:S(2)}) collective-permute-start(bf16[8,64,1280]{2,1,0:T(8,128)(2,1)} %add_convert_fusion.3), channel_id=1, source_target_pairs={{0,1},{1,0},{2,6},{3,7},{4,5},{5,4},{6,2},{7,3},{8,9},{9,8},{10,14... | collective-permute-start | bytes 3932168 | tf_op jit(solution)/shard_map/ppermute | solution.py:70
  362.1 18.2 %collective-permute-start.36 = (bf16[2,128,1408]{2,1,0:T(8,128)(2,1)S(1)}, bf16[2,128,1408]{2,1,0:T(8,128)(2,1)}, u32[]{:S(2)}, u32[]{:S(2)}) collective-permute-start(bf16[2,128,1408]{2,1,0:T(8,128)(2,1)S(1)} %add_convert_fusion.5), channel_id=1, source_target_pairs={{0,8},{1,9},{2,18},{3,19},{4,12},{5,13},{6,22},{7,23},{8,0},{9,1},... | collective-permute-start | bytes 2162696 | tf_op jit(solution)/shard_map/ppermute | solution.py:70
  382.0 20.4 %collective-permute-start.39 = (bf16[4,64,1280]{2,1,0:T(8,128)(2,1)S(1)}, bf16[4,64,1280]{2,1,0:T(8,128)(2,1)}, u32[]{:S(2)}, u32[]{:S(2)}) collective-permute-start(bf16[4,64,1280]{2,1,0:T(8,128)(2,1)S(1)} %add_convert_fusion.7), channel_id=1, source_target_pairs={{0,4},{1,5},{2,3},{3,2},{4,0},{5,1},{6,7},{7,6},{8,12},{9,13},{10,... | collective-permute-start | bytes 1966088 | tf_op jit(solution)/shard_map/ppermute | solution.py:70
  385.0 17.5 %collective-permute-start.38 = (bf16[1,128,1408]{2,1,0:T(8,128)(2,1)}, bf16[1,128,1408]{2,1,0:T(8,128)(2,1)S(1)}, u32[]{:S(2)}, u32[]{:S(2)}) collective-permute-start(bf16[1,128,1408]{2,1,0:T(8,128)(2,1)} %add_convert_fusion.9), channel_id=1, source_target_pairs={{0,16},{1,17},{2,10},{3,11},{4,20},{5,21},{6,14},{7,15},{8,24},{9,... | collective-permute-start | bytes 1081352 | tf_op jit(solution)/shard_map/ppermute | solution.py:70
  402.5 12.0 %copy-start.39 = (bf16[1,128,1408]{2,1,0:T(8,128)(2,1)}, bf16[1,128,1408]{2,1,0:T(8,128)(2,1)S(1)}, u32[]{:S(2)}) copy-start(bf16[1,128,1408]{2,1,0:T(8,128)(2,1)S(1)} %collective-permute-done.38) | copy-start | bytes 1081348
  404.0 10.4 %collective-permute-start.40 = (bf16[2,64,1280]{2,1,0:T(8,128)(2,1)S(1)}, bf16[2,64,1280]{2,1,0:T(8,128)(2,1)S(1)}, u32[]{:S(2)}, u32[]{:S(2)}) collective-permute-start(bf16[2,64,1280]{2,1,0:T(8,128)(2,1)S(1)} %add_convert_fusion.11), channel_id=1, source_target_pairs={{0,8},{1,9},{2,18},{3,19},{4,12},{5,13},{6,22},{7,23},{8,0},{9,1},... | collective-permute-start | bytes 983048 | tf_op jit(solution)/shard_map/ppermute | solution.py:70
  414.5 2.9 collective-permute-start.41
  414.6 3.7 collective-permute-start.42
  420.5 13.1 %collective-permute-start.43 = (bf16[8,64,768]{2,1,0:T(8,128)(2,1)}, bf16[8,64,768]{2,1,0:T(8,128)(2,1)}, u32[]{:S(2)}, u32[]{:S(2)}) collective-permute-start(bf16[8,64,768]{2,1,0:T(8,128)(2,1)} %add_convert_fusion.4), channel_id=1, source_target_pairs={{0,1},{1,0},{2,6},{3,7},{4,5},{5,4},{6,2},{7,3},{8,9},{9,8},{10,14... | collective-permute-start | bytes 2359304 | tf_op jit(solution)/shard_map/ppermute | solution.py:70
  422.8 11.5 %copy-start.27 = (bf16[8,64,768]{2,1,0:T(8,128)(2,1)S(1)}, bf16[8,64,768]{2,1,0:T(8,128)(2,1)}, u32[]{:S(2)}) copy-start(bf16[8,64,768]{2,1,0:T(8,128)(2,1)} %get-tuple-element.311) | copy-start | bytes 2359300
  422.8 10.8 %collective-permute-start.44 = (bf16[1,64,1280]{2,1,0:T(8,128)(2,1)S(1)}, bf16[1,64,1280]{2,1,0:T(8,128)(2,1)S(1)}, u32[]{:S(2)}, u32[]{:S(2)}) collective-permute-start(bf16[1,64,1280]{2,1,0:T(8,128)(2,1)S(1)} %add_convert_fusion.14), channel_id=1, source_target_pairs={{0,16},{1,17},{2,10},{3,11},{4,20},{5,21},{6,14},{7,15},{8,24},{9,... | collective-permute-start | bytes 491528 | tf_op jit(solution)/shard_map/ppermute | solution.py:70
  436.2 18.6 %collective-permute-start.45 = (bf16[4,64,768]{2,1,0:T(8,128)(2,1)}, bf16[4,64,768]{2,1,0:T(8,128)(2,1)S(1)}, u32[]{:S(2)}, u32[]{:S(2)}) collective-permute-start(bf16[4,64,768]{2,1,0:T(8,128)(2,1)} %add_convert_fusion.8), channel_id=1, source_target_pairs={{0,4},{1,5},{2,3},{3,2},{4,0},{5,1},{6,7},{7,6},{8,12},{9,13},{10,... | collective-permute-start | bytes 1179656 | tf_op jit(solution)/shard_map/ppermute | solution.py:70
  439.8 15.0 %copy-start.49 = (f32[1,1024]{1,0:T(1,128)S(1)}, f32[1,1024]{1,0:T(1,128)}, u32[]{:S(2)}) copy-start(f32[1,1024]{1,0:T(1,128)} %get-tuple-element.317) | copy-start | bytes 12292
  455.6 5.4 %collective-permute-start.47 = (f32[2,1024]{1,0:T(2,128)S(1)}, f32[2,1024]{1,0:T(2,128)S(1)}, u32[]{:S(2)}, u32[]{:S(2)}) collective-permute-start(f32[2,1024]{1,0:T(2,128)S(1)} %pad_maximum_fusion.11), channel_id=1, source_target_pairs={{0,4},{1,5},{2,3},{3,2},{4,0},{5,1},{6,7},{7,6},{8,12},{9,13},{10,... | collective-permute-start | bytes 24584 | tf_op jit(solution)/shard_map/ppermute | solution.py:70
  457.8 6.7 %collective-permute-start.46 = (bf16[2,64,768]{2,1,0:T(8,128)(2,1)S(1)}, bf16[2,64,768]{2,1,0:T(8,128)(2,1)S(1)}, u32[]{:S(2)}, u32[]{:S(2)}) collective-permute-start(bf16[2,64,768]{2,1,0:T(8,128)(2,1)S(1)} %add_convert_fusion.12), channel_id=1, source_target_pairs={{0,8},{1,9},{2,18},{3,19},{4,12},{5,13},{6,22},{7,23},{8,0},{9,1},... | collective-permute-start | bytes 589832 | tf_op jit(solution)/shard_map/ppermute | solution.py:70
  464.5 3.7 collective-permute-start.49
  468.2 4.6 collective-permute-start.50
  472.9 3.7 collective-permute-start.51
  476.5 2.8 collective-permute-start.52
  477.6 6.6 %collective-permute-start.48 = (bf16[1,64,768]{2,1,0:T(8,128)(2,1)S(1)}, bf16[1,64,768]{2,1,0:T(8,128)(2,1)S(1)}, u32[]{:S(2)}, u32[]{:S(2)}) collective-permute-start(bf16[1,64,768]{2,1,0:T(8,128)(2,1)S(1)} %add_convert_fusion.15), channel_id=1, source_target_pairs={{0,16},{1,17},{2,10},{3,11},{4,20},{5,21},{6,14},{7,15},{8,24},{9,... | collective-permute-start | bytes 294920 | tf_op jit(solution)/shard_map/ppermute | solution.py:70
  (44 other events, 218.1 us)

commit v3 on v2

--- a/solution.py
+++ b/solution.py
@@ -37,6 +37,9 @@
 HALF = 2 * PART
 FF_BLOCK = 256
 QUERY_BLOCK = 384
+N_GROUPS = 4
+GATHERED = 8
+SCATTERED = 4
 ROW_PARTS = (slice(0, 512), slice(512, LONG))
 
 
@@ -59,7 +62,7 @@
 
 BY_Z = (("z2", "z1"), ("z1", "z2"), ("x", "y"), ("y", "x"), ("core", "core"))
 BY_PLANE = (("x", "y"), ("y", "x"), ("z2", "z1"), ("z1", "z2"), ("core", "core"))
-BIT = {"y": 1, "core": 2, "x": 4, "z1": 8, "z2": 16}
+BIT = {"y": 1, "core": 2, "x": 4, "xy": 5, "z1": 8, "z2": 16}
 
 
 def partners(kinds):
@@ -102,9 +105,10 @@
         body(arrays[0].at[0], 0, 0)
         return
     me = me_ref[0]
+    slots = 32 // len(arrays)
     for index in range(32):
         dp, narrow = owner_of(me, index, order)
-        body(arrays[index // 8].at[index % 8], dp, narrow)
+        body(arrays[index // slots].at[index % slots], dp, narrow)
 
 
 def span(start, size, unit):
@@ -131,14 +135,14 @@
 
 
 def first_project_kernel(order, rows_piece, me_ref, x_ref, *refs):
-    n_arrays = 4 if order else 1
+    n_arrays = GATHERED if order else 1
     arrays = refs[:n_arrays]
     out_ref, normed_ref, normed_t_ref, gains_ref, weight, gain_parts, sem, gain_sem = refs[n_arrays:]
     step = pl.program_id(0)
 
     @pl.when(step == 0)
     def _():
-        slots = 8 if order else 1
+        slots = 32 // GATHERED if order else 1
         for index in range(n_arrays):
             pltpu.make_async_copy(
                 arrays[index].at[:, pl.ds(rows_piece, ROWS_GAIN), pl.ds(0, GAIN_COLS)],
@@ -187,7 +191,7 @@
 
 
 def second_project_kernel(order, rows_piece, me_ref, normed_ref, *refs):
-    n_arrays = 4 if order else 1
+    n_arrays = GATHERED if order else 1
     arrays = refs[:n_arrays]
     out_ref, weight, sem = refs[n_arrays:]
     step = pl.program_id(0)
@@ -398,43 +402,38 @@
     each_place(me_ref, arrays, order, start)
 
 
-def load_wide(me_ref, arrays, order, rows_piece, targets, sems):
-    cols = targets[0].shape[1] // (2 if order else 1)
-
-    def start(source, dp, narrow):
+def load_wide(me_ref, arrays, orders, targets, sems):
+    count = len(arrays) // 2
+    for index, target in enumerate(targets):
+        order = orders and orders[index]
+        cols = target.shape[1] // (2 if order else 1)
+
+        def start(source, dp, narrow, index=index, target=target, cols=cols):
+            rows = source.shape[0]
+            pltpu.make_async_copy(
+                source, target.at[span(dp, rows, 16), span(narrow, cols, 128)], sems[index]
+            ).start()
+
+        each_place(me_ref, arrays[index * count : (index + 1) * count], order, start)
+
+
+def load_wide_by_half(me_ref, arrays, orders, targets, sems):
+    whole = targets[0].shape[1]
+    count = len(arrays) // 2
+    for half in range(2):
+        cols = pl.ds(half * (whole // 2), whole // 2)
         for index, target in enumerate(targets):
-            pltpu.make_async_copy(
-                source.at[pl.ds(index * rows_piece, rows_piece)],
-                target.at[span(dp, rows_piece, 16), span(narrow, cols, 128)],
-                sems[index],
-            ).start()
-
-    each_place(me_ref, arrays, order, start)
-
-
-def load_wide_by_half(me_ref, arrays, order, rows_piece, targets, sems):
-    whole = targets[0].shape[1]
-    if order is None:
-        for index, target in enumerate(targets):
-            for half in range(2):
-                cols = pl.ds(half * (whole // 2), whole // 2)
-                pltpu.make_async_copy(
-                    arrays[0].at[0, pl.ds(index * rows_piece, rows_piece), cols], target.at[:, cols], sems.at[index, half]
-                ).start()
-        return
-    for half in range(2):
-
-        def start(source, dp, narrow, half=half):
-            @pl.when(narrow == half)
-            def _():
-                for index, target in enumerate(targets):
-                    pltpu.make_async_copy(
-                        source.at[pl.ds(index * rows_piece, rows_piece)],
-                        target.at[span(dp, rows_piece, 16), pl.ds(half * (whole // 2), whole // 2)],
-                        sems.at[index, half],
-                    ).start()
-
-        each_place(me_ref, arrays, order, start)
+            if orders is None:
+                pltpu.make_async_copy(arrays[index].at[0, :, cols], target.at[:, cols], sems.at[index, half]).start()
+                continue
+
+            def start(source, dp, narrow, half=half, index=index, target=target, cols=cols):
+                copy = pltpu.make_async_copy(
+                    source, target.at[span(dp, source.shape[0], 16), cols], sems.at[index, half]
+                )
+                pl.when(narrow == half)(copy.start)
+
+            each_place(me_ref, arrays[index * count : (index + 1) * count], orders[index], start)
 
 
 def wait_half(targets, sems, half):
@@ -451,9 +450,6 @@
         pltpu.make_async_copy(source, w_down.at[span(dp, rows, 16), span(narrow, cols, 128)], sem).start()
 
     each_place(me_ref, arrays, order, start)
-
-
-N_GROUPS = 4
 
 
 def load_down_by_group(me_ref, arrays, order, w_down, sems):
@@ -502,10 +498,11 @@
 
 
 def feed_in_kernel(orders, rows_piece, me_ref, x_ref, att_a, att_b, att_c, att_d, cotangent_ref, valid_ref, gains_ref, *refs):
-    square_order, wide_order, down_order = orders
-    n_arrays = 4 if wide_order else 1
-    square, wide = (refs[i * n_arrays : (i + 1) * n_arrays] for i in range(2))
-    refs = refs[2 * n_arrays :]
+    square_order, wide_orders, _, _, down_order = orders
+    n_arrays = GATHERED if down_order else 1
+    square, wide = refs[:n_arrays], refs[n_arrays : 3 * n_arrays]
+    refs = refs[3 * n_arrays :]
+    n_arrays = SCATTERED if down_order else 1
     active_ref, sloped_ref, inner_ref, hidden_out, normed_t_out, grad_mixed_out = refs[:6]
     grad_down = refs[6 : 6 + n_arrays]
     w_out, w_gate, w_up, w_down, hidden, normed, normed_t, grad_mixed, sem, wide_sems, out_sems, down_sems = refs[6 + n_arrays :]
@@ -514,7 +511,7 @@
     @pl.when(step == 0)
     def _():
         load_out(me_ref, square, square_order, rows_piece, w_out, sem)
-        load_wide_by_half(me_ref, wide, wide_order, rows_piece, (w_gate, w_up), wide_sems)
+        load_wide_by_half(me_ref, wide, wide_orders, (w_gate, w_up), wide_sems)
         gain = gains_ref[1:2]
         all_of(w_out, sem)
 
@@ -585,14 +582,15 @@
 def feed_in(me, tokens, attended, cotangent, valid, gains, square, wide, orders, rows_piece, ff, down_shape):
     rows = tokens.shape[0]
     n_arrays = len(square)
+    n_grads = SCATTERED if orders[2] else 1
     tile = pl.BlockSpec((rows, FF_BLOCK), lambda step: (0, step))
     outs = pl.pallas_call(
         functools.partial(feed_in_kernel, orders, rows_piece),
         grid=(ff // FF_BLOCK,),
         in_specs=[IN_SMEM]
         + [one_buffer(array.shape) for array in (tokens, *attended, cotangent, valid, gains)]
-        + [IN_HBM] * (2 * n_arrays),
-        out_specs=[tile] * 3 + [IN_HBM] * (3 + n_arrays),
+        + [IN_HBM] * (3 * n_arrays),
+        out_specs=[tile] * 3 + [IN_HBM] * (3 + n_grads),
         out_shape=[
             shape((rows, ff), BF),
             shape((rows, ff), BF),
@@ -601,7 +599,7 @@
             shape((HD, rows), BF),
             shape((rows, HD), BF),
         ]
-        + [shape(down_shape, BF)] * n_arrays,
+        + [shape(down_shape, BF)] * n_grads,
         scratch_shapes=[
             pltpu.VMEM((HD, HD), BF),
             pltpu.VMEM((HD, ff), BF),
@@ -623,12 +621,12 @@
 
 
 def feed_grad_kernel(orders, rows_piece, me_ref, active_ref, sloped_ref, grad_mixed_ref, normed_t_ref, *refs):
-    wide_order, down_order = orders
-    n_arrays = 4 if wide_order else 1
+    _, _, down_order, wide_order, _ = orders
+    n_arrays = GATHERED if wide_order else 1
     down = refs[:n_arrays]
     grad_gate_ref, grad_up_ref = refs[n_arrays : n_arrays + 2]
-    grad_wide = refs[n_arrays + 2 : 2 * n_arrays + 2]
-    w_down, w_gate, w_up, down_sems, out_sems = refs[2 * n_arrays + 2 :]
+    grad_wide = refs[n_arrays + 2 : -5]
+    w_down, w_gate, w_up, down_sems, out_sems = refs[-5:]
     step = pl.program_id(0)
 
     @pl.when(step == 0)
@@ -684,13 +682,14 @@
 def feed_grad(me, active, sloped, grad_mixed, normed_t, down, orders, rows_piece, wide_shape):
     rows, ff = active.shape
     n_arrays = len(down)
+    n_grads = SCATTERED if orders[2] else 1
     tile = pl.BlockSpec((rows, FF_BLOCK), lambda step: (0, step))
     outs = pl.pallas_call(
         functools.partial(feed_grad_kernel, orders, rows_piece),
         grid=(ff // FF_BLOCK,),
         in_specs=[IN_SMEM, tile, tile, one_buffer((rows, HD)), one_buffer((HD, rows))] + [IN_HBM] * n_arrays,
-        out_specs=[tile, tile] + [IN_HBM] * n_arrays,
-        out_shape=[shape((rows, ff), BF)] * 2 + [shape(wide_shape, BF)] * n_arrays,
+        out_specs=[tile, tile] + [IN_HBM] * n_grads,
+        out_shape=[shape((rows, ff), BF)] * 2 + [shape(wide_shape, BF)] * n_grads,
         scratch_shapes=[
             pltpu.VMEM((ff, HD), BF),
             pltpu.VMEM((HD, ff), BF),
@@ -705,17 +704,17 @@
 
 
 def feed_out_kernel(orders, rows_piece, me_ref, inner_ref, grad_gate_ref, grad_up_ref, hidden_ref, grad_mixed_ref, gains_ref, *refs):
-    square_order, wide_order, down_order = orders
-    n_arrays = 4 if wide_order else 1
-    square, wide, down = (refs[i * n_arrays : (i + 1) * n_arrays] for i in range(3))
-    mixed_ref, grad_hidden_ref, grad_attended_ref, gain_grad_ref = refs[3 * n_arrays : 3 * n_arrays + 4]
-    w_out, w_gate, w_up, w_down, sems = refs[3 * n_arrays + 4 :]
+    square_order, wide_orders, down_order, _, _ = orders
+    n_arrays = GATHERED if down_order else 1
+    square, wide, down = refs[:n_arrays], refs[n_arrays : 3 * n_arrays], refs[3 * n_arrays : 4 * n_arrays]
+    mixed_ref, grad_hidden_ref, grad_attended_ref, gain_grad_ref = refs[4 * n_arrays : 4 * n_arrays + 4]
+    w_out, w_gate, w_up, w_down, sems = refs[4 * n_arrays + 4 :]
     step = pl.program_id(0)
 
     @pl.when(step == 0)
     def _():
         load_down(me_ref, down, down_order, w_down, sems.at[3])
-        load_wide(me_ref, wide, wide_order, rows_piece, (w_gate, w_up), (sems.at[1], sems.at[2]))
+        load_wide(me_ref, wide, wide_orders, (w_gate, w_up), (sems.at[1], sems.at[2]))
         load_out(me_ref, square, square_order, rows_piece, w_out, sems.at[0])
         gain_grad_ref[...] = jnp.zeros_like(gain_grad_ref)
         all_of(w_down, sems.at[3])
@@ -756,7 +755,7 @@
         functools.partial(feed_out_kernel, orders, rows_piece),
         grid=(2 * count,),
         in_specs=[IN_SMEM, early(ff), late(ff), late(ff), both, late(HD), one_buffer((2, HD))]
-        + [IN_HBM] * (3 * n_arrays),
+        + [IN_HBM] * (4 * n_arrays),
         out_specs=[early(HD), late(HD), late(HD), pl.BlockSpec((1, HD), lambda step: (0, 0))],
         out_shape=[shape((rows, HD), BF), shape((rows, HD), F32), shape((rows, HD), BF), shape((1, HD), F32)],
         scratch_shapes=[
@@ -871,7 +870,7 @@
 
 
 def input_grad_kernel(order, rows_piece, n_grads, last, me_ref, *refs):
-    n_arrays = 4 if order else 1
+    n_arrays = GATHERED if order else 1
     n_in = n_grads + (3 if last else 0)
     arrays, sources = refs[:n_arrays], refs[n_arrays : n_arrays + n_in]
     refs = refs[n_arrays + n_in :]
@@ -981,121 +980,147 @@
     low_qkv = attn_qkv.astype(BF).reshape(3, row_d, 2, 2, 128).transpose(2, 1, 3, 0, 4).reshape(2, row_d, PART)
     one = joined(low_qkv[0], gain_block(low_gains, PART))[None]
     two = jnp.concatenate((low_qkv[1], attn_out.astype(BF)), axis=1)[None]
-    wide = ffn_in.astype(BF).reshape(1, 2 * row_d, col_f)
+    gate = ffn_in[0].astype(BF)[None]
+    up = ffn_in[1].astype(BF)[None]
     down = ffn_out.astype(BF)[None]
     z_a, z_b, z_c, z_d, core = BY_Z
     p_a, p_b, p_c, p_d, _ = BY_PLANE
 
-    one_in, down_in, two, wide = tie(swap(one, z_a), swap(down, p_a), two, wide)
-    one, down = joined(one, one_in), joined(down, down_in)
-    one_in, down_in, two, wide = tie(swap(one, z_b), swap(down, p_b), two, wide)
-    one, down = joined(one, one_in), joined(down, down_in)
-    one_in, two_in, down, wide, valid = tie(swap(one, z_c), swap(two, z_a), down, wide, valid)
-    one, two = joined(one, one_in), joined(two, two_in)
-    one_more, one_away, two_in, wide, down, mask_q, mask_k = tie(
-        swap(one, z_d), swap(one, core), swap(two, z_b), wide, down, mask_q, mask_k
-    )
-    one_last = swap(one_more, core)
+    one_in, gate_in, two, up = tie(swap(one, z_a), swap(gate, p_a), two, up)
+    one, gate = joined(one, one_in), joined(gate, gate_in)
+    one_in, gate_in, two, up = tie(swap(one, z_b), swap(gate, p_b), two, up)
+    one, gate = joined(one, one_in), joined(gate, gate_in)
+    one_c, one_d, one_x, two_in, gate, up, valid = tie(
+        swap(one, z_c), swap(one, z_d), swap(one, core), swap(two, z_a), gate, up, valid
+    )
     two = joined(two, two_in)
-    one_last, two, cotangent = tie(one_last, two, cotangent)
-    two_in = swap(two, z_c)
-    wide_in = swap(wide, z_a)
-    ones = (one, one_more, one_away, one_last)
+    two_in = swap(two, z_b)
+    one_cd, one_cx, one_dx, up, gate, mask_q, mask_k = tie(
+        swap(one_c, z_d), swap(one_c, core), swap(one_d, core), up, gate, mask_q, mask_k
+    )
+    one_cdx, two_in, up, gate, cotangent = tie(swap(one_cd, core), two_in, up, gate, cotangent)
+    two = joined(two, two_in)
+    ones = (one, one_c, one_d, one_cd, one_x, one_cx, one_dx, one_cdx)
+    two_c = swap(two, z_c)
+    up_in = swap(up, z_a)
+    two_x = swap(two, core)
+    gate_x = swap(gate, core)
     first, normed, normed_t, gains = first_project(me, tokens, ones, BY_Z, row_d)
-    first, two_in, wide_in, down = tie(first, two_in, wide_in, down)
-    two = joined(two, two_in)
-    wide = joined(wide, wide_in)
-    two_more = swap(two, z_d)
-    wide_in = swap(wide, z_b)
-    two_away = swap(two, core)
+    first, two, two_c, two_x, gate_x, up_in, gate = tie(first, two, two_c, two_x, gate_x, up_in, gate)
+    up = joined(up, up_in)
+    two_d = swap(two, z_d)
+    two_cd = swap(two_c, z_d)
+    gate_c = swap(gate, p_c)
+    two_cx = swap(two_c, core)
+    up_in = swap(up, z_b)
     att_a, extra_a = attend_forward(first, 0, mask_q, mask_k)
-    first, att_a, two_more, two_away, wide_in, down = tie(first, att_a, two_more, two_away, wide_in, down)
-    wide = joined(wide, wide_in)
-    two_last = swap(two_more, core)
-    wide_in = swap(wide, z_c)
-    down_in = swap(down, p_c)
+    first, att_a, two_d, two_cx, up_in, down = tie(first, att_a, two_d, two_cx, up_in, down)
+    up = joined(up, up_in)
+    up_c = swap(up, z_c)
+    two_dx = swap(two_d, core)
+    down_in = swap(down, z_a)
     att_b, extra_b = attend_forward(first, 1, mask_q, mask_k)
-    normed, att_b, two_last, wide_in, down_in = tie(normed, att_b, two_last, wide_in, down_in)
-    wide = joined(wide, wide_in)
+    normed, att_b, two_cd, two_dx, up_c, gate_c, down_in, up, gate = tie(
+        normed, att_b, two_cd, two_dx, up_c, gate_c, down_in, up, gate
+    )
     down = joined(down, down_in)
-    twos = (two, two_more, two_away, two_last)
-    wide_more = swap(wide, z_d)
-    wide_away = swap(wide, core)
-    down_more = swap(down, p_d)
+    up_d = swap(up, z_d)
+    gate_d = swap(gate, p_d)
+    normed, two_cdx = tie(normed, swap(two_cd, core))
+    twos = (two, two_c, two_d, two_cd, two_x, two_cx, two_dx, two_cdx)
+    up_x = swap(up, core)
+    gate_cx = swap(gate_c, core)
+    down_in = swap(down, z_b)
     second = second_project(me, normed, twos, BY_Z, row_d)
-    second, wide_away, down_next = tie(second, wide_away, down)
+    second, up_d, up_x, gate_cx, down_in, up_c, gate_c = tie(second, up_d, up_x, gate_cx, down_in, up_c, gate_c)
+    down = joined(down, down_in)
+    up_cd = swap(up_c, z_d)
+    gate_cd = swap(gate_c, p_d)
+    up_cx = swap(up_c, core)
+    up_dx = swap(up_d, core)
     att_c, extra_c = attend_forward(second, 0, mask_q, mask_k)
-    second, att_c, down_next = tie(second, att_c, down_next)
-    down_away = swap(down_next, core)
+    second, att_c, up_cd, up_cx, up_dx, gate_d, down = tie(second, att_c, up_cd, up_cx, up_dx, gate_d, down)
+    up_cdx = swap(up_cd, core)
+    gate_dx = swap(gate_d, core)
+    down_c = swap(down, z_c)
+    down_x = swap(down, core)
     att_d, extra_d = attend_forward(second, 1, mask_q, mask_k)
-    att_d, down_away, wide_more, down_more = tie(att_d, down_away, wide_more, down_more)
-    wide_last = swap(wide_more, core)
-    wide_last, down_more = tie(wide_last, down_more)
-    wides = (wide, wide_more, wide_away, wide_last)
+    att_d, up_cdx, gate_dx, gate_cd, down_c, down_x, down = tie(
+        att_d, up_cdx, gate_dx, gate_cd, down_c, down_x, down
+    )
+    down_d = swap(down, z_d)
+    gate_cdx, att_d = tie(swap(gate_cd, core), att_d)
+    down_cd = swap(down_c, z_d)
+    down_cx = swap(down_c, core)
+    gates = (gate, gate_c, gate_d, gate_cd, gate_x, gate_cx, gate_dx, gate_cdx)
+    ups = (up, up_c, up_d, up_cd, up_x, up_cx, up_dx, up_cdx)
+    wides = (*gates, *ups)
     attended = (att_a, att_b, att_c, att_d)
     extras = (extra_a, extra_b, extra_c, extra_d)
-    down_last = swap(down_more, core)
+    orders = (BY_Z, (BY_PLANE, BY_Z), BY_Z, BY_Z, BY_PLANE)
     active, sloped, inner, hidden, normed_two_t, grad_mixed, g_down = feed_in(
-        me, tokens, attended, cotangent, valid, gains, twos, wides, (BY_Z, BY_Z, BY_PLANE), row_d, 2 * col_f,
-        (8, row_f, width),
-    )
-    grad_mixed, g_down, down_last = tie(grad_mixed, g_down, down_last)
-    downs = (down, down_more, down_away, down_last)
-
-    def back(half, narrow, start, count, grad_now):
+        me, tokens, attended, cotangent, valid, gains, twos, wides, orders, row_d, 2 * col_f, (8, row_f, width)
+    )
+    grad_mixed, g_down, down_d, down_cd, down_cx = tie(grad_mixed, g_down, down_d, down_cd, down_cx)
+    down_dx = swap(down_d, core)
+    down_cdx = swap(down_cd, core)
+    d_on = swap(g_down[3], core)
+    d_other = swap(g_down[2], core)
+    grad_mixed, down_dx, down_cdx = tie(grad_mixed, down_dx, down_cdx)
+    downs = (down, down_c, down_d, down_cd, down_x, down_cx, down_dx, down_cdx)
+
+    def back(half, narrow, grad_now):
         place = half * 2 + narrow
         return attend_backward(
-            (first, second)[half], attended[place], grad_now, extras[place], mask_k, half, narrow, start, count
+            (first, second)[half], attended[place], grad_now, extras[place], mask_k, half, narrow, 0, 2
         )
 
-    d_on = swap(g_down[3], core)
-    d_other = swap(g_down[2], core)
     grad_gate, grad_up, g_wide = feed_grad(
-        me, active, sloped, grad_mixed, normed_two_t, downs, (BY_Z, BY_PLANE), row_d, (8, 2 * row_d, col_f)
+        me, active, sloped, grad_mixed, normed_two_t, downs, orders, row_d, (8, 2 * row_d, col_f)
     )
     grad_gate, g_wide, d_on, d_other = tie(grad_gate, g_wide, d_on, d_other)
     d_in = swap(add_low((g_down[1], d_on), 0, 8), p_d)
     w_on = swap(g_wide[3], core)
     w_other = swap(g_wide[2], core)
     mixed, grad_hidden, grad_att, gain_two = feed_out(
-        me, inner, grad_gate, grad_up, hidden, grad_mixed, gains, twos, wides, downs, (BY_Z, BY_Z, BY_PLANE), row_d
+        me, inner, grad_gate, grad_up, hidden, grad_mixed, gains, twos, wides, downs, orders, row_d
     )
     grad_att, d_in, w_on, w_other = tie(grad_att, d_in, w_on, w_other)
     w_in = swap(add_low((g_wide[1], w_on), 0, 8), z_d)
     d_parts = [g_down[0], d_other, d_in]
     d_next = swap(add_low(d_parts, 4, 8), p_c)
-    back_a = back(0, 0, 0, 2, grad_att)
+    back_a = back(0, 0, grad_att)
     grad_att, back_a, d_next = tie(grad_att, back_a, d_next)
     d_parts.append(d_next)
     d_next = swap(add_low(d_parts, 2, 4), p_b)
-    back_c = back(0, 1, 0, 2, grad_att)
-    normed_t, back_c, w_in, d_next = tie(normed_t, back_c, w_in, d_next)
+    back_b = back(0, 1, grad_att)
+    normed_t, back_b, w_in, d_next = tie(normed_t, back_b, w_in, d_next)
     d_parts.append(d_next)
     d_next = swap(add_low(d_parts, 1, 2), p_a)
     w_parts = [g_wide[0], w_other, w_in]
     w_next = swap(add_low(w_parts, 4, 8), z_c)
-    g_one = weight_grad(me, normed_t, (back_a, back_c), BY_Z, row_d, attended, grad_hidden)
-    grad_att, g_one, w_next, d_next = tie(grad_att, g_one, w_next, d_next)
+    g_one = weight_grad(me, normed_t, (back_a, back_b), BY_Z, row_d, attended, grad_hidden)
+    back_a, g_one, d_next = tie(back_a, g_one, d_next)
     d_parts.append(d_next)
-    w_parts.append(w_next)
     o_on = swap(g_one[3], core)
     o_other = swap(g_one[2], core)
+    (through,) = input_gradient(me, (back_a, back_b), ones, BY_Z, row_d)
+    grad_att, through, o_on, o_other, w_next = tie(grad_att, through, o_on, o_other, w_next)
+    w_parts.append(w_next)
+    o_in = swap(add_low((g_one[1], o_on), 0, 8), z_d)
     w_next = swap(add_low(w_parts, 2, 4), z_b)
-    back_d = back(1, 0, 0, 1, grad_att)
-    grad_att, back_d, o_on, o_other = tie(grad_att, back_d, o_on, o_other)
-    o_in = swap(add_low((g_one[1], o_on), 0, 8), z_d)
-    back_e = back(1, 0, 1, 1, grad_att)
-    grad_att, back_e, w_next, o_in = tie(grad_att, back_e, w_next, o_in)
+    back_c = back(1, 0, grad_att)
+    grad_att, back_c, w_next, o_in = tie(grad_att, back_c, w_next, o_in)
     w_parts.append(w_next)
     o_parts = [g_one[0], o_other, o_in]
+    o_next = swap(add_low(o_parts, 4, 8), z_c)
     w_next = swap(add_low(w_parts, 1, 2), z_a)
-    o_next = swap(add_low(o_parts, 4, 8), z_c)
-    back_f = back(1, 1, 0, 2, grad_att)
-    back_f, normed_t, w_next, o_next = tie(back_f, normed_t, w_next, o_next)
+    back_d = back(1, 1, grad_att)
+    back_d, normed_t, w_next, o_next = tie(back_d, normed_t, w_next, o_next)
     w_parts.append(w_next)
     o_parts.append(o_next)
     o_next = swap(add_low(o_parts, 2, 4), z_b)
-    g_two = weight_grad(me, normed_t, (back_d, back_e, back_f), BY_Z, row_d)
+    g_two = weight_grad(me, normed_t, (back_c, back_d), BY_Z, row_d)
     g_two, o_next = tie(g_two, o_next)
     o_parts.append(o_next)
     t_on = swap(g_two[3], core)
@@ -1103,29 +1128,28 @@
     tokens, t_on, t_other = tie(tokens, t_on, t_other)
     t_in = swap(add_low((g_two[1], t_on), 0, 8), z_d)
     o_next = swap(add_low(o_parts, 1, 2), z_a)
-    (through,) = input_gradient(me, (back_a, back_c), ones, BY_Z, row_d)
-    through, t_in, o_next = tie(through, t_in, o_next)
+    input_grad, gain_one = input_gradient(
+        me, (back_c, back_d), twos, BY_Z, row_d, (through, tokens, grad_hidden), gains
+    )
+    gain_one, t_in, o_next = tie(gain_one, t_in, o_next)
     o_parts.append(o_next)
     t_parts = [g_two[0], t_other, t_in]
     t_next = swap(add_low(t_parts, 4, 8), z_c)
-    input_grad, gain_one = input_gradient(
-        me, (back_d, back_e, back_f), twos, BY_Z, row_d, (through, tokens, grad_hidden), gains
-    )
-    gain_one, t_next = tie(gain_one, t_next)
     gain_sums = jnp.concatenate((gain_one, gain_two), axis=0)
-    t_parts.append(t_next)
-    t_next = swap(add_low(t_parts, 2, 4), z_b)
-    gain_in = swap(gain_sums, z_c)
+    gain_sums = gain_sums + swap(gain_sums, core)
+    gain_in = [swap(gain_sums, (kind, kind)) for kind in ("x", "y", "xy")]
     share_ffin = total(*(part[0] for part in w_parts)).reshape(2, row_d, col_f)
     share_down = total(*(part[0] for part in d_parts))
     t_next, gain_in = tie(t_next, gain_in)
     t_parts.append(t_next)
+    t_next = swap(add_low(t_parts, 2, 4), z_b)
+    gain_sums = gain_sums + (gain_in[0] + gain_in[1] + gain_in[2])
+    gain_in = swap(gain_sums, z_b)
+    t_next, gain_in = tie(t_next, gain_in)
+    t_parts.append(t_next)
+    t_next = swap(add_low(t_parts, 1, 2), z_a)
     gain_sums = gain_sums + gain_in
-    t_next = swap(add_low(t_parts, 1, 2), z_a)
-    gain_sums = gain_sums + swap(gain_sums, z_b)
     gain_sums = gain_sums + swap(gain_sums, z_a)
-    gain_sums = gain_sums + swap(gain_sums, z_d)
-    gain_sums = gain_sums + swap(gain_sums, core)
     t_parts.append(t_next)
     share_one = total(*(part[0] for part in o_parts))
     share_two = total(*(part[0] for part in t_parts))
@@ -1152,7 +1176,8 @@
     ff = full_ffin.shape[2]
     ones = (joined(halves[0], gain_block(full_gains, HALF))[None],)
     twos = (jnp.concatenate((halves[1], full_out), axis=1)[None],)
-    wides = (full_ffin.reshape(1, 2 * HD, ff),)
+    wides = (full_ffin[0][None], full_ffin[1][None])
+    orders = (None,) * 5
     downs = (whole(ffn_out, 0)[None],)
     first, normed, normed_t, gains = first_project(me, tokens, ones, None, HD)
     second = second_project(me, normed, twos, None, HD)
@@ -1160,13 +1185,13 @@
     found = [attend_forward(projected[i], i % 2, mask_q, mask_k) for i in range(4)]
     attended = tuple(pair[0] for pair in found)
     active, sloped, inner, hidden, normed_two_t, grad_mixed, g_down = feed_in(
-        me, tokens, attended, cotangent, valid, gains, twos, wides, (None,) * 3, HD, ff, (1, ff, HD)
+        me, tokens, attended, cotangent, valid, gains, twos, wides, orders, HD, ff, (1, ff, HD)
     )
     grad_gate, grad_up, g_wide = feed_grad(
-        me, active, sloped, grad_mixed, normed_two_t, downs, (None,) * 2, HD, (1, 2 * HD, ff)
+        me, active, sloped, grad_mixed, normed_two_t, downs, orders, HD, (1, 2 * HD, ff)
     )
     mixed, grad_hidden, grad_att, gain_two = feed_out(
-        me, inner, grad_gate, grad_up, hidden, grad_mixed, gains, twos, wides, downs, (None,) * 3, HD
+        me, inner, grad_gate, grad_up, hidden, grad_mixed, gains, twos, wides, downs, orders, HD
     )
     grads = [
         attend_backward(projected[i], attended[i], grad_att, found[i][1], mask_k, i // 2, i % 2, 0, 2)

time: 498 us -> 488 us (0.980)
  waiting for transfers between devices: 82.9 us -> 66 us
  starting transfers between devices: 43 us -> 59.6 us
    ppermute x53 -> x75, waiting for transfers between devices: 82.9 us -> 66 us  [swap(): return lax.ppermute(array, AXES, partners(kinds))]
    ppermute x53 -> x75, starting transfers between devices: 43 us -> 59.6 us  [swap(): return lax.ppermute(array, AXES, partners(kinds))]
    pallas_call x5 -> x4, Pallas kernels: 65.6 us -> 63.9 us  [attend_backward(): pl.pallas_call(attend_backward_kernel, grid=(count,), in_specs=tile_specs...]
  transfers between devices with their start and end apart: 53 -> 75, of which waited for: 22 -> 20; matrix products, arithmetic and copies ran while one was open for 10% -> 10% of each run, Pallas kernels for 57% -> 58%
where the time goes in v3:
time: 488 us; the launch traced here: 479 us
  Pallas kernels  276 us (57%)
  waiting for transfers between devices  66 us (14%)
  other arithmetic  60.1 us (12%)
  starting transfers between devices  59.6 us (12%)
  local copies, waits for them, and re-layouts  13.4 us (3%)
    ppermute x75, waiting for transfers between devices, swap(): return lax.ppermute(array, AXES, partners(kinds))  66 us
    pallas_call x4, Pallas kernels, attend_backward(): pl.pallas_call(attend_backward_kernel, grid=(count,), in_specs=tile_specs...  63.9 us
    ppermute x75, starting transfers between devices, swap(): return lax.ppermute(array, AXES, partners(kinds))  59.6 us
    pallas_call x1, Pallas kernels, feed_in(): pl.pallas_call(functools.partial(feed_in_kernel, orders, rows_piece), gri...  43.6 us
    pallas_call x4, Pallas kernels, attend_forward(): pl.pallas_call(attend_forward_kernel, grid=(2,), in_specs=tile_specs(rows...  37.2 us
    convert_element_type x16, other arithmetic, add_low(): return total(*(part[low:high] for part in parts)).astype(BF)  34.6 us
    pallas_call x1, Pallas kernels, feed_out(): pl.pallas_call(functools.partial(feed_out_kernel, orders, rows_piece), gr...  34.4 us
    pallas_call x1, Pallas kernels, feed_grad(): pl.pallas_call(functools.partial(feed_grad_kernel, orders, rows_piece), g...  33.3 us
  transfers between devices with their start and end apart: 75, of which 20 were waited for; matrix products, arithmetic and copies ran while one was open for 10% of the time, Pallas kernels for 58%

profile of v3, /device:TPU:0, one launch (start us, length us, event | category | flops | bytes accessed | tf_op | source)
XLA Modules:
  0.0 478.8 jit_solution(12043629408091262005)
XLA Ops:
  3.2 4.1 collective-permute-start
  8.0 1.5 collective-permute-start.1
  11.5 2.0 select_add_fusion
  13.5 1.6 collective-permute-start.2
  15.2 1.7 collective-permute-start.3
  17.1 5.2 %collective-permute-done.2 = bf16[2,80,768]{2,1,0:T(8,128)(2,1)S(1)} collective-permute-done((bf16[2,80,768]{2,1,0:T(8,128)(2,1)S(1)}, bf16[2,80,768]{2,1,0:T(8,128)(2,1)S(1)}, u32[]{:S(2)}, u32[]{:S(2)}) %collective-permute-start.2) | collective-permute-done | bytes 245792 | tf_op jit(solution)/shard_map/ppermute | solution.py:73
  22.9 1.7 collective-permute-start.5
  24.6 1.5 collective-permute-start.4
  26.0 3.1 fusion.7.valid_ref
  30.0 7.1 %collective-permute-done.7 = bf16[1,64,1280]{2,1,0:T(8,128)(2,1)S(1)} collective-permute-done((bf16[1,64,1280]{2,1,0:T(8,128)(2,1)S(1)}, bf16[1,64,1280]{2,1,0:T(8,128)(2,1)S(1)}, u32[]{:S(2)}, u32[]{:S(2)}) %collective-permute-start.7) | collective-permute-done | bytes 163872 | tf_op jit(solution)/shard_map/ppermute | solution.py:73
  40.3 5.7 %collective-permute-done.8.refs_3_ = bf16[4,80,768]{2,1,0:T(8,128)(2,1)S(1)} collective-permute-done((bf16[4,80,768]{2,1,0:T(8,128)(2,1)S(1)}, bf16[4,80,768]{2,1,0:T(8,128)(2,1)S(1)}, u32[]{:S(2)}, u32[]{:S(2)}) %collective-permute-start.8) | collective-permute-done | bytes 491552 | tf_op jit(solution)/shard_map/ppermute | solution.py:73
  46.3 10.1 %collective-permute-done.12 = bf16[2,64,1280]{2,1,0:T(8,128)(2,1)S(1)} collective-permute-done((bf16[2,64,1280]{2,1,0:T(8,128)(2,1)S(1)}, bf16[2,64,1280]{2,1,0:T(8,128)(2,1)S(1)}, u32[]{:S(2)}, u32[]{:S(2)}) %collective-permute-start.12) | collective-permute-done | bytes 327712 | tf_op jit(solution)/shard_map/ppermute | solution.py:73
  59.9 9.2 %first_project.1 = (bf16[1152,1536]{1,0:T(8,128)(2,1)}, bf16[1152,1024]{1,0:T(8,128)(2,1)}, bf16[1024,1152]{1,0:T(8,128)(2,1)}, f32[2,1024]{1,0:T(2,128)}) custom-call(s32[1]{0:T(128)} %bitcast.me_ref, bf16[1152,1024]{1,0:T(8,128)(2,1)} %refs_11_, bf16[4,80,768]{2,1,0:T(8,128)(2,1)} %copy-done.10, bf16[4,80,768]{2,1,0:T(8,128)(2,1)} %copy-done.28, ...), custom_call_target="tpu_custom_call" | custom-call | tf_op jit(solution)/shard_map/first_project/pallas_call | solution.py:171
  70.6 1.6 collective-permute-start.17
  72.3 1.8 pad_maximum_fusion.4
  74.8 1.6 constant_dynamic-update-slice_fusion.5
  76.4 1.8 collective-permute-start.23
  78.3 9.2 %attend_forward.4 = (bf16[1152,256]{1,0:T(8,128)(2,1)}, bf16[1152,256]{1,0:T(8,128)(2,1)}) custom-call(bf16[1152,1536]{1,0:T(8,128)(2,1)} %get-tuple-element.236.q_ref.k_ref.v_ref, bf16[1152,1536]{1,0:T(8,128)(2,1)} %get-tuple-element.236.q_ref.k_ref.v_ref, bf16[1152,1536]{1,0:T(8,128)(2,1)} %get-tuple-element.236.q_ref.k_ref.v_ref, ...), custom_call_target="tpu_custom_call" | custom-call | tf_op jit(solution)/shard_map/attend_forward/pallas_call | solution.py:297
  87.4 1.6 constant_dynamic-update-slice_fusion.4
  90.0 2.1 constant_dynamic-update-slice_fusion.3.refs_16_
  93.6 9.4 %attend_forward.5 = (bf16[1152,256]{1,0:T(8,128)(2,1)}, bf16[1152,256]{1,0:T(8,128)(2,1)}) custom-call(bf16[1152,1536]{1,0:T(8,128)(2,1)} %get-tuple-element.236.q_ref.k_ref.v_ref, bf16[1152,1536]{1,0:T(8,128)(2,1)} %get-tuple-element.236.q_ref.k_ref.v_ref, bf16[1152,1536]{1,0:T(8,128)(2,1)} %get-tuple-element.236.q_ref.k_ref.v_ref, ...), custom_call_target="tpu_custom_call" | custom-call | tf_op jit(solution)/shard_map/attend_forward/pallas_call | solution.py:297
  103.0 7.1 %collective-permute-done.20.refs_3_ = bf16[4,64,1280]{2,1,0:T(8,128)(2,1)S(1)} collective-permute-done((bf16[4,64,1280]{2,1,0:T(8,128)(2,1)S(1)}, bf16[4,64,1280]{2,1,0:T(8,128)(2,1)S(1)}, u32[]{:S(2)}, u32[]{:S(2)}) %collective-permute-start.20) | collective-permute-done | bytes 655392 | tf_op jit(solution)/shard_map/ppermute | solution.py:73
  115.3 9.0 %second_project.1.q_ref.k_ref.v_ref = bf16[1152,1536]{1,0:T(8,128)(2,1)} custom-call(s32[1]{0:T(128)} %bitcast.me_ref, bf16[1152,1024]{1,0:T(8,128)(2,1)} %get-tuple-element.245.normed_ref, bf16[4,64,1280]{2,1,0:T(8,128)(2,1)} %copy-done, bf16[4,64,1280]{2,1,0:T(8,128)(2,1)} %copy-done.2, bf16[4,64,1280]{2,1,0:T(8,128)(2,1)} %copy-done.3, ...), custom_call_target="tpu_custom_call" | custom-call | tf_op jit(solution)/shard_map/second_project/pallas_call | solution.py:210
  127.4 9.1 %attend_forward.6 = (bf16[1152,256]{1,0:T(8,128)(2,1)}, bf16[1152,256]{1,0:T(8,128)(2,1)}) custom-call(bf16[1152,1536]{1,0:T(8,128)(2,1)} %second_project.1.q_ref.k_ref.v_ref, bf16[1152,1536]{1,0:T(8,128)(2,1)} %second_project.1.q_ref.k_ref.v_ref, bf16[1152,1536]{1,0:T(8,128)(2,1)} %second_project.1.q_ref.k_ref.v_ref, ...), custom_call_target="tpu_custom_call" | custom-call | tf_op jit(solution)/shard_map/attend_forward/pallas_call | solution.py:297
  137.6 1.5 collective-permute-done.33.refs_10_
  141.3 9.6 %attend_forward.7 = (bf16[1152,256]{1,0:T(8,128)(2,1)}, bf16[1152,256]{1,0:T(8,128)(2,1)}) custom-call(bf16[1152,1536]{1,0:T(8,128)(2,1)} %second_project.1.q_ref.k_ref.v_ref, bf16[1152,1536]{1,0:T(8,128)(2,1)} %second_project.1.q_ref.k_ref.v_ref, bf16[1152,1536]{1,0:T(8,128)(2,1)} %second_project.1.q_ref.k_ref.v_ref, ...), custom_call_target="tpu_custom_call" | custom-call | tf_op jit(solution)/shard_map/attend_forward/pallas_call | solution.py:297
  150.9 3.7 collective-permute-done.36.refs_11_
  158.1 43.6 %feed_in.1 = (bf16[1152,2816]{1,0:T(8,128)(2,1)}, bf16[1152,2816]{1,0:T(8,128)(2,1)}, bf16[1152,2816]{1,0:T(8,128)(2,1)}, f32[1152,1024]{1,0:T(8,128)}, bf16[102...) custom-call(s32[1]{0:T(128)} %bitcast.me_ref, ...), custom_call_target="tpu_custom_call" | custom-call | tf_op jit(solution)/shard_map/feed_in/pallas_call | solution.py:587
  202.8 4.3 collective-permute-done.43.refs_6_.refs_30_
  207.1 2.3 collective-permute-done.44.refs_7_.refs_31_
  210.3 33.3 %feed_grad.1 = (bf16[1152,2816]{1,0:T(8,128)(2,1)}, bf16[1152,2816]{1,0:T(8,128)(2,1)}, bf16[8,128,1408]{2,1,0:T(8,128)(2,1)}, bf16[8,128,1408]{2,1,0:T(8,128)(2...) custom-call(s32[1]{0:T(128)} %bitcast.me_ref, bf16[1152,2816]{1,0:T(8,128)(2,1)} %get-tuple-element.282.active_ref, ...), custom_call_target="tpu_custom_call" | custom-call | tf_op jit(solution)/shard_map/feed_grad/pallas_call | solution.py:687
  244.2 3.3 add_convert_fusion.2
  248.3 34.4 %feed_out.1 = (bf16[1152,1024]{1,0:T(8,128)(2,1)}, f32[1152,1024]{1,0:T(8,128)}, bf16[1152,1024]{1,0:T(8,128)(2,1)}, f32[1,1024]{1,0:T(1,128)}) custom-call(s32[1]{0:T(128)} %bitcast.me_ref, bf16[1152,2816]{1,0:T(8,128)(2,1)} %get-tuple-element.281.inner_ref, bf16[1152,2816]{1,0:T(8,128)(2,1)} %get-tuple-element.307.grad_gate_ref, ...), custom_call_target="tpu_custom_call" | custom-call | tf_op jit(solution)/shard_map/feed_out/pallas_call | solution.py:754
  282.8 4.2 add_convert_fusion
  289.1 2.4 collective-permute-start.50
  291.6 15.8 %attend_backward.4.refs_1_.refs_8_ = bf16[1152,768]{1,0:T(8,128)(2,1)} custom-call(bf16[1152,1536]{1,0:T(8,128)(2,1)} %get-tuple-element.236.q_ref.k_ref.v_ref, bf16[1152,1536]{1,0:T(8,128)(2,1)} %get-tuple-element.236.q_ref.k_ref.v_ref, bf16[1152,1536]{1,0:T(8,128)(2,1)} %get-tuple-element.236.q_ref.k_ref.v_ref, ...), custom_call_target="tpu_custom_call" | custom-call | tf_op jit(solution)/shard_map/attend_backward/pallas_call | solution.py:371
  307.4 1.8 collective-permute-done.50
  309.1 2.1 add_convert_fusion.10
  312.5 16.5 %attend_backward.5.refs_2_.refs_9_ = bf16[1152,768]{1,0:T(8,128)(2,1)} custom-call(bf16[1152,1536]{1,0:T(8,128)(2,1)} %get-tuple-element.236.q_ref.k_ref.v_ref, bf16[1152,1536]{1,0:T(8,128)(2,1)} %get-tuple-element.236.q_ref.k_ref.v_ref, bf16[1152,1536]{1,0:T(8,128)(2,1)} %get-tuple-element.236.q_ref.k_ref.v_ref, ...), custom_call_target="tpu_custom_call" | custom-call | tf_op jit(solution)/shard_map/attend_backward/pallas_call | solution.py:371
  329.0 1.9 add_convert_fusion.13
  331.8 3.4 add_convert_fusion.1
  336.4 12.6 %weight_grad.2 = (bf16[8,64,1280]{2,1,0:T(8,128)(2,1)}, bf16[8,64,1280]{2,1,0:T(8,128)(2,1)}, bf16[8,64,1280]{2,1,0:T(8,128)(2,1)}, bf16[8,64,1280]{2,1,0:T(8,128)(2,1)}) custom-call(s32[1]{0:T(128)} %bitcast.me_ref, bf16[1024,1152]{1,0:T(8,128)(2,1)} %get-tuple-element.356.refs_0_, bf16[1152,768]{1,0:T(8,128)(2,1)} %attend_backward.4.refs_1_.refs_8_, ...), custom_call_target="tpu_custom_call" | custom-call | tf_op jit(solution)/shard_map/weight_grad/pallas_call | solution.py:861
  349.6 9.4 %input_gradient.2.refs_10_ = f32[1152,1024]{1,0:T(8,128)} custom-call(s32[1]{0:T(128)} %bitcast.me_ref, bf16[4,80,768]{2,1,0:T(8,128)(2,1)} %copy-done.10, bf16[4,80,768]{2,1,0:T(8,128)(2,1)} %copy-done.28, bf16[4,80,768]{2,1,0:T(8,128)(2,1)} %copy-done.27, bf16[4,80,768]{2,1,0:T(8,128)(2,1)} %copy-done.30, bf16[4,80,768]{2,1,0:T(8,128)(2,1)} %copy-done.26, ...), custom_call_target="tpu_custom_call" | custom-call | tf_op jit(solution)/shard_map/input_gradient/pallas_call | solution.py:906
  359.0 3.1 add_convert_fusion.3
  362.9 2.8 add_convert_fusion.5
  366.1 15.8 %attend_backward.6.refs_1_.refs_8_ = bf16[1152,768]{1,0:T(8,128)(2,1)} custom-call(bf16[1152,1536]{1,0:T(8,128)(2,1)} %second_project.1.q_ref.k_ref.v_ref, bf16[1152,1536]{1,0:T(8,128)(2,1)} %second_project.1.q_ref.k_ref.v_ref, bf16[1152,1536]{1,0:T(8,128)(2,1)} %second_project.1.q_ref.k_ref.v_ref, ...), custom_call_target="tpu_custom_call" | custom-call | tf_op jit(solution)/shard_map/attend_backward/pallas_call | solution.py:371
  381.9 3.0 collective-permute-done.57
  384.9 2.6 add_convert_fusion.7
  388.8 2.3 add_convert_fusion.9
  391.3 15.8 %attend_backward.7.refs_2_.refs_9_ = bf16[1152,768]{1,0:T(8,128)(2,1)} custom-call(bf16[1152,1536]{1,0:T(8,128)(2,1)} %second_project.1.q_ref.k_ref.v_ref, bf16[1152,1536]{1,0:T(8,128)(2,1)} %second_project.1.q_ref.k_ref.v_ref, bf16[1152,1536]{1,0:T(8,128)(2,1)} %second_project.1.q_ref.k_ref.v_ref, ...), custom_call_target="tpu_custom_call" | custom-call | tf_op jit(solution)/shard_map/attend_backward/pallas_call | solution.py:371
  407.9 2.1 add_convert_fusion.11
  410.0 2.6 collective-permute-start.61
  412.6 9.1 %weight_grad.3 = (bf16[8,64,768]{2,1,0:T(8,128)(2,1)}, bf16[8,64,768]{2,1,0:T(8,128)(2,1)}, bf16[8,64,768]{2,1,0:T(8,128)(2,1)}, bf16[8,64,768]{2,1,0:T(8,128)(2,1)}) custom-call(s32[1]{0:T(128)} %bitcast.me_ref, bf16[1024,1152]{1,0:T(8,128)(2,1)} %get-tuple-element.356.refs_0_, bf16[1152,768]{1,0:T(8,128)(2,1)} %attend_backward.6.refs_1_.refs_8_, ...), custom_call_target="tpu_custom_call" | custom-call | tf_op jit(solution)/shard_map/weight_grad/pallas_call | solution.py:861
  422.3 2.5 multiply_subtract_fusion.2
  424.8 1.8 add_add_fusion
  430.1 1.7 multiply_subtract_fusion
  431.8 14.4 %input_gradient.3 = (f32[1152,1024]{1,0:T(8,128)}, f32[1,1024]{1,0:T(1,128)}) custom-call(s32[1]{0:T(128)} %bitcast.me_ref, bf16[4,64,1280]{2,1,0:T(8,128)(2,1)} %copy-done, bf16[4,64,1280]{2,1,0:T(8,128)(2,1)} %copy-done.2, bf16[4,64,1280]{2,1,0:T(8,128)(2,1)} %copy-done.3, bf16[4,64,1280]{2,1,0:T(8,128)(2,1)} %copy-done.5, bf16[4,64,1280]{2,1,0:T(8,128)(2,1)} %copy-done.1, ...), custom_call_target="tpu_custom_call" | custom-call | tf_op jit(solution)/shard_map/input_gradient/pallas_call | solution.py:906
  448.3 1.4 collective-permute-start.66
  449.7 1.4 collective-permute-start.70
  454.6 2.5 collective-permute-done.70
  457.1 1.9 collective-permute-start.72
  461.3 6.6 %collective-permute-done.71 = bf16[2,64,768]{2,1,0:T(8,128)(2,1)S(1)} collective-permute-done((bf16[2,64,768]{2,1,0:T(8,128)(2,1)S(1)}, bf16[2,64,768]{2,1,0:T(8,128)(2,1)S(1)}, u32[]{:S(2)}, u32[]{:S(2)}) %collective-permute-start.71) | collective-permute-done | bytes 196640 | tf_op jit(solution)/shard_map/ppermute | solution.py:73
  469.2 2.7 collective-permute-start.73
  473.1 1.7 collective-permute-done.73
  (305 shorter events, 63.0 us)
Async XLA Ops:
  3.2 10.3 %collective-permute-start = (bf16[1,80,768]{2,1,0:T(8,128)(2,1)S(1)}, bf16[1,80,768]{2,1,0:T(8,128)(2,1)S(1)}, u32[]{:S(2)}, u32[]{:S(2)}) collective-permute-start(bf16[1,80,768]{2,1,0:T(8,128)(2,1)S(1)} %fusion.13), channel_id=1, source_target_pairs={{0,16},{1,17},{2,10},{3,11},{4,20},{5,21},{6,14},{7,15},{8,24},{9,... | collective-permute-start | bytes 368648 | tf_op jit(solution)/shard_map/ppermute | solution.py:73
  8.0 5.5 %collective-permute-start.1 = (bf16[1,64,1408]{2,1,0:T(8,128)(2,1)S(1)}, bf16[1,64,1408]{2,1,0:T(8,128)(2,1)S(1)}, u32[]{:S(2)}, u32[]{:S(2)}) collective-permute-start(bf16[1,64,1408]{2,1,0:T(8,128)(2,1)S(1)} %get-tuple-element.403), channel_id=1, source_target_pairs={{0,4},{1,5},{2,3},{3,2},{4,0},{5,1},{6,7},{7,6},{8,12},{9,13},{10,... | collective-permute-start | bytes 540680 | tf_op jit(solution)/shard_map/ppermute | solution.py:73
  13.5 8.8 %collective-permute-start.2 = (bf16[2,80,768]{2,1,0:T(8,128)(2,1)S(1)}, bf16[2,80,768]{2,1,0:T(8,128)(2,1)S(1)}, u32[]{:S(2)}, u32[]{:S(2)}) collective-permute-start(bf16[2,80,768]{2,1,0:T(8,128)(2,1)S(1)} %pad_maximum_fusion.9), channel_id=1, source_target_pairs={{0,8},{1,9},{2,18},{3,19},{4,12},{5,13},{6,22},{7,23},{8,0},{9,1},... | collective-permute-start | bytes 737288 | tf_op jit(solution)/shard_map/ppermute | solution.py:73
  15.2 7.5 %collective-permute-start.3 = (bf16[2,64,1408]{2,1,0:T(8,128)(2,1)S(1)}, bf16[2,64,1408]{2,1,0:T(8,128)(2,1)S(1)}, u32[]{:S(2)}, u32[]{:S(2)}) collective-permute-start(bf16[2,64,1408]{2,1,0:T(8,128)(2,1)S(1)} %pad_maximum_fusion.3), channel_id=1, source_target_pairs={{0,1},{1,0},{2,6},{3,7},{4,5},{5,4},{6,2},{7,3},{8,9},{9,8},{10,14... | collective-permute-start | bytes 1081352 | tf_op jit(solution)/shard_map/ppermute | solution.py:73
  22.8 14.3 %collective-permute-start.6 = (bf16[4,80,768]{2,1,0:T(8,128)(2,1)S(1)}, bf16[4,80,768]{2,1,0:T(8,128)(2,1)S(1)}, u32[]{:S(2)}, u32[]{:S(2)}) collective-permute-start(bf16[4,80,768]{2,1,0:T(8,128)(2,1)S(1)} %pad_maximum_fusion.2.refs_0_), channel_id=1, source_target_pairs={{0,2},{1,3},{2,0},{3,1},{4,6},{5,7},{6,4},{7,5},{8,10},{9,11},{10,... | collective-permute-start | bytes 1474568 | tf_op jit(solution)/shard_map/ppermute | solution.py:73
  22.9 14.2 %collective-permute-start.5 = (bf16[4,80,768]{2,1,0:T(8,128)(2,1)S(1)}, bf16[4,80,768]{2,1,0:T(8,128)(2,1)S(1)}, u32[]{:S(2)}, u32[]{:S(2)}) collective-permute-start(bf16[4,80,768]{2,1,0:T(8,128)(2,1)S(1)} %pad_maximum_fusion.2.refs_0_), channel_id=1, source_target_pairs={{0,1},{1,0},{2,6},{3,7},{4,5},{5,4},{6,2},{7,3},{8,9},{9,8},{10,14... | collective-permute-start | bytes 1474568 | tf_op jit(solution)/shard_map/ppermute | solution.py:73
  24.6 12.5 %collective-permute-start.4 = (bf16[4,80,768]{2,1,0:T(8,128)(2,1)S(1)}, bf16[4,80,768]{2,1,0:T(8,128)(2,1)S(1)}, u32[]{:S(2)}, u32[]{:S(2)}) collective-permute-start(bf16[4,80,768]{2,1,0:T(8,128)(2,1)S(1)} %pad_maximum_fusion.2.refs_0_), channel_id=1, source_target_pairs={{0,4},{1,5},{2,3},{3,2},{4,0},{5,1},{6,7},{7,6},{8,12},{9,13},{10,... | collective-permute-start | bytes 1474568 | tf_op jit(solution)/shard_map/ppermute | solution.py:73
  29.1 7.9 %collective-permute-start.7 = (bf16[1,64,1280]{2,1,0:T(8,128)(2,1)S(1)}, bf16[1,64,1280]{2,1,0:T(8,128)(2,1)S(1)}, u32[]{:S(2)}, u32[]{:S(2)}) collective-permute-start(bf16[1,64,1280]{2,1,0:T(8,128)(2,1)S(1)} %maximum_bitcast_fusion.1), channel_id=1, source_target_pairs={{0,16},{1,17},{2,10},{3,11},{4,20},{5,21},{6,14},{7,15},{8,24},{9,... | collective-permute-start | bytes 491528 | tf_op jit(solution)/shard_map/ppermute | solution.py:73
  37.2 8.9 %collective-permute-start.8 = (bf16[4,80,768]{2,1,0:T(8,128)(2,1)S(1)}, bf16[4,80,768]{2,1,0:T(8,128)(2,1)S(1)}, u32[]{:S(2)}, u32[]{:S(2)}) collective-permute-start(bf16[4,80,768]{2,1,0:T(8,128)(2,1)S(1)} %collective-permute-done.4.refs_1_), channel_id=1, source_target_pairs={{0,1},{1,0},{2,6},{3,7},{4,5},{5,4},{6,2},{7,3},{8,9},{9,8},{10,14... | collective-permute-start | bytes 1474568 | tf_op jit(solution)/shard_map/ppermute | solution.py:73
  46.1 10.3 %collective-permute-start.11 = (bf16[4,80,768]{2,1,0:T(8,128)(2,1)S(1)}, bf16[4,80,768]{2,1,0:T(8,128)(2,1)S(1)}, u32[]{:S(2)}, u32[]{:S(2)}) collective-permute-start(bf16[4,80,768]{2,1,0:T(8,128)(2,1)S(1)} %collective-permute-done.8.refs_3_), channel_id=1, source_target_pairs={{0,2},{1,3},{2,0},{3,1},{4,6},{5,7},{6,4},{7,5},{8,10},{9,11},{10,... | collective-permute-start | bytes 1474568 | tf_op jit(solution)/shard_map/ppermute | solution.py:73
  46.1 10.2 %collective-permute-start.12 = (bf16[2,64,1280]{2,1,0:T(8,128)(2,1)S(1)}, bf16[2,64,1280]{2,1,0:T(8,128)(2,1)S(1)}, u32[]{:S(2)}, u32[]{:S(2)}) collective-permute-start(bf16[2,64,1280]{2,1,0:T(8,128)(2,1)S(1)} %pad_maximum_fusion.6), channel_id=1, source_target_pairs={{0,8},{1,9},{2,18},{3,19},{4,12},{5,13},{6,22},{7,23},{8,0},{9,1},... | collective-permute-start | bytes 983048 | tf_op jit(solution)/shard_map/ppermute | solution.py:73
  56.4 12.8 %collective-permute-start.15 = (bf16[4,64,1408]{2,1,0:T(8,128)(2,1)S(1)}, bf16[4,64,1408]{2,1,0:T(8,128)(2,1)S(1)}, u32[]{:S(2)}, u32[]{:S(2)}) collective-permute-start(bf16[4,64,1408]{2,1,0:T(8,128)(2,1)S(1)} %pad_maximum_fusion.refs_8_), channel_id=1, source_target_pairs={{0,2},{1,3},{2,0},{3,1},{4,6},{5,7},{6,4},{7,5},{8,10},{9,11},{10,... | collective-permute-start | bytes 2162696 | tf_op jit(solution)/shard_map/ppermute | solution.py:73
  56.9 12.3 %collective-permute-start.14 = (bf16[4,64,1280]{2,1,0:T(8,128)(2,1)S(1)}, bf16[4,64,1280]{2,1,0:T(8,128)(2,1)S(1)}, u32[]{:S(2)}, u32[]{:S(2)}) collective-permute-start(bf16[4,64,1280]{2,1,0:T(8,128)(2,1)S(1)} %constant_dynamic-update-slice_fusion.refs_0_), channel_id=1, source_target_pairs={{0,2},{1,3},{2,0},{3,1},{4,6},{5,7},{6,4},{7,5},{8,10},{9,11},{10,... | collective-permute-start | bytes 1966088 | tf_op jit(solution)/shard_map/ppermute | solution.py:73
  57.0 12.1 %collective-permute-start.13 = (bf16[4,64,1280]{2,1,0:T(8,128)(2,1)S(1)}, bf16[4,64,1280]{2,1,0:T(8,128)(2,1)S(1)}, u32[]{:S(2)}, u32[]{:S(2)}) collective-permute-start(bf16[4,64,1280]{2,1,0:T(8,128)(2,1)S(1)} %constant_dynamic-update-slice_fusion.refs_0_), channel_id=1, source_target_pairs={{0,4},{1,5},{2,3},{3,2},{4,0},{5,1},{6,7},{7,6},{8,12},{9,13},{10,... | collective-permute-start | bytes 1966088 | tf_op jit(solution)/shard_map/ppermute | solution.py:73
  58.3 10.8 %collective-permute-start.16 = (bf16[1,64,1408]{2,1,0:T(8,128)(2,1)}, bf16[1,64,1408]{2,1,0:T(8,128)(2,1)S(1)}, u32[]{:S(2)}, u32[]{:S(2)}) collective-permute-start(bf16[1,64,1408]{2,1,0:T(8,128)(2,1)} %get-tuple-element.226), channel_id=1, source_target_pairs={{0,16},{1,17},{2,10},{3,11},{4,20},{5,21},{6,14},{7,15},{8,24},{9,... | collective-permute-start | bytes 540680 | tf_op jit(solution)/shard_map/ppermute | solution.py:73
  70.6 19.3 %collective-permute-start.17 = (bf16[4,64,1280]{2,1,0:T(8,128)(2,1)S(1)}, bf16[4,64,1280]{2,1,0:T(8,128)(2,1)S(1)}, u32[]{:S(2)}, u32[]{:S(2)}) collective-permute-start(bf16[4,64,1280]{2,1,0:T(8,128)(2,1)S(1)} %constant_dynamic-update-slice_fusion.refs_0_), channel_id=1, source_target_pairs={{0,1},{1,0},{2,6},{3,7},{4,5},{5,4},{6,2},{7,3},{8,9},{9,8},{10,14... | collective-permute-start | bytes 1966088 | tf_op jit(solution)/shard_map/ppermute | solution.py:73
  72.3 17.7 %collective-permute-start.18 = (bf16[4,64,1280]{2,1,0:T(8,128)(2,1)S(1)}, bf16[4,64,1280]{2,1,0:T(8,128)(2,1)S(1)}, u32[]{:S(2)}, u32[]{:S(2)}) collective-permute-start(bf16[4,64,1280]{2,1,0:T(8,128)(2,1)S(1)} %collective-permute-done.13.refs_1_), channel_id=1, source_target_pairs={{0,2},{1,3},{2,0},{3,1},{4,6},{5,7},{6,4},{7,5},{8,10},{9,11},{10,... | collective-permute-start | bytes 1966088 | tf_op jit(solution)/shard_map/ppermute | solution.py:73
  74.0 15.9 %collective-permute-start.19 = (bf16[2,64,1408]{2,1,0:T(8,128)(2,1)}, bf16[2,64,1408]{2,1,0:T(8,128)(2,1)}, u32[]{:S(2)}, u32[]{:S(2)}) collective-permute-start(bf16[2,64,1408]{2,1,0:T(8,128)(2,1)} %pad_maximum_fusion.4), channel_id=1, source_target_pairs={{0,8},{1,9},{2,18},{3,19},{4,12},{5,13},{6,22},{7,23},{8,0},{9,1},... | collective-permute-start | bytes 1081352 | tf_op jit(solution)/shard_map/ppermute | solution.py:73
  76.4 33.6 %collective-permute-start.23 = (bf16[4,64,1408]{2,1,0:T(8,128)(2,1)S(1)}, bf16[4,64,1408]{2,1,0:T(8,128)(2,1)}, u32[]{:S(2)}, u32[]{:S(2)}) collective-permute-start(bf16[4,64,1408]{2,1,0:T(8,128)(2,1)S(1)} %pad_maximum_fusion.refs_8_), channel_id=1, source_target_pairs={{0,16},{1,17},{2,10},{3,11},{4,20},{5,21},{6,14},{7,15},{8,24},{9,... | collective-permute-start | bytes 2162696 | tf_op jit(solution)/shard_map/ppermute | solution.py:73
  92.0 18.3 %collective-permute-start.22 = (bf16[4,64,1408]{2,1,0:T(8,128)(2,1)}, bf16[4,64,1408]{2,1,0:T(8,128)(2,1)}, u32[]{:S(2)}, u32[]{:S(2)}) collective-permute-start(bf16[4,64,1408]{2,1,0:T(8,128)(2,1)} %constant_dynamic-update-slice_fusion.3.refs_16_), channel_id=1, source_target_pairs={{0,4},{1,5},{2,3},{3,2},{4,0},{5,1},{6,7},{7,6},{8,12},{9,13},{10,... | collective-permute-start | bytes 2162696 | tf_op jit(solution)/shard_map/ppermute | solution.py:73
  92.5 17.5 %collective-permute-start.20 = (bf16[4,64,1280]{2,1,0:T(8,128)(2,1)S(1)}, bf16[4,64,1280]{2,1,0:T(8,128)(2,1)S(1)}, u32[]{:S(2)}, u32[]{:S(2)}) collective-permute-start(bf16[4,64,1280]{2,1,0:T(8,128)(2,1)S(1)} %collective-permute-done.13.refs_1_), channel_id=1, source_target_pairs={{0,1},{1,0},{2,6},{3,7},{4,5},{5,4},{6,2},{7,3},{8,9},{9,8},{10,14... | collective-permute-start | bytes 1966088 | tf_op jit(solution)/shard_map/ppermute | solution.py:73
  92.9 17.2 %collective-permute-start.21 = (bf16[4,64,1280]{2,1,0:T(8,128)(2,1)S(1)}, bf16[4,64,1280]{2,1,0:T(8,128)(2,1)S(1)}, u32[]{:S(2)}, u32[]{:S(2)}) collective-permute-start(bf16[4,64,1280]{2,1,0:T(8,128)(2,1)S(1)} %collective-permute-done.17.refs_2_), channel_id=1, source_target_pairs={{0,2},{1,3},{2,0},{3,1},{4,6},{5,7},{6,4},{7,5},{8,10},{9,11},{10,... | collective-permute-start | bytes 1966088 | tf_op jit(solution)/shard_map/ppermute | solution.py:73
  93.1 17.0 %collective-permute-start.24 = (bf16[1,176,512]{2,1,0:T(8,128)(2,1)}, bf16[1,176,512]{2,1,0:T(8,128)(2,1)}, u32[]{:S(2)}, u32[]{:S(2)}) collective-permute-start(bf16[1,176,512]{2,1,0:T(8,128)(2,1)} %convert_bitcast_fusion), channel_id=1, source_target_pairs={{0,16},{1,17},{2,10},{3,11},{4,20},{5,21},{6,14},{7,15},{8,24},{9,... | collective-permute-start | bytes 540680 | tf_op jit(solution)/shard_map/ppermute | solution.py:73
  110.3 14.0 %collective-permute-start.28 = (bf16[4,64,1408]{2,1,0:T(8,128)(2,1)}, bf16[4,64,1408]{2,1,0:T(8,128)(2,1)S(1)}, u32[]{:S(2)}, u32[]{:S(2)}) collective-permute-start(bf16[4,64,1408]{2,1,0:T(8,128)(2,1)} %collective-permute-done.23.refs_9_), channel_id=1, source_target_pairs={{0,2},{1,3},{2,0},{3,1},{4,6},{5,7},{6,4},{7,5},{8,10},{9,11},{10,... | collective-permute-start | bytes 2162696 | tf_op jit(solution)/shard_map/ppermute | solution.py:73
  110.4 13.9 %collective-permute-start.27 = (bf16[4,64,1408]{2,1,0:T(8,128)(2,1)}, bf16[4,64,1408]{2,1,0:T(8,128)(2,1)}, u32[]{:S(2)}, u32[]{:S(2)}) collective-permute-start(bf16[4,64,1408]{2,1,0:T(8,128)(2,1)} %constant_dynamic-update-slice_fusion.3.refs_16_), channel_id=1, source_target_pairs={{0,2},{1,3},{2,0},{3,1},{4,6},{5,7},{6,4},{7,5},{8,10},{9,11},{10,... | collective-permute-start | bytes 2162696 | tf_op jit(solution)/shard_map/ppermute | solution.py:73
  110.8 13.5 %collective-permute-start.26 = (bf16[4,64,1408]{2,1,0:T(8,128)(2,1)}, bf16[4,64,1408]{2,1,0:T(8,128)(2,1)}, u32[]{:S(2)}, u32[]{:S(2)}) collective-permute-start(bf16[4,64,1408]{2,1,0:T(8,128)(2,1)} %constant_dynamic-update-slice_fusion.3.refs_16_), channel_id=1, source_target_pairs={{0,1},{1,0},{2,6},{3,7},{4,5},{5,4},{6,2},{7,3},{8,9},{9,8},{10,14... | collective-permute-start | bytes 2162696 | tf_op jit(solution)/shard_map/ppermute | solution.py:73
  112.5 11.7 %collective-permute-start.29 = (bf16[2,176,512]{2,1,0:T(8,128)(2,1)S(1)}, bf16[2,176,512]{2,1,0:T(8,128)(2,1)}, u32[]{:S(2)}, u32[]{:S(2)}) collective-permute-start(bf16[2,176,512]{2,1,0:T(8,128)(2,1)S(1)} %pad_maximum_fusion.5), channel_id=1, source_target_pairs={{0,8},{1,9},{2,18},{3,19},{4,12},{5,13},{6,22},{7,23},{8,0},{9,1},... | collective-permute-start | bytes 1081352 | tf_op jit(solution)/shard_map/ppermute | solution.py:73
  114.5 24.6 %collective-permute-start.33 = (bf16[4,64,1408]{2,1,0:T(8,128)(2,1)S(1)}, bf16[4,64,1408]{2,1,0:T(8,128)(2,1)}, u32[]{:S(2)}, u32[]{:S(2)}) collective-permute-start(bf16[4,64,1408]{2,1,0:T(8,128)(2,1)S(1)} %pad_maximum_fusion.refs_8_), channel_id=1, source_target_pairs={{0,8},{1,9},{2,18},{3,19},{4,12},{5,13},{6,22},{7,23},{8,0},{9,1},... | collective-permute-start | bytes 2162696 | tf_op jit(solution)/shard_map/ppermute | solution.py:73
  124.3 14.8 %collective-permute-start.32 = (bf16[4,64,1408]{2,1,0:T(8,128)(2,1)}, bf16[4,64,1408]{2,1,0:T(8,128)(2,1)S(1)}, u32[]{:S(2)}, u32[]{:S(2)}) collective-permute-start(bf16[4,64,1408]{2,1,0:T(8,128)(2,1)} %collective-permute-done.26.refs_18_), channel_id=1, source_target_pairs={{0,2},{1,3},{2,0},{3,1},{4,6},{5,7},{6,4},{7,5},{8,10},{9,11},{10,... | collective-permute-start | bytes 2162696 | tf_op jit(solution)/shard_map/ppermute | solution.py:73
  124.7 14.4 %collective-permute-start.31 = (bf16[4,64,1408]{2,1,0:T(8,128)(2,1)}, bf16[4,64,1408]{2,1,0:T(8,128)(2,1)S(1)}, u32[]{:S(2)}, u32[]{:S(2)}) collective-permute-start(bf16[4,64,1408]{2,1,0:T(8,128)(2,1)} %collective-permute-done.22.refs_17_), channel_id=1, source_target_pairs={{0,2},{1,3},{2,0},{3,1},{4,6},{5,7},{6,4},{7,5},{8,10},{9,11},{10,... | collective-permute-start | bytes 2162696 | tf_op jit(solution)/shard_map/ppermute | solution.py:73
  124.9 14.2 %collective-permute-start.30 = (bf16[4,64,1408]{2,1,0:T(8,128)(2,1)}, bf16[4,64,1408]{2,1,0:T(8,128)(2,1)}, u32[]{:S(2)}, u32[]{:S(2)}) collective-permute-start(bf16[4,64,1408]{2,1,0:T(8,128)(2,1)} %collective-permute-done.22.refs_17_), channel_id=1, source_target_pairs={{0,1},{1,0},{2,6},{3,7},{4,5},{5,4},{6,2},{7,3},{8,9},{9,8},{10,14... | collective-permute-start | bytes 2162696 | tf_op jit(solution)/shard_map/ppermute | solution.py:73
  126.1 28.4 %collective-permute-start.36 = (bf16[4,64,1408]{2,1,0:T(8,128)(2,1)}, bf16[4,64,1408]{2,1,0:T(8,128)(2,1)}, u32[]{:S(2)}, u32[]{:S(2)}) collective-permute-start(bf16[4,64,1408]{2,1,0:T(8,128)(2,1)} %collective-permute-done.23.refs_9_), channel_id=1, source_target_pairs={{0,8},{1,9},{2,18},{3,19},{4,12},{5,13},{6,22},{7,23},{8,0},{9,1},... | collective-permute-start | bytes 2162696 | tf_op jit(solution)/shard_map/ppermute | solution.py:73
  139.2 15.4 %collective-permute-start.34 = (bf16[4,64,1408]{2,1,0:T(8,128)(2,1)}, bf16[4,64,1408]{2,1,0:T(8,128)(2,1)S(1)}, u32[]{:S(2)}, u32[]{:S(2)}) collective-permute-start(bf16[4,64,1408]{2,1,0:T(8,128)(2,1)} %collective-permute-done.30.refs_19_), channel_id=1, source_target_pairs={{0,2},{1,3},{2,0},{3,1},{4,6},{5,7},{6,4},{7,5},{8,10},{9,11},{10,... | collective-permute-start | bytes 2162696 | tf_op jit(solution)/shard_map/ppermute | solution.py:73
  139.7 14.9 %collective-permute-start.35 = (bf16[4,64,1408]{2,1,0:T(8,128)(2,1)}, bf16[4,64,1408]{2,1,0:T(8,128)(2,1)S(1)}, u32[]{:S(2)}, u32[]{:S(2)}) collective-permute-start(bf16[4,64,1408]{2,1,0:T(8,128)(2,1)} %collective-permute-done.33.refs_10_), channel_id=1, source_target_pairs={{0,2},{1,3},{2,0},{3,1},{4,6},{5,7},{6,4},{7,5},{8,10},{9,11},{10,... | collective-permute-start | bytes 2162696 | tf_op jit(solution)/shard_map/ppermute | solution.py:73
  139.8 14.8 %collective-permute-start.38 = (bf16[4,176,512]{2,1,0:T(8,128)(2,1)S(1)}, bf16[4,176,512]{2,1,0:T(8,128)(2,1)}, u32[]{:S(2)}, u32[]{:S(2)}) collective-permute-start(bf16[4,176,512]{2,1,0:T(8,128)(2,1)S(1)} %pad_maximum_fusion.1.refs_0_.refs_24_), channel_id=1, source_target_pairs={{0,2},{1,3},{2,0},{3,1},{4,6},{5,7},{6,4},{7,5},{8,10},{9,11},{10,... | collective-permute-start | bytes 2162696 | tf_op jit(solution)/shard_map/ppermute | solution.py:73
  140.2 14.4 %collective-permute-start.37 = (bf16[4,176,512]{2,1,0:T(8,128)(2,1)S(1)}, bf16[4,176,512]{2,1,0:T(8,128)(2,1)}, u32[]{:S(2)}, u32[]{:S(2)}) collective-permute-start(bf16[4,176,512]{2,1,0:T(8,128)(2,1)S(1)} %pad_maximum_fusion.1.refs_0_.refs_24_), channel_id=1, source_target_pairs={{0,4},{1,5},{2,3},{3,2},{4,0},{5,1},{6,7},{7,6},{8,12},{9,13},{10,... | collective-permute-start | bytes 2162696 | tf_op jit(solution)/shard_map/ppermute | solution.py:73
  155.2 46.6 %collective-permute-start.40 = (bf16[4,176,512]{2,1,0:T(8,128)(2,1)S(1)}, bf16[4,176,512]{2,1,0:T(8,128)(2,1)S(1)}, u32[]{:S(2)}, u32[]{:S(2)}) collective-permute-start(bf16[4,176,512]{2,1,0:T(8,128)(2,1)S(1)} %pad_maximum_fusion.1.refs_0_.refs_24_), channel_id=1, source_target_pairs={{0,1},{1,0},{2,6},{3,7},{4,5},{5,4},{6,2},{7,3},{8,9},{9,8},{10,14... | collective-permute-start | bytes 2162696 | tf_op jit(solution)/shard_map/ppermute | solution.py:73
  156.3 45.4 %collective-permute-start.42 = (bf16[4,176,512]{2,1,0:T(8,128)(2,1)}, bf16[4,176,512]{2,1,0:T(8,128)(2,1)}, u32[]{:S(2)}, u32[]{:S(2)}) collective-permute-start(bf16[4,176,512]{2,1,0:T(8,128)(2,1)} %collective-permute-done.37.refs_1_.refs_25_), channel_id=1, source_target_pairs={{0,2},{1,3},{2,0},{3,1},{4,6},{5,7},{6,4},{7,5},{8,10},{9,11},{10,... | collective-permute-start | bytes 2162696 | tf_op jit(solution)/shard_map/ppermute | solution.py:73
  156.4 45.4 %collective-permute-start.41 = (bf16[4,176,512]{2,1,0:T(8,128)(2,1)}, bf16[4,176,512]{2,1,0:T(8,128)(2,1)}, u32[]{:S(2)}, u32[]{:S(2)}) collective-permute-start(bf16[4,176,512]{2,1,0:T(8,128)(2,1)} %collective-permute-done.37.refs_1_.refs_25_), channel_id=1, source_target_pairs={{0,1},{1,0},{2,6},{3,7},{4,5},{5,4},{6,2},{7,3},{8,9},{9,8},{10,14... | collective-permute-start | bytes 2162696 | tf_op jit(solution)/shard_map/ppermute | solution.py:73
  201.8 41.9 %collective-permute-start.45 = (bf16[8,176,512]{2,1,0:T(8,128)(2,1)}, bf16[8,176,512]{2,1,0:T(8,128)(2,1)}, u32[]{:S(2)}, u32[]{:S(2)}) collective-permute-start(bf16[8,176,512]{2,1,0:T(8,128)(2,1)} %get-tuple-element.305), channel_id=1, source_target_pairs={{0,2},{1,3},{2,0},{3,1},{4,6},{5,7},{6,4},{7,5},{8,10},{9,11},{10,... | collective-permute-start | bytes 4325384 | tf_op jit(solution)/shard_map/ppermute | solution.py:73
  202.1 41.5 %collective-permute-start.46 = (bf16[8,176,512]{2,1,0:T(8,128)(2,1)}, bf16[8,176,512]{2,1,0:T(8,128)(2,1)S(1)}, u32[]{:S(2)}, u32[]{:S(2)}) collective-permute-start(bf16[8,176,512]{2,1,0:T(8,128)(2,1)} %get-tuple-element.306), channel_id=1, source_target_pairs={{0,2},{1,3},{2,0},{3,1},{4,6},{5,7},{6,4},{7,5},{8,10},{9,11},{10,... | collective-permute-start | bytes 4325384 | tf_op jit(solution)/shard_map/ppermute | solution.py:73
  202.6 6.8 %collective-permute-start.44 = (bf16[4,176,512]{2,1,0:T(8,128)(2,1)}, bf16[4,176,512]{2,1,0:T(8,128)(2,1)S(1)}, u32[]{:S(2)}, u32[]{:S(2)}) collective-permute-start(bf16[4,176,512]{2,1,0:T(8,128)(2,1)} %collective-permute-done.41.refs_3_.refs_27_), channel_id=1, source_target_pairs={{0,2},{1,3},{2,0},{3,1},{4,6},{5,7},{6,4},{7,5},{8,10},{9,11},{10,... | collective-permute-start | bytes 2162696 | tf_op jit(solution)/shard_map/ppermute | solution.py:73
  243.6 39.1 %collective-permute-start.48 = (bf16[8,128,1408]{2,1,0:T(8,128)(2,1)}, bf16[8,128,1408]{2,1,0:T(8,128)(2,1)}, u32[]{:S(2)}, u32[]{:S(2)}) collective-permute-start(bf16[8,128,1408]{2,1,0:T(8,128)(2,1)} %get-tuple-element.314), channel_id=1, source_target_pairs={{0,2},{1,3},{2,0},{3,1},{4,6},{5,7},{6,4},{7,5},{8,10},{9,11},{10,... | collective-permute-start | bytes 8650760 | tf_op jit(solution)/shard_map/ppermute | solution.py:73
  244.0 38.8 %collective-permute-start.49 = (bf16[8,128,1408]{2,1,0:T(8,128)(2,1)}, bf16[8,128,1408]{2,1,0:T(8,128)(2,1)}, u32[]{:S(2)}, u32[]{:S(2)}) collective-permute-start(bf16[8,128,1408]{2,1,0:T(8,128)(2,1)} %get-tuple-element.315), channel_id=1, source_target_pairs={{0,2},{1,3},{2,0},{3,1},{4,6},{5,7},{6,4},{7,5},{8,10},{9,11},{10,... | collective-permute-start | bytes 8650760 | tf_op jit(solution)/shard_map/ppermute | solution.py:73
  247.6 35.2 %collective-permute-start.47 = (bf16[8,176,512]{2,1,0:T(8,128)(2,1)}, bf16[8,176,512]{2,1,0:T(8,128)(2,1)}, u32[]{:S(2)}, u32[]{:S(2)}) collective-permute-start(bf16[8,176,512]{2,1,0:T(8,128)(2,1)} %add_convert_fusion.2), channel_id=1, source_target_pairs={{0,8},{1,9},{2,18},{3,19},{4,12},{5,13},{6,22},{7,23},{8,0},{9,1},... | collective-permute-start | bytes 4325384 | tf_op jit(solution)/shard_map/ppermute | solution.py:73
  287.0 42.0 %collective-permute-start.51 = (bf16[8,128,1408]{2,1,0:T(8,128)(2,1)}, bf16[8,128,1408]{2,1,0:T(8,128)(2,1)}, u32[]{:S(2)}, u32[]{:S(2)}) collective-permute-start(bf16[8,128,1408]{2,1,0:T(8,128)(2,1)} %add_convert_fusion), channel_id=1, source_target_pairs={{0,1},{1,0},{2,6},{3,7},{4,5},{5,4},{6,2},{7,3},{8,9},{9,8},{10,14... | collective-permute-start | bytes 8650760 | tf_op jit(solution)/shard_map/ppermute | solution.py:73
  289.1 20.0 %collective-permute-start.50 = (bf16[4,176,512]{2,1,0:T(8,128)(2,1)S(1)}, bf16[4,176,512]{2,1,0:T(8,128)(2,1)S(1)}, u32[]{:S(2)}, u32[]{:S(2)}) collective-permute-start(bf16[4,176,512]{2,1,0:T(8,128)(2,1)S(1)} %add_convert_fusion.6), channel_id=1, source_target_pairs={{0,16},{1,17},{2,10},{3,11},{4,20},{5,21},{6,14},{7,15},{8,24},{9,... | collective-permute-start | bytes 2162696 | tf_op jit(solution)/shard_map/ppermute | solution.py:73
  311.3 17.8 %collective-permute-start.52 = (bf16[2,176,512]{2,1,0:T(8,128)(2,1)}, bf16[2,176,512]{2,1,0:T(8,128)(2,1)S(1)}, u32[]{:S(2)}, u32[]{:S(2)}) collective-permute-start(bf16[2,176,512]{2,1,0:T(8,128)(2,1)} %add_convert_fusion.10), channel_id=1, source_target_pairs={{0,1},{1,0},{2,6},{3,7},{4,5},{5,4},{6,2},{7,3},{8,9},{9,8},{10,14... | collective-permute-start | bytes 1081352 | tf_op jit(solution)/shard_map/ppermute | solution.py:73
  330.9 18.1 %collective-permute-start.53 = (bf16[1,176,512]{2,1,0:T(8,128)(2,1)}, bf16[1,176,512]{2,1,0:T(8,128)(2,1)}, u32[]{:S(2)}, u32[]{:S(2)}) collective-permute-start(bf16[1,176,512]{2,1,0:T(8,128)(2,1)} %add_convert_fusion.13), channel_id=1, source_target_pairs={{0,4},{1,5},{2,3},{3,2},{4,0},{5,1},{6,7},{7,6},{8,12},{9,13},{10,... | collective-permute-start | bytes 540680 | tf_op jit(solution)/shard_map/ppermute | solution.py:73
  335.2 23.8 %collective-permute-start.56 = (bf16[4,128,1408]{2,1,0:T(8,128)(2,1)}, bf16[4,128,1408]{2,1,0:T(8,128)(2,1)}, u32[]{:S(2)}, u32[]{:S(2)}) collective-permute-start(bf16[4,128,1408]{2,1,0:T(8,128)(2,1)} %add_convert_fusion.1), channel_id=1, source_target_pairs={{0,4},{1,5},{2,3},{3,2},{4,0},{5,1},{6,7},{7,6},{8,12},{9,13},{10,... | collective-permute-start | bytes 4325384 | tf_op jit(solution)/shard_map/ppermute | solution.py:73
  349.0 10.0 %collective-permute-start.54 = (bf16[8,64,1280]{2,1,0:T(8,128)(2,1)}, bf16[8,64,1280]{2,1,0:T(8,128)(2,1)}, u32[]{:S(2)}, u32[]{:S(2)}) collective-permute-start(bf16[8,64,1280]{2,1,0:T(8,128)(2,1)} %get-tuple-element.337), channel_id=1, source_target_pairs={{0,2},{1,3},{2,0},{3,1},{4,6},{5,7},{6,4},{7,5},{8,10},{9,11},{10,... | collective-permute-start | bytes 3932168 | tf_op jit(solution)/shard_map/ppermute | solution.py:73
  349.1 9.9 %collective-permute-start.55 = (bf16[8,64,1280]{2,1,0:T(8,128)(2,1)}, bf16[8,64,1280]{2,1,0:T(8,128)(2,1)}, u32[]{:S(2)}, u32[]{:S(2)}) collective-permute-start(bf16[8,64,1280]{2,1,0:T(8,128)(2,1)} %get-tuple-element.338), channel_id=1, source_target_pairs={{0,2},{1,3},{2,0},{3,1},{4,6},{5,7},{6,4},{7,5},{8,10},{9,11},{10,... | collective-permute-start | bytes 3932168 | tf_op jit(solution)/shard_map/ppermute | solution.py:73
  362.1 22.8 %collective-permute-start.58 = (bf16[8,64,1280]{2,1,0:T(8,128)(2,1)}, bf16[8,64,1280]{2,1,0:T(8,128)(2,1)}, u32[]{:S(2)}, u32[]{:S(2)}) collective-permute-start(bf16[8,64,1280]{2,1,0:T(8,128)(2,1)} %add_convert_fusion.3), channel_id=1, source_target_pairs={{0,1},{1,0},{2,6},{3,7},{4,5},{5,4},{6,2},{7,3},{8,9},{9,8},{10,14... | collective-permute-start | bytes 3932168 | tf_op jit(solution)/shard_map/ppermute | solution.py:73
  365.6 19.3 %collective-permute-start.57 = (bf16[2,128,1408]{2,1,0:T(8,128)(2,1)}, bf16[2,128,1408]{2,1,0:T(8,128)(2,1)}, u32[]{:S(2)}, u32[]{:S(2)}) collective-permute-start(bf16[2,128,1408]{2,1,0:T(8,128)(2,1)} %add_convert_fusion.5), channel_id=1, source_target_pairs={{0,8},{1,9},{2,18},{3,19},{4,12},{5,13},{6,22},{7,23},{8,0},{9,1},... | collective-permute-start | bytes 2162696 | tf_op jit(solution)/shard_map/ppermute | solution.py:73
  387.5 19.7 %collective-permute-start.60 = (bf16[4,64,1280]{2,1,0:T(8,128)(2,1)}, bf16[4,64,1280]{2,1,0:T(8,128)(2,1)}, u32[]{:S(2)}, u32[]{:S(2)}) collective-permute-start(bf16[4,64,1280]{2,1,0:T(8,128)(2,1)} %add_convert_fusion.7), channel_id=1, source_target_pairs={{0,4},{1,5},{2,3},{3,2},{4,0},{5,1},{6,7},{7,6},{8,12},{9,13},{10,... | collective-permute-start | bytes 1966088 | tf_op jit(solution)/shard_map/ppermute | solution.py:73
  391.1 16.1 %collective-permute-start.59 = (bf16[1,128,1408]{2,1,0:T(8,128)(2,1)}, bf16[1,128,1408]{2,1,0:T(8,128)(2,1)S(1)}, u32[]{:S(2)}, u32[]{:S(2)}) collective-permute-start(bf16[1,128,1408]{2,1,0:T(8,128)(2,1)} %add_convert_fusion.9), channel_id=1, source_target_pairs={{0,16},{1,17},{2,10},{3,11},{4,20},{5,21},{6,14},{7,15},{8,24},{9,... | collective-permute-start | bytes 1081352 | tf_op jit(solution)/shard_map/ppermute | solution.py:73
  410.0 11.7 %collective-permute-start.61 = (bf16[2,64,1280]{2,1,0:T(8,128)(2,1)}, bf16[2,64,1280]{2,1,0:T(8,128)(2,1)}, u32[]{:S(2)}, u32[]{:S(2)}) collective-permute-start(bf16[2,64,1280]{2,1,0:T(8,128)(2,1)} %add_convert_fusion.11), channel_id=1, source_target_pairs={{0,8},{1,9},{2,18},{3,19},{4,12},{5,13},{6,22},{7,23},{8,0},{9,1},... | collective-permute-start | bytes 983048 | tf_op jit(solution)/shard_map/ppermute | solution.py:73
  427.7 18.5 %collective-permute-start.64 = (bf16[8,64,768]{2,1,0:T(8,128)(2,1)}, bf16[8,64,768]{2,1,0:T(8,128)(2,1)}, u32[]{:S(2)}, u32[]{:S(2)}) collective-permute-start(bf16[8,64,768]{2,1,0:T(8,128)(2,1)} %add_convert_fusion.4), channel_id=1, source_target_pairs={{0,1},{1,0},{2,6},{3,7},{4,5},{5,4},{6,2},{7,3},{8,9},{9,8},{10,14... | collective-permute-start | bytes 2359304 | tf_op jit(solution)/shard_map/ppermute | solution.py:73
  429.6 16.6 %collective-permute-start.65 = (bf16[1,64,1280]{2,1,0:T(8,128)(2,1)S(1)}, bf16[1,64,1280]{2,1,0:T(8,128)(2,1)S(1)}, u32[]{:S(2)}, u32[]{:S(2)}) collective-permute-start(bf16[1,64,1280]{2,1,0:T(8,128)(2,1)S(1)} %add_convert_fusion.14), channel_id=1, source_target_pairs={{0,16},{1,17},{2,10},{3,11},{4,20},{5,21},{6,14},{7,15},{8,24},{9,... | collective-permute-start | bytes 491528 | tf_op jit(solution)/shard_map/ppermute | solution.py:73
  448.3 8.8 %collective-permute-start.66 = (bf16[4,64,768]{2,1,0:T(8,128)(2,1)S(1)}, bf16[4,64,768]{2,1,0:T(8,128)(2,1)S(1)}, u32[]{:S(2)}, u32[]{:S(2)}) collective-permute-start(bf16[4,64,768]{2,1,0:T(8,128)(2,1)S(1)} %add_convert_fusion.8), channel_id=1, source_target_pairs={{0,4},{1,5},{2,3},{3,2},{4,0},{5,1},{6,7},{7,6},{8,12},{9,13},{10,... | collective-permute-start | bytes 1179656 | tf_op jit(solution)/shard_map/ppermute | solution.py:73
  449.7 7.3 %collective-permute-start.70 = (f32[2,1024]{1,0:T(2,128)S(1)}, f32[2,1024]{1,0:T(2,128)S(1)}, u32[]{:S(2)}, u32[]{:S(2)}) collective-permute-start(f32[2,1024]{1,0:T(2,128)S(1)} %fusion.19), channel_id=1, source_target_pairs={{0,5},{1,4},{2,7},{3,6},{4,1},{5,0},{6,3},{7,2},{8,13},{9,12},{10,... | collective-permute-start | bytes 24584 | tf_op jit(solution)/shard_map/ppermute | solution.py:73
  451.2 5.9 %collective-permute-start.69 = (f32[2,1024]{1,0:T(2,128)S(1)}, f32[2,1024]{1,0:T(2,128)S(1)}, u32[]{:S(2)}, u32[]{:S(2)}) collective-permute-start(f32[2,1024]{1,0:T(2,128)S(1)} %fusion.19), channel_id=1, source_target_pairs={{0,1},{1,0},{2,3},{3,2},{4,5},{5,4},{6,7},{7,6},{8,9},{9,8},{10,11... | collective-permute-start | bytes 24584 | tf_op jit(solution)/shard_map/ppermute | solution.py:73
  460.1 7.8 %collective-permute-start.71 = (bf16[2,64,768]{2,1,0:T(8,128)(2,1)S(1)}, bf16[2,64,768]{2,1,0:T(8,128)(2,1)S(1)}, u32[]{:S(2)}, u32[]{:S(2)}) collective-permute-start(bf16[2,64,768]{2,1,0:T(8,128)(2,1)S(1)} %add_convert_fusion.12), channel_id=1, source_target_pairs={{0,8},{1,9},{2,18},{3,19},{4,12},{5,13},{6,22},{7,23},{8,0},{9,1},... | collective-permute-start | bytes 589832 | tf_op jit(solution)/shard_map/ppermute | solution.py:73
  469.2 5.6 %collective-permute-start.73 = (bf16[1,64,768]{2,1,0:T(8,128)(2,1)S(1)}, bf16[1,64,768]{2,1,0:T(8,128)(2,1)S(1)}, u32[]{:S(2)}, u32[]{:S(2)}) collective-permute-start(bf16[1,64,768]{2,1,0:T(8,128)(2,1)S(1)} %add_convert_fusion.15), channel_id=1, source_target_pairs={{0,16},{1,17},{2,10},{3,11},{4,20},{5,21},{6,14},{7,15},{8,24},{9,... | collective-permute-start | bytes 294920 | tf_op jit(solution)/shard_map/ppermute | solution.py:73
  (76 other events, 730.1 us)
